TPU v7x, 32 devices: a whole 2x2x4 slice. The times are simulated.
32 devices in a mesh: row: 8 (over z, y), col: 4 (over x, core).
Axes of the slice: x: 2, y: 2, z: 4, core: 2. Of those that a mesh axis runs over, the one named last changes fastest.
Arguments:
- tokens: bfloat16 [16384, 768], P(('row', 'col')), may hold values from -12 to 12
- cotangent: bfloat16 [16384, 768], P(('row', 'col')), may hold values from -6 to 6
- w_qkv: float32 [768, 3, 768], P('row', None, 'col'), may hold values from -0.21875 to 0.21875
- w_out: float32 [768, 768], P('col', 'row'), may hold values from -0.625 to 0.625
- w_up: float32 [768, 3072], P('row', 'col'), may hold values from -0.21875 to 0.21875
- w_down: float32 [3072, 768], P('col', 'row'), may hold values from -0.109375 to 0.109375
- vectors: float32 [12, 768], P(None, 'row'), may hold values from -0.4 to 1.5
- first_qkv: float32 [768, 3, 768], P('row', None, 'col'), may hold values from -24 to 24
- first_out: float32 [768, 768], P('col', 'row'), may hold values from -32 to 32
- first_up: float32 [768, 3072], P('row', 'col'), may hold values from -20 to 20
- first_down: float32 [3072, 768], P('col', 'row'), may hold values from -48 to 48
- first_vectors: float32 [12, 768], P(None, 'row'), may hold values from -80 to 80
- second_qkv: float32 [768, 3, 768], P('row', None, 'col'), may hold values from 1.47456 to 5.89824
- second_out: float32 [768, 768], P('col', 'row'), may hold values from 2.62144 to 10.48576
- second_up: float32 [768, 3072], P('row', 'col'), may hold values from 1.024 to 4.096
- second_down: float32 [3072, 768], P('col', 'row'), may hold values from 5.89824 to 23.59296
- second_vectors: float32 [12, 768], P(None, 'row'), may hold values from 16.384 to 65.536
Outputs:
- mixed_out: float32 [16384, 768], P(('row', 'col'))
- token_grad: float32 [16384, 768], P(('row', 'col'))
- new_qkv: float32 [768, 3, 768], P('row', None, 'col')
- new_out: float32 [768, 768], P('col', 'row')
- new_up: float32 [768, 3072], P('row', 'col')
- new_down: float32 [3072, 768], P('col', 'row')
- new_vectors: float32 [12, 768], P(None, 'row')
- new_first_qkv: float32 [768, 3, 768], P('row', None, 'col')
- new_first_out: float32 [768, 768], P('col', 'row')
- new_first_up: float32 [768, 3072], P('row', 'col')
- new_first_down: float32 [3072, 768], P('col', 'row')
- new_first_vectors: float32 [12, 768], P(None, 'row')
- new_second_qkv: float32 [768, 3, 768], P('row', None, 'col')
- new_second_out: float32 [768, 768], P('col', 'row')
- new_second_up: float32 [768, 3072], P('row', 'col')
- new_second_down: float32 [3072, 768], P('col', 'row')
- new_second_vectors: float32 [12, 768], P(None, 'row')
All inputs are finite; a program needn't handle non-finite values.
Results may differ from a plain program's by a relative error of at most 0.008.
The roundings to bfloat16 on the way count: a program that leaves them out, or rounds other values in their place, can miss the bound.
Values may be sent and summed in bfloat16 or wider, within the bound.
No kernel may reach another device: no remote copies, remote signals or barrier semaphores. Data moves between devices by JAX's collectives and lax.ppermute only.
A program may use at most 128 MiB of HBM per device.

v0:
```python
import jax
import jax.numpy as jnp
from jax import lax
from jax.sharding import PartitionSpec as P

HEAD_DIM = 64
LENGTH = 1024
STEP_NUMBER = 10


EPS = 1e-05
BETA_ONE = 0.9
BETA_TWO = 0.999
ADAM_EPS = 1e-08
DECAY = 0.1
RATE_MATRIX = 0.04
RATE_VECTOR = 0.3


def normalize_rows(values_in):
    row_mean = jnp.mean(values_in, axis=-1, keepdims=True)
    centred = values_in - row_mean
    row_var = jnp.mean(centred * centred, axis=-1, keepdims=True)
    inv_std = lax.rsqrt(row_var + EPS)
    return (centred * inv_std, inv_std)


def norm_back(grad_in, normed, inv_std):
    mean_grad = jnp.mean(grad_in, axis=-1, keepdims=True)
    mean_cross = jnp.mean(grad_in * normed, axis=-1, keepdims=True)
    return inv_std * (grad_in - mean_grad - normed * mean_cross)


def adamw(weight, moment_one, moment_two, gradient, rate):
    first = BETA_ONE * moment_one + (1 - BETA_ONE) * gradient
    second = BETA_TWO * moment_two + (1 - BETA_TWO) * gradient * gradient
    first_hat = first / (1 - BETA_ONE**STEP_NUMBER)
    second_hat = second / (1 - BETA_TWO**STEP_NUMBER)
    updated = weight - rate * (first_hat / (jnp.sqrt(second_hat) + ADAM_EPS) + DECAY * weight)
    return (updated, first, second)


def causal_mask(first_row, last_row):
    rows_at = first_row + jnp.arange(last_row - first_row)[:, None]
    cols_at = jnp.arange(last_row)[None, :]
    return (cols_at <= rows_at)[None]


def attend_forward(triple):
    queries, keys_in, values_in = triple
    length = queries.shape[0]
    rows_per = min(512, length)
    scaling = HEAD_DIM ** (-0.5)
    outputs = []
    totals = []
    for first_row in range(0, length, rows_per):
        last_row = first_row + rows_per
        scores = (
            jnp.einsum(
                "qhe,khe->hqk",
                queries[first_row:last_row],
                keys_in[:last_row],
                preferred_element_type=jnp.float32,
            )
            * scaling
        )
        scores = jnp.where(causal_mask(first_row, last_row), scores, -1e30)
        row_top = jnp.max(scores, axis=-1, keepdims=True)
        expo = jnp.exp(scores - row_top)
        row_total = jnp.sum(expo, axis=-1, keepdims=True)
        probs_low = (expo / row_total).astype(jnp.bfloat16)
        outputs.append(
            jnp.einsum(
                "hqk,khe->qhe", probs_low, values_in[:last_row], preferred_element_type=jnp.float32
            )
        )
        totals.append(row_top + jnp.log(row_total))
    return (jnp.concatenate(outputs, axis=0), jnp.concatenate(totals, axis=1))


def attend_backward(bundle):
    queries, keys_in, values_in, grad_heads, totals = bundle
    length = queries.shape[0]
    rows_per = min(512, length)
    scaling = HEAD_DIM ** (-0.5)
    grad_keys = jnp.zeros(keys_in.shape, jnp.float32)
    grad_values = jnp.zeros(values_in.shape, jnp.float32)
    grad_queries = []
    for first_row in range(0, length, rows_per):
        last_row = first_row + rows_per
        query_rows = queries[first_row:last_row]
        grad_rows = grad_heads[first_row:last_row]
        scores = (
            jnp.einsum(
                "qhe,khe->hqk", query_rows, keys_in[:last_row], preferred_element_type=jnp.float32
            )
            * scaling
        )
        allowed = causal_mask(first_row, last_row)
        probs = jnp.where(allowed, jnp.exp(scores - totals[:, first_row:last_row]), 0.0)
        grad_probs = jnp.einsum(
            "qhe,khe->hqk", grad_rows, values_in[:last_row], preferred_element_type=jnp.float32
        )
        inner = jnp.sum(probs * grad_probs, axis=-1, keepdims=True)
        grad_scores = (probs * (grad_probs - inner)).astype(jnp.bfloat16)
        grad_queries.append(
            jnp.einsum(
                "hqk,khe->qhe", grad_scores, keys_in[:last_row], preferred_element_type=jnp.float32
            )
            * scaling
        )
        grad_keys = grad_keys.at[:last_row].add(
            jnp.einsum("hqk,qhe->khe", grad_scores, query_rows, preferred_element_type=jnp.float32)
            * scaling
        )
        grad_values = grad_values.at[:last_row].add(
            jnp.einsum(
                "hqk,qhe->khe",
                probs.astype(jnp.bfloat16),
                grad_rows,
                preferred_element_type=jnp.float32,
            )
        )
    return (jnp.concatenate(grad_queries, axis=0), grad_keys, grad_values)


def gelu_value(value_up):
    return jax.nn.gelu(value_up, approximate=True)


def shards(
    tokens,
    cotangent,
    w_qkv,
    w_out,
    w_up,
    w_down,
    vectors,
    first_qkv,
    first_out,
    first_up,
    first_down,
    first_vectors,
    second_qkv,
    second_out,
    second_up,
    second_down,
    second_vectors,
):
    col_index = lax.axis_index("col")
    col_count = lax.axis_size("col")
    width = tokens.shape[1]
    width_loc = w_qkv.shape[2]
    heads_loc = width_loc // HEAD_DIM
    start_col = col_index * width_loc
    full_qkv, full_out, full_up, full_down, full_vec = (
        lax.all_gather(w_qkv.astype(jnp.bfloat16), "row", axis=0, tiled=True),
        lax.all_gather(w_out.astype(jnp.bfloat16), "row", axis=1, tiled=True),
        lax.all_gather(w_up.astype(jnp.bfloat16), "row", axis=0, tiled=True),
        lax.all_gather(w_down.astype(jnp.bfloat16), "row", axis=1, tiled=True),
        lax.all_gather(vectors.astype(jnp.bfloat16), "row", axis=1, tiled=True),
    )
    vec_all = full_vec.astype(jnp.float32)

    def block_of(vec_row):
        return lax.dynamic_slice_in_dim(vec_row, start_col, width_loc, 0)

    inputs_loc = tokens.astype(jnp.float32)
    normed_one, inv_one = normalize_rows(inputs_loc)
    first_loc = (normed_one * vec_all[0] + vec_all[1]).astype(jnp.bfloat16)
    first_in = lax.all_gather(first_loc, "col", axis=0, tiled=True)
    rows_dev = first_in.shape[0]
    seq_count = rows_dev // LENGTH
    qkv = jnp.einsum("nd,dkc->nkc", first_in, full_qkv, preferred_element_type=jnp.float32)
    queries = (qkv[:, 0] + block_of(vec_all[2])).astype(jnp.bfloat16)
    keys_in = qkv[:, 1].astype(jnp.bfloat16)
    values_in = (qkv[:, 2] + block_of(vec_all[3])).astype(jnp.bfloat16)
    shaped = (seq_count, LENGTH, heads_loc, HEAD_DIM)
    query_seq = queries.reshape(shaped)
    key_seq = keys_in.reshape(shaped)
    value_seq = values_in.reshape(shaped)
    heads_out, totals = lax.map(attend_forward, (query_seq, key_seq, value_seq))
    heads_low = heads_out.reshape(rows_dev, width_loc).astype(jnp.bfloat16)
    attended = lax.psum_scatter(
        jnp.dot(heads_low, full_out, preferred_element_type=jnp.float32),
        "col",
        scatter_dimension=0,
        tiled=True,
    )
    hidden_state = inputs_loc + attended + vec_all[4]
    normed_two, inv_two = normalize_rows(hidden_state)
    second_loc = (normed_two * vec_all[5] + vec_all[6]).astype(jnp.bfloat16)
    grad_out_loc = cotangent.astype(jnp.float32)
    second_in = lax.all_gather(second_loc, "col", axis=0, tiled=True)
    bias_up = lax.dynamic_index_in_dim(vec_all[8:], col_index, 0, keepdims=False)
    up_proj = jnp.dot(second_in, full_up, preferred_element_type=jnp.float32) + bias_up
    gelu_out, gelu_back = jax.vjp(gelu_value, up_proj)
    activated = gelu_out.astype(jnp.bfloat16)
    down_proj = lax.psum_scatter(
        jnp.dot(activated, full_down, preferred_element_type=jnp.float32).astype(jnp.bfloat16),
        "col",
        scatter_dimension=0,
        tiled=True,
    ).astype(jnp.float32)
    mixed_out = hidden_state + down_proj + vec_all[7]
    grad_out_full = lax.all_gather(cotangent, "col", axis=0, tiled=True)
    grad_act = jnp.einsum("nd,fd->nf", grad_out_full, full_down, preferred_element_type=jnp.float32)
    grad_down = jnp.einsum(
        "nf,nd->fd", activated, grad_out_full, preferred_element_type=jnp.float32
    )
    grad_upper = gelu_back(grad_act)[0].astype(jnp.bfloat16)
    grad_bias_up = jnp.sum(grad_upper.astype(jnp.float32), axis=0)
    grad_up = jnp.einsum("nd,nf->df", second_in, grad_upper, preferred_element_type=jnp.float32)
    grad_second = lax.psum_scatter(
        jnp.einsum("nf,df->nd", grad_upper, full_up, preferred_element_type=jnp.float32),
        "col",
        scatter_dimension=0,
        tiled=True,
    )
    up_rows = jnp.where(jnp.arange(col_count)[:, None] == col_index, grad_bias_up[None, :], 0.0)
    grad_gain_two = jnp.sum(grad_second * normed_two, axis=0)
    grad_bias_two = jnp.sum(grad_second, axis=0)
    grad_hidden = grad_out_loc + norm_back(grad_second * vec_all[5], normed_two, inv_two)
    grad_bias_out = jnp.sum(grad_hidden, axis=0)
    grad_bias_down = jnp.sum(grad_out_loc, axis=0)
    grad_hidden_full = lax.all_gather(grad_hidden.astype(jnp.bfloat16), "col", axis=0, tiled=True)
    grad_proj = jnp.einsum(
        "nc,nd->cd", heads_low, grad_hidden_full, preferred_element_type=jnp.float32
    )
    grad_heads = jnp.einsum(
        "nd,cd->nc", grad_hidden_full, full_out, preferred_element_type=jnp.float32
    ).astype(jnp.bfloat16)
    grad_q, grad_k, grad_v = lax.map(
        attend_backward, (query_seq, key_seq, value_seq, grad_heads.reshape(shaped), totals)
    )
    grad_qkv_low = jnp.stack(
        [
            grad_q.reshape(rows_dev, width_loc),
            grad_k.reshape(rows_dev, width_loc),
            grad_v.reshape(rows_dev, width_loc),
        ],
        axis=1,
    ).astype(jnp.bfloat16)
    grad_bias_q = jnp.sum(grad_qkv_low[:, 0].astype(jnp.float32), axis=0)
    grad_bias_v = jnp.sum(grad_qkv_low[:, 2].astype(jnp.float32), axis=0)
    grad_qkv = jnp.einsum("nd,nkc->dkc", first_in, grad_qkv_low, preferred_element_type=jnp.float32)
    grad_first = lax.psum_scatter(
        jnp.einsum("nkc,dkc->nd", grad_qkv_low, full_qkv, preferred_element_type=jnp.float32),
        "col",
        scatter_dimension=0,
        tiled=True,
    )
    grad_gain_one = jnp.sum(grad_first * normed_one, axis=0)
    grad_bias_one = jnp.sum(grad_first, axis=0)
    token_grad = grad_hidden + norm_back(grad_first * vec_all[0], normed_one, inv_one)

    def placed(part_row):
        return lax.dynamic_update_slice_in_dim(
            jnp.zeros((width,), jnp.float32), part_row, start_col, 0
        )

    front_rows = jnp.stack(
        [
            grad_gain_one,
            grad_bias_one,
            placed(grad_bias_q),
            placed(grad_bias_v),
            grad_bias_out,
            grad_gain_two,
            grad_bias_two,
            grad_bias_down,
        ]
    )
    grad_vec_all = jnp.concatenate([front_rows, up_rows], axis=0)
    owned_qkv, owned_out, owned_up, owned_down, owned_vec = (
        lax.psum_scatter(grad_qkv, "row", scatter_dimension=0, tiled=True),
        lax.psum_scatter(grad_proj, "row", scatter_dimension=1, tiled=True),
        lax.psum_scatter(grad_up, "row", scatter_dimension=0, tiled=True),
        lax.psum_scatter(grad_down, "row", scatter_dimension=1, tiled=True),
        lax.psum_scatter(grad_vec_all, "row", scatter_dimension=1, tiled=True),
    )
    owned_vec = lax.psum(owned_vec, "col")
    new_qkv, new_first_qkv, new_second_qkv = adamw(
        w_qkv, first_qkv, second_qkv, owned_qkv, RATE_MATRIX
    )
    new_out, new_first_out, new_second_out = adamw(
        w_out, first_out, second_out, owned_out, RATE_MATRIX
    )
    new_up, new_first_up, new_second_up = adamw(w_up, first_up, second_up, owned_up, RATE_MATRIX)
    new_down, new_first_down, new_second_down = adamw(
        w_down, first_down, second_down, owned_down, RATE_MATRIX
    )
    new_vectors, new_first_vectors, new_second_vectors = adamw(
        vectors, first_vectors, second_vectors, owned_vec, RATE_VECTOR
    )
    return (
        mixed_out,
        token_grad,
        new_qkv,
        new_out,
        new_up,
        new_down,
        new_vectors,
        new_first_qkv,
        new_first_out,
        new_first_up,
        new_first_down,
        new_first_vectors,
        new_second_qkv,
        new_second_out,
        new_second_up,
        new_second_down,
        new_second_vectors,
    )


def solution(mesh):
    placed = (
        P(("row", "col"), None),
        P(("row", "col"), None),
        P("row", None, "col"),
        P("col", "row"),
        P("row", "col"),
        P("col", "row"),
        P(None, "row"),
        P("row", None, "col"),
        P("col", "row"),
        P("row", "col"),
        P("col", "row"),
        P(None, "row"),
        P("row", None, "col"),
        P("col", "row"),
        P("row", "col"),
        P("col", "row"),
        P(None, "row"),
    )
    return jax.shard_map(
        shards,
        mesh=mesh,
        in_specs=placed,
        out_specs=(
            P(("row", "col"), None),
            P(("row", "col"), None),
            P("row", None, "col"),
            P("col", "row"),
            P("row", "col"),
            P("col", "row"),
            P(None, "row"),
            P("row", None, "col"),
            P("col", "row"),
            P("row", "col"),
            P("col", "row"),
            P(None, "row"),
            P("row", None, "col"),
            P("col", "row"),
            P("row", "col"),
            P("col", "row"),
            P(None, "row"),
        ),
        check_vma=False,
    )
```

profile of v0, /device:TPU:0, one launch (start us, length us, event | category | flops | bytes accessed | tf_op | source)
XLA Modules:
  0.0 868.8 jit_solution(15386113393220185431)
XLA Ops:
  11.7 32.2 %all-gather = bf16[8,96,12]{1,2,0:T(8,128)(2,1)S(1)} all-gather(bf16[1,96,12]{1,2,0:T(8,128)(2,1)S(1)} %convert_bitcast_fusion), channel_id=1, replica_groups=mesh['row'=8,'col'=4] {'row'}, dimensions={0}, use_global_device_ids=true | all-gather | bytes 20736 | tf_op jit(solution)/shard_map/all_gather | solution.py:161
  44.6 2.4 fusion.90
  48.2 38.1 %all_gather.29 = bf16[768,3,192]{2,1,0:T(4,128)(2,1)S(1)} all-gather(bf16[96,3,192]{2,1,0:T(4,128)(2,1)S(1)} %copy.90), channel_id=1, replica_groups=mesh['row'=8,'col'=4] {'row'}, dimensions={0}, use_global_device_ids=true | all-gather | bytes 995328 | tf_op jit(solution)/shard_map/all_gather | solution.py:157
  87.3 31.0 %all_gather.30 = bf16[192,768]{0,1:T(8,128)(2,1)S(1)} all-gather(bf16[192,96]{0,1:T(8,128)(2,1)S(1)} %copy.96), channel_id=1, replica_groups=mesh['row'=8,'col'=4] {'row'}, dimensions={1}, use_global_device_ids=true | all-gather | bytes 331776 | tf_op jit(solution)/shard_map/all_gather | solution.py:158
  118.2 3.9 fusion.116
  125.8 2.9 convert_element_type.120
  128.9 3.4 squeeze.45
  134.9 18.5 %while.35 = (s32[]{:T(128)}, bf16[2,1024,3,64]{1,3,2,0:T(8,128)(2,1)S(1)}, f32[2,3,1024,1]{2,1,3,0:T(4,128)}, bf16[2,1024,3,64]{1,3,2,0:T(8,128)(2,1)S(1)}, bf16...) while((s32[]{:T(128)}, ...), condition=%wide.region_7.8_spmd, body=%wide.region_2.7_spmd.sunk | while | flops 633864704 | bytes 34552504 | solution.py:182
  141.1 2.1 fusion.178
  150.1 2.1 fusion.178
  155.3 3.7 fusion.117
  160.8 55.4 %reduce-scatter.14.cloned.1.call-done = f32[512,768]{1,0:T(8,128)} async-done(((f32[2048,768]{1,0:T(8,128)}), f32[512,768]{1,0:T(8,128)}) %reduce-scatter.14.cloned.1.call-update) | async-done | bytes 1572880 | tf_op jit(solution)/shard_map/reduce_scatter | solution.py:184
  216.2 1.9 fusion.112
  224.2 23.9 %all-gather.10.cloned.1.call-done = bf16[2048,768]{1,0:T(8,128)(2,1)} async-done(((bf16[512,768]{1,0:T(8,128)(2,1)}), bf16[2048,768]{1,0:T(8,128)(2,1)}) %all-gather.10.cloned.1.call-update) | async-done | bytes 3145744 | tf_op jit(solution)/shard_map/all_gather | solution.py:194
  248.1 7.5 fusion.118
  255.6 36.9 %all-gather.14.cloned.1.call-done = bf16[768,768]{0,1:T(8,128)(2,1)} async-done(((bf16[768,96]{0,1:T(8,128)(2,1)}), bf16[768,768]{0,1:T(8,128)(2,1)}) %all-gather.14.cloned.1.call-update) | async-done | bytes 1179664 | tf_op jit(solution)/shard_map/all_gather | solution.py:160
  292.5 28.5 %all-gather.16.cloned.1.call-done = bf16[2048,768]{1,0:T(8,128)(2,1)} async-done(((bf16[512,768]{1,0:T(8,128)(2,1)}), bf16[2048,768]{1,0:T(8,128)(2,1)}) %all-gather.16.cloned.1.call-update) | async-done | bytes 3145744 | tf_op jit(solution)/shard_map/all_gather | solution.py:206
  321.1 10.9 %convert_reduce_fusion = (f32[768]{0:T(1024)}, bf16[2048,768]{1,0:T(8,128)(2,1)S(1)}, bf16[2048,768]{1,0:T(8,128)(2,1)}) fusion(f32[2048,768]{1,0:T(8,128)} %fusion.118, f32[768]{0:T(1024)S(1)} %dynamic-slice_reduce_fusion, bf16[2048,768]{1,0:T(8,128)(2,1)} %all-gather.16.cloned.1.call-done, bf16[768,768]{0,1:T(8,128)(2,1)} %all-gather.14.cloned.1.call-done), kind=kOutput, calls=%fused_computation.112 | convolution fusion | flops 2455239936 | bytes 16914432 | tf_op jit(solution)/shard_map/nd,fd->nf/dot_general | solution.py:207
  333.6 4.6 fusion.119
  338.4 6.5 convolution_convert_fusion
  345.0 51.5 %reduce-scatter.18.cloned.1.call-done = f32[512,768]{1,0:T(8,128)} async-done(((f32[2048,768]{1,0:T(8,128)}), f32[512,768]{1,0:T(8,128)}) %reduce-scatter.18.cloned.1.call-update) | async-done | bytes 1572880 | tf_op jit(solution)/shard_map/reduce_scatter | solution.py:214
  396.6 2.7 multiply_reduce_fusion.2
  400.4 36.6 %reduce-scatter.16.cloned.1.call-done = bf16[512,768]{1,0:T(8,128)(2,1)} async-done(((bf16[2048,768]{1,0:T(8,128)(2,1)}), bf16[512,768]{1,0:T(8,128)(2,1)}) %reduce-scatter.16.cloned.1.call-update) | async-done | bytes 786448 | tf_op jit(solution)/shard_map/reduce_scatter | solution.py:199
  437.0 4.4 fusion.107
  443.6 6.9 fusion.121
  450.6 7.5 fusion.120
  458.2 14.1 %all-gather.18.cloned.1.call-done = bf16[2048,768]{1,0:T(8,128)(2,1)} async-done(((bf16[512,768]{1,0:T(8,128)(2,1)}), bf16[2048,768]{1,0:T(8,128)(2,1)}) %all-gather.18.cloned.1.call-update) | async-done | bytes 3145744 | tf_op jit(solution)/shard_map/all_gather | solution.py:226
  472.2 3.1 convolution_convert_fusion.1
  481.1 32.5 %while.36 = (s32[]{:T(128)}, bf16[2,1024,3,64]{1,3,2,0:T(8,128)(2,1)}, bf16[2,1024,3,64]{1,3,2,0:T(8,128)(2,1)}, bf16[2,1024,3,64]{1,3,2,0:T(8,128)(2,1)}, bf16[...) while((s32[]{:T(128)}, ...), condition=%wide.region_18.19_spmd, body=%wide.region_15.18_spmd.sunk | while | flops 1543271936 | bytes 100059472 | solution.py:233
  488.8 2.6 multiply_reduce_fusion.9
  491.4 1.9 multiply_convert_fusion.5
  504.7 2.6 multiply_reduce_fusion.9
  507.3 1.9 multiply_convert_fusion.5
  513.6 2.0 copy.99
  516.3 4.2 convolution_bitcast_fusion.1
  526.3 6.7 fusion.81
  533.1 7.0 convolution_bitcast_fusion
  541.5 2.0 multiply_subtract_fusion
  543.6 48.1 %reduce-scatter.24.cloned.1.call-done = f32[96,768]{1,0:T(8,128)} async-done(((f32[768,768]{1,0:T(8,128)}), f32[96,768]{1,0:T(8,128)}) %reduce-scatter.24.cloned.1.call-update) | async-done | bytes 294928 | tf_op jit(solution)/shard_map/reduce_scatter | solution.py:278
  591.6 2.2 multiply_subtract_fusion.1
  597.6 59.1 %reduce-scatter.28.cloned.1.call-done = f32[96,192]{1,0:T(8,128)} async-done(((f32[768,192]{1,0:T(8,128)}), f32[96,192]{1,0:T(8,128)}) %reduce-scatter.28.cloned.1.call-update) | async-done | bytes 73744
  659.5 68.7 %reduce-scatter.22.cloned.1.call-done = f32[96,3,192]{2,0,1:T(8,128)} async-done(((f32[768,3,192]{2,0,1:T(8,128)}), f32[96,3,192]{2,0,1:T(8,128)}) %reduce-scatter.22.cloned.1.call-update) | async-done | bytes 221200 | tf_op jit(solution)/shard_map/reduce_scatter | solution.py:276
  728.1 2.2 multiply_subtract_fusion.2
  730.3 57.6 %reduce-scatter.20.cloned.1.call-done = f32[512,768]{1,0:T(8,128)} async-done(((f32[2048,768]{1,0:T(8,128)}), f32[512,768]{1,0:T(8,128)}) %reduce-scatter.20.cloned.1.call-update) | async-done | bytes 1572880 | tf_op jit(solution)/shard_map/reduce_scatter | solution.py:247
  787.9 2.2 fusion.95
  792.6 3.1 fusion.94
  795.7 58.5 %reduce-scatter.30.cloned.1.call-done = f32[96,12]{1,0:T(8,128)} async-done(((f32[768,12]{1,0:T(8,128)}), f32[96,12]{1,0:T(8,128)}) %reduce-scatter.30.cloned.1.call-update) | async-done | bytes 4624
  855.1 5.8 psum.7
  (274 shorter events, 88.2 us)
Async XLA Ops:
  8.0 39.9 %copy-start.23 = (f32[192,96]{1,0:T(8,128)S(1)}, f32[192,96]{1,0:T(8,128)}, u32[]{:S(2)}) copy-start(f32[192,96]{1,0:T(8,128)} %param.36) | copy-start | bytes 221188
  8.0 40.0 %copy-start.19 = (f32[96,3,192]{2,0,1:T(8,128)S(1)}, f32[96,3,192]{2,0,1:T(8,128)}, u32[]{:S(2)}) copy-start(f32[96,3,192]{2,0,1:T(8,128)} %param.35) | copy-start | bytes 663556
  8.0 110.2 %all-gather.8.cloned.1.call-start = ((), (), s32[]{:S(2)}) async-start(), calls=%async_computation.9 | async-start | bytes 3932160 | tf_op jit(solution)/shard_map/all_gather | solution.py:171
  9.5 38.6 %copy-start.33 = (f32[512]{0:T(512)}, f32[512]{0:T(512)S(1)}, u32[]{:S(2)}) copy-start(f32[512]{0:T(512)S(1)} %broadcast_multiply_fusion.5) | copy-start | bytes 6148
  11.0 37.1 %copy-start.35 = (f32[512]{0:T(512)}, f32[512]{0:T(512)S(1)}, u32[]{:S(2)}) copy-start(f32[512]{0:T(512)S(1)} %add_rsqrt_fusion.1) | copy-start | bytes 6148
  44.0 4.1 copy-start.30
  44.6 3.3 copy-start.31
  47.0 169.2 %reduce-scatter.14.cloned.1.call-start = ((), (), s32[]{:S(2)}) async-start(), calls=%async_computation.10 | async-start | bytes 7864320 | tf_op jit(solution)/shard_map/reduce_scatter | solution.py:184
  87.2 34.9 %copy-start.21 = (bf16[768,3,192]{0,2,1:T(8,128)(2,1)}, bf16[768,3,192]{0,2,1:T(8,128)(2,1)S(1)}, u32[]{:S(2)}) copy-start(bf16[768,3,192]{0,2,1:T(8,128)(2,1)S(1)} %copy.91) | copy-start | bytes 2654212
  153.4 5.7 copy-start.1
  159.1 65.1 %all-gather.12.cloned.1.call-start = ((), (), s32[]{:S(2)}) async-start(), calls=%async_computation.12 | async-start | bytes 1327104 | tf_op jit(solution)/shard_map/all_gather | solution.py:159
  160.7 87.4 %all-gather.10.cloned.1.call-start = ((), (), s32[]{:S(2)}) async-start(), calls=%async_computation.11 | async-start | bytes 3932160 | tf_op jit(solution)/shard_map/all_gather | solution.py:194
  219.6 72.9 %all-gather.14.cloned.1.call-start = ((), (), s32[]{:S(2)}) async-start(), calls=%async_computation.13 | async-start | bytes 1327104 | tf_op jit(solution)/shard_map/all_gather | solution.py:160
  221.3 99.7 %all-gather.16.cloned.1.call-start = ((), (), s32[]{:S(2)}) async-start(), calls=%async_computation.15 | async-start | bytes 3932160 | tf_op jit(solution)/shard_map/all_gather | solution.py:206
  222.1 174.5 %reduce-scatter.18.cloned.1.call-start = ((), (), s32[]{:S(2)}) async-start(), calls=%async_computation.16 | async-start | bytes 7864320 | tf_op jit(solution)/shard_map/reduce_scatter | solution.py:214
  321.1 12.5 %copy-start.48 = (bf16[768,768]{1,0:T(8,128)(2,1)S(1)}, bf16[768,768]{1,0:T(8,128)(2,1)}, u32[]{:S(2)}) copy-start(bf16[768,768]{1,0:T(8,128)(2,1)} %all-gather.12.cloned.1.call-done) | copy-start | bytes 3538948
  338.2 98.8 %reduce-scatter.16.cloned.1.call-start = ((), (), s32[]{:S(2)}) async-start(), calls=%async_computation.14 | async-start | bytes 3932160 | tf_op jit(solution)/shard_map/reduce_scatter | solution.py:199
  345.0 92.0 %copy-start.38 = (f32[768]{0:T(1024)S(1)}, f32[768]{0:T(1024)}, u32[]{:S(2)}) copy-start(f32[768]{0:T(1024)} %get-tuple-element.420) | copy-start | bytes 9220
  345.0 127.2 %all-gather.18.cloned.1.call-start = ((), (), s32[]{:S(2)}) async-start(), calls=%async_computation.17 | async-start | bytes 3932160 | tf_op jit(solution)/shard_map/all_gather | solution.py:226
  443.5 98.0 %reduce-scatter.26.cloned.1.call-start = ((), (), s32[]{:S(2)}) async-start(), calls=%async_computation.21 | async-start | bytes 2654208 | tf_op jit(solution)/shard_map/reduce_scatter | solution.py:279
  450.5 141.1 %reduce-scatter.24.cloned.1.call-start = ((), (), s32[]{:S(2)}) async-start(), calls=%async_computation.20 | async-start | bytes 2654208 | tf_op jit(solution)/shard_map/reduce_scatter | solution.py:278
  458.1 198.7 %reduce-scatter.28.cloned.1.call-start = ((), (), s32[]{:S(2)}) async-start(), calls=%async_computation.22 | async-start | bytes 884736
  475.3 5.8 copy-start.2
  475.3 5.8 copy-start.29
  488.8 2.6 copy-start.9
  504.7 2.6 copy-start.9
  513.6 2.6 copy-start.7
  516.3 5.3 copy-start.10
  520.5 207.6 %reduce-scatter.22.cloned.1.call-start = ((), (), s32[]{:S(2)}) async-start(), calls=%async_computation.19 | async-start | bytes 2654208 | tf_op jit(solution)/shard_map/reduce_scatter | solution.py:276
  526.3 6.8 copy-start.22
  533.1 254.8 %reduce-scatter.20.cloned.1.call-start = ((), (), s32[]{:S(2)}) async-start(), calls=%async_computation.18 | async-start | bytes 7864320 | tf_op jit(solution)/shard_map/reduce_scatter | solution.py:247
  540.1 51.5 %copy-start.18 = (f32[96,768]{1,0:T(8,128)S(1)}, f32[96,768]{1,0:T(8,128)}, u32[]{:S(2)}) copy-start(f32[96,768]{1,0:T(8,128)} %param.37) | copy-start | bytes 884740
  540.2 53.6 %copy-start.40 = (f32[768]{0:T(1024)S(1)}, f32[768]{0:T(1024)}, u32[]{:S(2)}) copy-start(f32[768]{0:T(1024)} %get-tuple-element.331) | copy-start | bytes 9220
  540.2 53.6 %copy-start.42 = (f32[768]{0:T(1024)S(1)}, f32[768]{0:T(1024)}, u32[]{:S(2)}) copy-start(f32[768]{0:T(1024)} %get-tuple-element.380) | copy-start | bytes 9220
  540.2 54.2 %copy-start.41 = (f32[768]{0:T(1024)S(1)}, f32[768]{0:T(1024)}, u32[]{:S(2)}) copy-start(f32[768]{0:T(1024)} %get-tuple-element.412) | copy-start | bytes 9220
  540.2 54.8 %copy-start.39 = (f32[768]{0:T(1024)S(1)}, f32[768]{0:T(1024)}, u32[]{:S(2)}) copy-start(f32[768]{0:T(1024)} %get-tuple-element.337) | copy-start | bytes 9220
  540.2 117.5 %copy-start.24 = (f32[192,96]{1,0:T(8,128)S(1)}, f32[192,96]{1,0:T(8,128)}, u32[]{:S(2)}) copy-start(f32[192,96]{1,0:T(8,128)} %param.36) | copy-start | bytes 221188
  540.2 314.0 %reduce-scatter.30.cloned.1.call-start = ((), (), s32[]{:S(2)}) async-start(), calls=%async_computation.23 | async-start | bytes 442368
  541.5 186.7 %copy-start.20 = (f32[96,3,192]{2,0,1:T(8,128)S(1)}, f32[96,3,192]{2,0,1:T(8,128)}, u32[]{:S(2)}) copy-start(f32[96,3,192]{2,0,1:T(8,128)} %param.35) | copy-start | bytes 663556
  543.6 244.4 %copy-start = (bf16[512,768]{1,0:T(8,128)(2,1)S(1)}, bf16[512,768]{1,0:T(8,128)(2,1)}, u32[]{:S(2)}) copy-start(bf16[512,768]{1,0:T(8,128)(2,1)} %param.33) | copy-start | bytes 2359300
  543.6 244.4 %copy-start.32 = (f32[768]{0:T(1024)S(1)}, f32[768]{0:T(1024)}, u32[]{:S(2)}) copy-start(f32[768]{0:T(1024)} %copy-done.31) | copy-start | bytes 9220
  543.6 244.4 %copy-start.34 = (f32[512]{0:T(512)S(1)}, f32[512]{0:T(512)}, u32[]{:S(2)}) copy-start(f32[512]{0:T(512)} %copy-done.33) | copy-start | bytes 6148
  543.6 244.4 %copy-start.36 = (f32[512]{0:T(512)S(1)}, f32[512]{0:T(512)}, u32[]{:S(2)}) copy-start(f32[512]{0:T(512)} %copy-done.35) | copy-start | bytes 6148
  596.7 193.4 %copy-start.44 = (f32[1,768]{1,0:T(1,128)S(1)}, f32[1,768]{1,0:T(1,128)}, u32[]{:S(2)}) copy-start(f32[1,768]{1,0:T(1,128)} %copy-done.43) | copy-start | bytes 9220
  596.7 195.9 %copy-start.4 = (f32[512,768]{1,0:T(8,128)S(1)}, f32[512,768]{1,0:T(8,128)}, u32[]{:S(2)}) copy-start(f32[512,768]{1,0:T(8,128)} %copy-done.3) | copy-start | bytes 4718596
  791.6 69.2 %copy-start.37 = (f32[12,96]{1,0:T(8,128)S(1)}, f32[12,96]{1,0:T(8,128)}, u32[]{:S(2)}) copy-start(f32[12,96]{1,0:T(8,128)} %param.39) | copy-start | bytes 13828
  791.6 69.2 %copy-start.45 = (f32[12,96]{1,0:T(8,128)S(1)}, f32[12,96]{1,0:T(8,128)}, u32[]{:S(2)}) copy-start(f32[12,96]{1,0:T(8,128)} %param.44) | copy-start | bytes 13828
  791.7 69.2 %copy-start.46 = (f32[12,96]{1,0:T(8,128)S(1)}, f32[12,96]{1,0:T(8,128)}, u32[]{:S(2)}) copy-start(f32[12,96]{1,0:T(8,128)} %param.49) | copy-start | bytes 13828
  (25 other events, 30.0 us)
Sparse Core Ops, SparseCore 0:
  47.1 29.4 all-gather.7
  159.2 56.9 reduce-scatter.13
  443.6 28.5 all-gather.17
Sparse Core Ops, SparseCore 1:
  162.3 40.0 all-gather.11
  219.7 28.4 all-gather.9
  251.0 41.5 all-gather.13
  294.2 26.8 all-gather.15
  338.3 58.2 reduce-scatter.17
  399.1 37.8 reduce-scatter.15
  450.6 69.0 reduce-scatter.25
  523.5 68.1 reduce-scatter.23
  595.2 61.6 reduce-scatter.27
  660.3 67.8 reduce-scatter.21
  730.5 57.3 reduce-scatter.19
  792.7 61.5 reduce-scatter.29
where the time goes:
time: 875 us; the launch traced here: 869 us
  waiting for transfers between devices  540 us (62%)
  blocking collectives  107 us (12%)
  matrix products  104 us (12%)
  other arithmetic  50.5 us (6%)
  local copies, waits for them, and re-layouts  48.9 us (6%)
  between operations  16.2 us (2%)
    unnamed x17, waiting for transfers between devices  119 us
    reduce_scatter x1, waiting for transfers between devices, shards(): lax.psum_scatter(grad_qkv, 'row', scatter_dimension=0, tiled=True)  68.7 us
    reduce_scatter x1, waiting for transfers between devices, shards(): lax.psum_scatter(jnp.einsum('nkc,dkc->nd', grad_qkv_low, full_qkv, prefer...  57.6 us
    reduce_scatter x1, waiting for transfers between devices, shards(): lax.psum_scatter(jnp.dot(heads_low, full_out, preferred_element_type=jnp....  55.4 us
    reduce_scatter x1, waiting for transfers between devices, shards(): lax.psum_scatter(jnp.einsum('nf,df->nd', grad_upper, full_up, preferred_e...  51.5 us
    reduce_scatter x1, waiting for transfers between devices, shards(): lax.psum_scatter(grad_up, 'row', scatter_dimension=0, tiled=True)  48.1 us
    all_gather x1, blocking collectives, shards(): lax.all_gather(w_qkv.astype(jnp.bfloat16), 'row', axis=0, tiled=True)  38.1 us
    all_gather x1, waiting for transfers between devices, shards(): lax.all_gather(w_down.astype(jnp.bfloat16), 'row', axis=1, tiled=True)  36.9 us
  transfers between devices with their start and end apart: 15, of which 12 were waited for; matrix products, arithmetic and copies ran while one was open for 14% of the time, Pallas kernels for 0%

commit v1 on v0

v1 whole, which is shorter than its diff:
```python
import jax
import jax.numpy as jnp
from jax import lax
from jax.experimental import pallas as pl
from jax.experimental.pallas import tpu as pltpu
from jax.sharding import PartitionSpec as P

HEAD_DIM = 64
LENGTH = 1024
STEP_NUMBER = 10
VEC_ROWS = 12
PAIR = 2 * HEAD_DIM
QUERY_BLOCK = 256


EPS = 1e-05
BETA_ONE = 0.9
BETA_TWO = 0.999
ADAM_EPS = 1e-08
DECAY = 0.1
RATE_MATRIX = 0.04
RATE_VECTOR = 0.3

F32 = jnp.float32
BF16 = jnp.bfloat16


def normalize_rows(values_in):
    row_mean = jnp.mean(values_in, axis=-1, keepdims=True)
    centred = values_in - row_mean
    row_var = jnp.mean(centred * centred, axis=-1, keepdims=True)
    inv_std = lax.rsqrt(row_var + EPS)
    return (centred * inv_std, inv_std)


def norm_back(grad_in, normed, inv_std):
    mean_grad = jnp.mean(grad_in, axis=-1, keepdims=True)
    mean_cross = jnp.mean(grad_in * normed, axis=-1, keepdims=True)
    return inv_std * (grad_in - mean_grad - normed * mean_cross)


def adamw(weight, moment_one, moment_two, gradient, rate):
    first = BETA_ONE * moment_one + (1 - BETA_ONE) * gradient
    second = BETA_TWO * moment_two + (1 - BETA_TWO) * gradient * gradient
    first_hat = first / (1 - BETA_ONE**STEP_NUMBER)
    second_hat = second / (1 - BETA_TWO**STEP_NUMBER)
    updated = weight - rate * (first_hat / (jnp.sqrt(second_hat) + ADAM_EPS) + DECAY * weight)
    return (updated, first, second)


def gelu_value(value_up):
    return jax.nn.gelu(value_up, approximate=True)


def row_lines(count):
    factors = {8: (4, 2), 64: (2, 8, 4)}.get(count, (count,))
    lines = []
    stride = count
    for size in factors:
        stride //= size
        lines.append(("row", count, size, stride))
    return lines


def place_on(line):
    name, _, size, stride = line
    return lax.axis_index(name) // stride % size


def hop_pairs(line, hop, keep):
    _, count, size, stride = line
    pairs = []
    for index in range(count):
        place = index // stride % size
        if 0 <= place + hop < size and keep(place):
            pairs.append((index, index + hop * stride))
    return pairs


def swap_over(value, line):
    name, count, _, stride = line
    pairs = [(index, index ^ stride) for index in range(count)]
    return lax.ppermute(value, name, pairs)


def gather_line(block, line, dim):
    name, _, size, _ = line
    if size == 1:
        return jnp.expand_dims(block, dim)
    place = place_on(line)
    below, above = [block], [block]
    if size == 2:
        other = swap_over(block, line)
        below.append(other)
        above.append(other)
    else:
        for step in range(1, size):
            below.append(
                lax.ppermute(below[-1], name, hop_pairs(line, 1, lambda at: at >= step - 1))
            )
            above.append(
                lax.ppermute(above[-1], name, hop_pairs(line, -1, lambda at: at <= size - step))
            )
    shape = block.shape[:dim] + (size,) + block.shape[dim:]
    gathered = jnp.broadcast_to(jnp.expand_dims(block, dim), shape)
    for ahead in range(1, size):
        if size == 2:
            piece = above[1]
        else:
            piece = jnp.where(place + ahead < size, above[ahead], below[size - ahead])
        gathered = lax.dynamic_update_slice_in_dim(
            gathered, jnp.expand_dims(piece, dim), (place + ahead) % size, dim
        )
    return gathered


def reduce_line(parts, line, dim):
    name, _, size, _ = line
    place = place_on(line)

    def part(index):
        return lax.dynamic_index_in_dim(parts, index % size, dim, keepdims=False)

    if size == 1:
        return part(0)
    if size == 2:
        return part(place) + swap_over(part(1 - place).astype(BF16), line).astype(F32)
    up_sum = down_sum = None
    for step in range(1, size):
        far = size - step
        up_send, down_send = part(place + far), part(place - far + size)
        if up_sum is not None:
            up_send, down_send = up_send + up_sum, down_send + down_sum
        up_sum = lax.ppermute(
            up_send.astype(BF16), name, hop_pairs(line, 1, lambda at: at + far < size)
        ).astype(F32)
        down_sum = lax.ppermute(
            down_send.astype(BF16), name, hop_pairs(line, -1, lambda at: at - far >= 0)
        ).astype(F32)
    return part(place) + up_sum + down_sum


def gather_far(block, lines):
    for line in reversed(lines[:-1]):
        block = gather_line(block, line, 0)
        if block.ndim > 3:
            block = block.reshape((-1,) + block.shape[2:])
    if len(lines) == 1:
        block = block[None]
    return block


def gather_near(stacked, near, x_line):
    far, rows, cols = stacked.shape
    half = rows // 2
    front, back = stacked[:, :half], stacked[:, half:]
    front_own = gather_line(front, near, 1)
    front_other = swap_over(front_own, x_line)
    back_pair = jnp.stack([back, swap_over(back, x_line)])
    back_pair = gather_line(back_pair, near, 2)

    def joined(front_part, back_part):
        return jnp.stack([front_part, back_part], axis=2).reshape(-1, cols)

    return joined(front_own, back_pair[0]), joined(front_other, back_pair[1])


def reduce_all(own, other, lines, x_line):
    near = lines[-1]
    cols = own.shape[1]
    count, near_size = near[1], near[2]
    rows = own.shape[0] // count
    shape = (count // near_size, near_size, 2, rows // 2, cols)
    own, other = own.reshape(shape), other.reshape(shape)
    front = own[:, :, 0] + swap_over(other[:, :, 0].astype(BF16), x_line).astype(F32)
    front = reduce_line(front, near, 1)
    back_pair = jnp.stack([own[:, :, 1], other[:, :, 1]])
    back_pair = reduce_line(back_pair, near, 2)
    back = back_pair[0] + swap_over(back_pair[1].astype(BF16), x_line).astype(F32)
    total = jnp.concatenate([front, back], axis=1)
    for line in lines[:-1]:
        total = total.reshape((line[2], -1) + total.shape[1:])
        total = reduce_line(total, line, 0)
    return total.reshape(rows, cols)


def sum_everywhere(value):
    for name in ("col", "row"):
        count = lax.axis_size(name)
        stride = 1
        while stride < count:
            value = value + swap_over(value, (name, count, 2, stride))
            stride *= 2
    return value


def dot_nt(left, right):
    return lax.dot_general(left, right, (((1,), (1,)), ((), ())), preferred_element_type=F32)


def dot_nn(left, right):
    return lax.dot_general(left, right, (((1,), (0,)), ((), ())), preferred_element_type=F32)


def lane_pick(half):
    lanes = lax.broadcasted_iota(jnp.int32, (1, PAIR), 1)
    return jnp.where((lanes // HEAD_DIM) == half, 1.0, 0.0).astype(BF16)


def causal_block(size):
    key_at = lax.broadcasted_iota(jnp.int32, (size, size), 0)
    query_at = lax.broadcasted_iota(jnp.int32, (size, size), 1)
    return key_at <= query_at


def attend_kernel(q_ref, k_ref, v_ref, out_ref, lse_ref):
    length = q_ref.shape[0]
    block = min(QUERY_BLOCK, length)
    allowed = causal_block(block)
    values_t = v_ref[...].T
    scaling = jnp.asarray(HEAD_DIM**-0.5, BF16)
    for first in range(0, length, block):
        last = first + block
        query = q_ref[first:last, :] * scaling
        outs = []
        for half in range(2):
            rows = slice(half * HEAD_DIM, (half + 1) * HEAD_DIM)
            query_half = query * lane_pick(half)
            diag = dot_nt(k_ref[first:last, :], query_half)
            diag = jnp.where(allowed, diag, -1e30)
            top = jnp.max(diag, axis=0, keepdims=True)
            if first:
                rest = dot_nt(k_ref[0:first, :], query_half)
                top = jnp.maximum(top, jnp.max(rest, axis=0, keepdims=True))
            diag = jnp.exp(diag - top)
            total = jnp.sum(diag, axis=0, keepdims=True)
            if first:
                rest = jnp.exp(rest - top)
                total = total + jnp.sum(rest, axis=0, keepdims=True)
            inverse = 1.0 / total
            result = dot_nn(values_t[rows, first:last], (diag * inverse).astype(BF16))
            if first:
                result = result + dot_nn(values_t[rows, 0:first], (rest * inverse).astype(BF16))
            outs.append(result)
            lse_ref[0, half : half + 1, first:last] = top + jnp.log(total)
        out_ref[first:last, :] = jnp.concatenate(outs, axis=0).T.astype(BF16)


def attend_forward(qkv):
    length, width = qkv.shape
    pairs = width // (3 * PAIR)

    def lanes(part):
        return pl.BlockSpec((length, PAIR), lambda pair: (0, part * pairs + pair))

    return pl.pallas_call(
        attend_kernel,
        grid=(pairs,),
        in_specs=[lanes(0), lanes(1), lanes(2)],
        out_specs=[lanes(0), pl.BlockSpec((1, 8, length), lambda pair: (pair, 0, 0))],
        out_shape=[
            jax.ShapeDtypeStruct((length, pairs * PAIR), BF16),
            jax.ShapeDtypeStruct((pairs, 8, length), F32),
        ],
        compiler_params=pltpu.CompilerParams(vmem_limit_bytes=40 * 2**20),
        cost_estimate=pl.CostEstimate(
            flops=pairs * 2 * 4 * length * length * HEAD_DIM,
            bytes_accessed=4 * length * pairs * PAIR * 2,
            transcendentals=pairs * length * length,
        ),
        name="attend_forward",
    )(qkv, qkv, qkv)


def attend_back_kernel(q_ref, k_ref, v_ref, go_ref, lse_ref, grad_ref, gk_sum, gv_sum):
    length = q_ref.shape[0]
    pairs = grad_ref.shape[1] // (3 * PAIR)
    block = min(QUERY_BLOCK, length)
    allowed = causal_block(block)
    keys_t = k_ref[...].T
    scaling = jnp.asarray(HEAD_DIM**-0.5, BF16)
    pair = pl.program_id(0)

    def lanes(part):
        return pl.ds(pl.multiple_of((part * pairs + pair) * PAIR, PAIR), PAIR)

    gk_sum[...] = jnp.zeros_like(gk_sum)
    gv_sum[...] = jnp.zeros_like(gv_sum)
    for first in range(0, length, block):
        last = first + block
        query = q_ref[first:last, :] * scaling
        grad_out = go_ref[first:last, :]
        outs = []
        for half in range(2):
            rows = slice(half * HEAD_DIM, (half + 1) * HEAD_DIM)
            pick = lane_pick(half)
            query_half = query * pick
            grad_half = grad_out * pick
            lse = lse_ref[0, half : half + 1, first:last]
            spans = [(first, last)] if first == 0 else [(0, first), (first, last)]
            probs, grads, inner = [], [], None
            for low, high in spans:
                scores = dot_nt(k_ref[low:high, :], query_half)
                if low == first:
                    scores = jnp.where(allowed, scores, -1e30)
                prob = jnp.exp(scores - lse)
                grad_prob = dot_nt(v_ref[low:high, :], grad_half)
                part = jnp.sum(prob * grad_prob, axis=0, keepdims=True)
                inner = part if inner is None else inner + part
                probs.append(prob)
                grads.append(grad_prob)
            result = None
            for (low, high), prob, grad_prob in zip(spans, probs, grads):
                grad_score = (prob * (grad_prob - inner)).astype(BF16)
                gk_sum[low:high, :] += dot_nn(grad_score, query_half)
                gv_sum[low:high, :] += dot_nn(prob.astype(BF16), grad_half)
                part = dot_nn(keys_t[rows, low:high], grad_score)
                result = part if result is None else result + part
            outs.append(result)
        grad_query = jnp.concatenate(outs, axis=0).T * (HEAD_DIM**-0.5)
        grad_ref[first:last, lanes(0)] = grad_query.astype(BF16)
    grad_ref[:, lanes(1)] = gk_sum[...].astype(BF16)
    grad_ref[:, lanes(2)] = gv_sum[...].astype(BF16)


def attend_backward(qkv, grad_heads, lse):
    length, width = qkv.shape
    pairs = width // (3 * PAIR)

    def lanes(part):
        return pl.BlockSpec((length, PAIR), lambda pair: (0, part * pairs + pair))

    return pl.pallas_call(
        attend_back_kernel,
        grid=(pairs,),
        in_specs=[
            lanes(0),
            lanes(1),
            lanes(2),
            lanes(0),
            pl.BlockSpec((1, 8, length), lambda pair: (pair, 0, 0)),
        ],
        out_specs=pl.BlockSpec((length, width), lambda pair: (0, 0)),
        out_shape=jax.ShapeDtypeStruct((length, width), BF16),
        scratch_shapes=[pltpu.VMEM((length, PAIR), F32), pltpu.VMEM((length, PAIR), F32)],
        compiler_params=pltpu.CompilerParams(vmem_limit_bytes=40 * 2**20),
        cost_estimate=pl.CostEstimate(
            flops=pairs * 2 * 10 * length * length * HEAD_DIM,
            bytes_accessed=7 * length * pairs * PAIR * 2,
            transcendentals=pairs * length * length,
        ),
        name="attend_backward",
    )(qkv, qkv, qkv, grad_heads, lse)


def shards(
    tokens,
    cotangent,
    w_qkv,
    w_out,
    w_up,
    w_down,
    vectors,
    first_qkv,
    first_out,
    first_up,
    first_down,
    first_vectors,
    second_qkv,
    second_out,
    second_up,
    second_down,
    second_vectors,
):
    row_index = lax.axis_index("row")
    row_count = lax.axis_size("row")
    col_index = lax.axis_index("col")
    col_count = lax.axis_size("col")
    lines = row_lines(row_count)
    near = lines[-1]
    x_line = ("col", col_count, col_count // 2, 2)
    core_line = ("col", col_count, 2, 1)
    core = col_index % 2
    other_col = col_index ^ 2
    rows_loc, width = tokens.shape
    width_loc = w_qkv.shape[2]
    hidden_loc = w_up.shape[1]
    shard_rows = w_up.shape[0]

    pad = -(3 * width_loc + VEC_ROWS) % 128
    pack_qkv = jnp.concatenate(
        [
            w_qkv.reshape(shard_rows, 3 * width_loc).astype(BF16),
            vectors.T.astype(BF16),
            jnp.zeros((shard_rows, pad), BF16),
        ],
        axis=1,
    )
    pack_up = jnp.concatenate([w_up.astype(BF16), w_out.T.astype(BF16)], axis=1)
    pack_down = w_down.T.astype(BF16)

    def both_halves(mine):
        other = swap_over(mine, core_line)
        return jnp.where(
            core == 0,
            jnp.concatenate([mine, other], axis=0),
            jnp.concatenate([other, mine], axis=0),
        )

    def own_rows(value):
        return lax.dynamic_slice_in_dim(value, core * rows_loc, rows_loc, 0)

    def partner_rows(value):
        return lax.dynamic_slice_in_dim(value, (1 - core) * rows_loc, rows_loc, 0)

    far_qkv = gather_far(pack_qkv, lines)
    pack_up, far_qkv = lax.optimization_barrier((pack_up, far_qkv))
    own_qkv, other_qkv = gather_near(far_qkv, near, x_line)
    far_up = gather_far(pack_up, lines)
    pack_down, far_up = lax.optimization_barrier((pack_down, far_up))
    own_up, other_up = gather_near(far_up, near, x_line)
    far_down = gather_far(pack_down, lines)
    own_down, other_down = gather_near(far_down, near, x_line)

    all_tokens = both_halves(tokens)
    all_cot = both_halves(cotangent)

    vec_all = own_qkv[:, 3 * width_loc : 3 * width_loc + VEC_ROWS].T.astype(F32)

    def cat_blocks(vec_row, size):
        return jnp.concatenate(
            [
                lax.dynamic_slice_in_dim(vec_row, col_index * size, size, 0),
                lax.dynamic_slice_in_dim(vec_row, other_col * size, size, 0),
            ]
        )

    full_qkv = jnp.concatenate(
        [
            block[:, part * width_loc : (part + 1) * width_loc]
            for part in range(3)
            for block in (own_qkv, other_qkv)
        ],
        axis=1,
    )
    full_up = jnp.concatenate([own_up[:, :hidden_loc], other_up[:, :hidden_loc]], axis=1)
    full_out = jnp.concatenate([own_up[:, hidden_loc:], other_up[:, hidden_loc:]], axis=1)
    full_down = jnp.concatenate([own_down, other_down], axis=1)
    partner_out = swap_over(full_out, core_line)
    width_core = 2 * width_loc

    inputs_all = all_tokens.astype(F32)
    normed_one, inv_one = normalize_rows(inputs_all)
    first_in = (normed_one * vec_all[0] + vec_all[1]).astype(BF16)
    bias_qkv = jnp.concatenate(
        [
            cat_blocks(vec_all[2], width_loc),
            jnp.zeros((width_core,), F32),
            cat_blocks(vec_all[3], width_loc),
        ]
    )
    qkv = (dot_nn(first_in, full_qkv) + bias_qkv).astype(BF16)
    heads_low, lse = attend_forward(qkv)
    partner_heads = swap_over(heads_low, core_line)
    attended = dot_nt(heads_low, full_out) + dot_nt(partner_heads, partner_out)
    hidden_state = inputs_all + attended + vec_all[4]
    normed_two, inv_two = normalize_rows(hidden_state)
    second_in = (normed_two * vec_all[5] + vec_all[6]).astype(BF16)
    bias_up = cat_blocks(vec_all[8:].reshape(-1), hidden_loc)
    up_proj = dot_nn(second_in, full_up) + bias_up
    gelu_out, gelu_back = jax.vjp(gelu_value, up_proj)
    activated = gelu_out.astype(BF16)
    down_part = dot_nt(activated, full_down)
    down_other = swap_over(partner_rows(down_part).astype(BF16), core_line).astype(F32)
    mixed_out = own_rows(hidden_state) + own_rows(down_part) + down_other + vec_all[7]

    def tokens_dot(left, right):
        return lax.dot_general(left, right, (((0,), (0,)), ((), ())), preferred_element_type=F32)

    grad_act = dot_nn(all_cot, full_down)
    grad_upper = gelu_back(grad_act)[0].astype(BF16)
    grad_second_part = dot_nt(grad_upper, full_up)
    grad_second_other = swap_over(grad_second_part.astype(BF16), core_line).astype(F32)
    grad_second = grad_second_part + grad_second_other
    grad_hidden = all_cot.astype(F32) + norm_back(grad_second * vec_all[5], normed_two, inv_two)
    grad_hidden_low = grad_hidden.astype(BF16)
    grad_heads = dot_nn(grad_hidden_low, full_out).astype(BF16)
    grad_qkv_low = attend_backward(qkv, grad_heads, lse)
    grad_first_part = dot_nt(grad_qkv_low, full_qkv)
    grad_first_other = swap_over(partner_rows(grad_first_part).astype(BF16), core_line).astype(F32)
    grad_first = own_rows(grad_first_part) + grad_first_other
    token_grad = own_rows(grad_hidden) + norm_back(
        grad_first * vec_all[0], own_rows(normed_one), own_rows(inv_one)
    )

    grad_down = tokens_dot(all_cot, activated)
    grad_up = tokens_dot(second_in, grad_upper)
    grad_out = tokens_dot(grad_hidden_low, heads_low)
    grad_qkv = tokens_dot(first_in, grad_qkv_low)
    owned_down = reduce_all(grad_down[:, :hidden_loc], grad_down[:, hidden_loc:], lines, x_line)
    owned_up = reduce_all(grad_up[:, :hidden_loc], grad_up[:, hidden_loc:], lines, x_line)
    owned_out = reduce_all(grad_out[:, :width_loc], grad_out[:, width_loc:], lines, x_line)
    by_block = grad_qkv.reshape(width, 3, 2, width_loc)
    owned_qkv = reduce_all(
        by_block[:, :, 0].reshape(width, -1), by_block[:, :, 1].reshape(width, -1), lines, x_line
    )

    def placed(part_row, length):
        size = part_row.shape[0] // 2
        start = jnp.zeros((length,), F32)
        start = lax.dynamic_update_slice_in_dim(start, part_row[:size], col_index * size, 0)
        return lax.dynamic_update_slice_in_dim(start, part_row[size:], other_col * size, 0)

    bias_sums = jnp.sum(grad_qkv_low.astype(F32), axis=0)
    front_rows = jnp.stack(
        [
            jnp.sum(grad_first_part * normed_one, axis=0),
            jnp.sum(grad_first_part, axis=0),
            placed(bias_sums[:width_core], width),
            placed(bias_sums[2 * width_core :], width),
            0.5 * jnp.sum(grad_hidden, axis=0),
            jnp.sum(grad_second_part * normed_two, axis=0),
            jnp.sum(grad_second_part, axis=0),
            jnp.sum(cotangent.astype(F32), axis=0),
        ]
    )
    grad_bias_up = jnp.sum(grad_upper.astype(F32), axis=0)
    up_rows = placed(grad_bias_up, hidden_loc * col_count).reshape(-1, width)
    grad_vec = sum_everywhere(jnp.concatenate([front_rows, up_rows], axis=0))
    owned_vec = lax.dynamic_slice_in_dim(grad_vec, row_index * shard_rows, shard_rows, 1)

    new_qkv, new_first_qkv, new_second_qkv = adamw(
        w_qkv, first_qkv, second_qkv, owned_qkv.reshape(w_qkv.shape), RATE_MATRIX
    )
    new_out, new_first_out, new_second_out = adamw(
        w_out, first_out, second_out, owned_out.T, RATE_MATRIX
    )
    new_up, new_first_up, new_second_up = adamw(w_up, first_up, second_up, owned_up, RATE_MATRIX)
    new_down, new_first_down, new_second_down = adamw(
        w_down, first_down, second_down, owned_down.T, RATE_MATRIX
    )
    new_vectors, new_first_vectors, new_second_vectors = adamw(
        vectors, first_vectors, second_vectors, owned_vec, RATE_VECTOR
    )
    return (
        mixed_out,
        token_grad,
        new_qkv,
        new_out,
        new_up,
        new_down,
        new_vectors,
        new_first_qkv,
        new_first_out,
        new_first_up,
        new_first_down,
        new_first_vectors,
        new_second_qkv,
        new_second_out,
        new_second_up,
        new_second_down,
        new_second_vectors,
    )


def solution(mesh):
    by_token = P(("row", "col"), None)
    weights = (
        P("row", None, "col"),
        P("col", "row"),
        P("row", "col"),
        P("col", "row"),
        P(None, "row"),
    )
    return jax.shard_map(
        shards,
        mesh=mesh,
        in_specs=(by_token, by_token) + weights * 3,
        out_specs=(by_token, by_token) + weights * 3,
        check_vma=False,
    )
```

time: 875 us -> 472 us (0.54)
  waiting for transfers between devices: 540 us -> 86.7 us
  starting transfers between devices: 0.99 us -> 126 us
  blocking collectives: 107 us -> 0 us
  local copies, waits for them, and re-layouts: 48.9 us -> 113 us
  matrix products: 104 us -> 49.3 us
  Pallas kernels: 0 us -> 28.1 us
  between operations: 16.2 us -> 3.23 us
    reduce_scatter x7 -> x0, waiting for transfers between devices: 318 us -> none  [the longest x1 68.7 us: shards(): lax.psum_scatter(grad_qkv, 'row', scatter_dimension=0, tiled=True)]
    ppermute x0 -> x82, starting transfers between devices: none -> 126 us  [the longest x12 46.2 us: reduce_line(): lax.ppermute(up_send.astype(BF16), name, hop_pairs(line, 1, lambda at: at...]
    unnamed x17 -> x0, waiting for transfers between devices: 119 us -> none
    all_gather x6 -> x0, waiting for transfers between devices: 103 us -> none  [the longest x1 36.9 us: shards(): lax.all_gather(w_down.astype(jnp.bfloat16), 'row', axis=1, tiled=True)]
    all_gather x3 -> x0, blocking collectives: 101 us -> none  [the longest x1 38.1 us: shards(): lax.all_gather(w_qkv.astype(jnp.bfloat16), 'row', axis=0, tiled=True)]
    ppermute x0 -> x82, waiting for transfers between devices: none -> 86.7 us  [the longest x40 51.7 us: swap_over(): return lax.ppermute(value, name, pairs)]
    dot_general x38 -> x13, matrix products: 95.9 us -> 49.3 us  [the longest x4 19 us: dot_nn(): lax.dot_general(left, right, (((1,), (0,)), ((), ())), preferred_element_...]
    pallas_call x0 -> x2, Pallas kernels: none -> 28.1 us  [the longest x1 15.7 us: attend_backward(): pl.pallas_call(attend_back_kernel, grid=(pairs,), in_specs=[lanes(0), lan...]
  transfers between devices with their start and end apart: 15 -> 82, of which waited for: 12 -> 29; matrix products, arithmetic and copies ran while one was open for 14% -> 35% of each run, Pallas kernels for 0% -> 3%
where the time goes in v1:
time: 472 us; the launch traced here: 463 us
  starting transfers between devices  126 us (27%)
  local copies, waits for them, and re-layouts  113 us (24%)
  waiting for transfers between devices  86.7 us (18%)
  other arithmetic  57 us (12%)
  matrix products  49.3 us (10%)
  Pallas kernels  28.1 us (6%)
    ppermute x40, waiting for transfers between devices, swap_over(): return lax.ppermute(value, name, pairs)  51.7 us
    ppermute x12, starting transfers between devices, reduce_line(): lax.ppermute(up_send.astype(BF16), name, hop_pairs(line, 1, lambda at: at...  46.2 us
    ppermute x40, starting transfers between devices, swap_over(): return lax.ppermute(value, name, pairs)  35.9 us
    ppermute x9, waiting for transfers between devices, gather_line(): lax.ppermute(above[-1], name, hop_pairs(line, -1, lambda at: at <= size -...  25.5 us
    unnamed x216, local copies, waits for them, and re-layouts  25.3 us
    ppermute x9, starting transfers between devices, gather_line(): lax.ppermute(below[-1], name, hop_pairs(line, 1, lambda at: at >= step - 1))  20.1 us
    dot_general x4, matrix products, dot_nn(): lax.dot_general(left, right, (((1,), (0,)), ((), ())), preferred_element_...  19 us
    pallas_call x1, Pallas kernels, attend_backward(): pl.pallas_call(attend_back_kernel, grid=(pairs,), in_specs=[lanes(0), lan...  15.7 us
  transfers between devices with their start and end apart: 82, of which 29 were waited for; matrix products, arithmetic and copies ran while one was open for 35% of the time, Pallas kernels for 3%

profile of v1, /device:TPU:0, one launch (start us, length us, event | category | flops | bytes accessed | tf_op | source)
XLA Modules:
  0.0 462.6 jit_solution(2893857472049550274)
XLA Ops:
  2.8 4.9 %collective-permute-start.2 = (bf16[96,640]{0,1:T(8,128)(2,1)S(1)}, bf16[96,640]{0,1:T(8,128)(2,1)S(1)}, u32[]{:S(2)}, u32[]{:S(2)}) collective-permute-start(bf16[96,640]{0,1:T(8,128)(2,1)S(1)} %maximum_maximum_fusion), channel_id=1, source_target_pairs={{0,8},{4,12},{8,16},{12,20},{16,24},{20,28},{1,9},{5,13},{9,17},{1... | collective-permute-start | bytes 368648 | tf_op jit(solution)/shard_map/ppermute | solution.py:99
  18.4 5.6 %collective-permute-done.5 = bf16[96,640]{0,1:T(8,128)(2,1)} collective-permute-done((bf16[96,640]{0,1:T(8,128)(2,1)S(1)}, bf16[96,640]{0,1:T(8,128)(2,1)}, u32[]{:S(2)}, u32[]{:S(2)}) %collective-permute-start.5) | collective-permute-done | bytes 122912 | tf_op jit(solution)/shard_map/ppermute | solution.py:102
  27.9 5.5 %collective-permute-done.6 = bf16[96,640]{0,1:T(8,128)(2,1)} collective-permute-done((bf16[96,640]{0,1:T(8,128)(2,1)}, bf16[96,640]{0,1:T(8,128)(2,1)}, u32[]{:S(2)}, u32[]{:S(2)}) %collective-permute-start.6) | collective-permute-done | bytes 122912 | tf_op jit(solution)/shard_map/ppermute | solution.py:102
  50.6 4.6 collective-permute-start.12
  63.8 4.4 collective-permute-done.15
  72.2 4.4 collective-permute-done.16
  78.0 5.2 %collective-permute-start.24 = (bf16[96,768]{1,0:T(8,128)(2,1)S(1)}, bf16[96,768]{1,0:T(8,128)(2,1)}, u32[]{:S(2)}, u32[]{:S(2)}) collective-permute-start(bf16[96,768]{1,0:T(8,128)(2,1)S(1)} %convert_bitcast_fusion.1), channel_id=1, source_target_pairs={{0,8},{4,12},{8,16},{12,20},{16,24},{20,28},{1,9},{5,13},{9,17},{1... | collective-permute-start | bytes 442376 | tf_op jit(solution)/shard_map/ppermute | solution.py:99
  95.3 4.4 add_convert_fusion.q_ref.k_ref.v_ref
  99.7 12.4 %attend_forward.1 = (bf16[1024,384]{1,0:T(8,128)(2,1)S(1)}, f32[3,8,1024]{2,1,0:T(8,128)S(1)}) custom-call(bf16[1024,1152]{1,0:T(8,128)(2,1)S(1)} %add_convert_fusion.q_ref.k_ref.v_ref, bf16[1024,1152]{1,0:T(8,128)(2,1)S(1)} %add_convert_fusion.q_ref.k_ref.v_ref, bf16[1024,1152]{1,0:T(8,128)(2,1)S(1)} %add_convert_fusion.q_ref.k_ref.v_ref), custom_call_target="tpu_custom_call" | custom-call | flops 1610612736 | bytes 3145728 | tf_op jit(solution)/shard_map/attend_forward/pallas_call | solution.py:256
  129.4 4.6 collective-permute-done.30
  135.5 9.6 %collective-permute-done.29 = bf16[4,48,768]{2,1,0:T(8,128)(2,1)S(1)} collective-permute-done((bf16[4,48,768]{2,1,0:T(8,128)(2,1)S(1)}, bf16[4,48,768]{2,1,0:T(8,128)(2,1)S(1)}, u32[]{:S(2)}, u32[]{:S(2)}) %collective-permute-start.29) | collective-permute-done | bytes 294944 | tf_op jit(solution)/shard_map/ppermute | solution.py:83
  148.1 6.4 %collective-permute-done.20 = bf16[4,2,48,960]{3,2,1,0:T(8,128)(2,1)S(1)} collective-permute-done((bf16[4,2,48,960]{3,2,1,0:T(8,128)(2,1)S(1)}, bf16[4,2,48,960]{3,2,1,0:T(8,128)(2,1)S(1)}, u32[]{:S(2)}, u32[]{:S(2)}) %collective-permute-start.20) | collective-permute-done | bytes 737312 | tf_op jit(solution)/shard_map/ppermute | solution.py:83
  156.3 3.8 collective-permute-done.31
  160.3 4.8 %collective-permute-done.32 = bf16[4,2,48,768]{3,2,1,0:T(8,128)(2,1)S(1)} collective-permute-done((bf16[4,2,48,768]{3,2,1,0:T(8,128)(2,1)S(1)}, bf16[4,2,48,768]{3,2,1,0:T(8,128)(2,1)S(1)}, u32[]{:S(2)}, u32[]{:S(2)}) %collective-permute-start.32) | collective-permute-done | bytes 589856 | tf_op jit(solution)/shard_map/ppermute | solution.py:83
  169.1 3.0 fusion.14
  174.9 10.6 %convert_reduce_fusion = (f32[1536]{0:T(1024)}, bf16[1024,1536]{1,0:T(8,128)(2,1)S(1)}) fusion(f32[1024,1536]{1,0:T(8,128)S(1)} %fusion.14, f32[1536]{0:T(1024)S(1)} %pad_maximum_fusion.19, bf16[768,768]{1,0:T(8,128)(2,1)S(1)} %bitcast.257, bf16[768,768]{1,0:T(8,128)(2,1)S(1)} %bitcast.259, bf16[512,768]{0,1:T(8,128)(2,1)} %collective-permute-done.34, ...), kind=kOutput, calls=%fused_computation.9 | convolution fusion | flops 2463889920 | bytes 13381633 | tf_op jit(solution)/shard_map/dot_general | solution.py:202
  185.5 4.9 %fusion.133 = (f32[768]{0:T(1024)}, f32[1024,768]{1,0:T(8,128)}) fusion(bf16[1024,1536]{1,0:T(8,128)(2,1)S(1)} %get-tuple-element.165, bf16[768,768]{1,0:T(8,128)(2,1)S(1)} %slice.317, bf16[768,768]{1,0:T(8,128)(2,1)S(1)} %slice.316), kind=kOutput, calls=%fused_computation.336 | convolution fusion | flops 2421423360 | bytes 8653824 | tf_op jit(solution)/shard_map/dot_general | solution.py:198
  198.1 3.6 copy.95
  201.7 3.5 convert_element_type.395
  211.5 6.8 %fusion.110 = f32[768,1536]{1,0:T(8,128)S(1)} fusion(bf16[512,768]{0,1:T(8,128)(2,1)} %collective-permute-done.34, bf16[512,768]{0,1:T(8,128)(2,1)} %copy.92, pred[]{:T(512)S(6)} %eq.86, f32[1024,1536]{1,0:T(8,128)} %copy-done.98, f32[1536]{0:T(1024)S(1)} %copy-done.88), kind=kOutput, calls=%fused_computation.318 | convolution fusion | flops 2438725632 | bytes 12589057 | tf_op jit(solution)/shard_map/dot_general | solution.py:478
  232.4 5.3 %collective-permute-done.69 = bf16[2,4,48,768]{3,2,1,0:T(8,128)(2,1)} collective-permute-done((bf16[2,4,48,768]{3,2,1,0:T(8,128)(2,1)}, bf16[2,4,48,768]{3,2,1,0:T(8,128)(2,1)}, u32[]{:S(2)}, u32[]{:S(2)}) %collective-permute-start.69) | collective-permute-done | bytes 589856 | tf_op jit(solution)/shard_map/ppermute | solution.py:83
  249.0 3.0 copy.128
  254.7 4.5 collective-permute-start.61
  264.5 3.3 collective-permute-start.62
  267.9 3.0 collective-permute-start.72
  271.6 5.0 %collective-permute-start.63 = (bf16[1,96,768]{2,1,0:T(8,128)(2,1)S(1)}, bf16[1,96,768]{2,1,0:T(8,128)(2,1)S(1)}, u32[]{:S(2)}, u32[]{:S(2)}) collective-permute-start(bf16[1,96,768]{2,1,0:T(8,128)(2,1)S(1)} %get-tuple-element.115), channel_id=1, source_target_pairs={{0,8},{4,12},{8,16},{12,20},{16,24},{20,28},{1,9},{5,13},{9,17},{1... | collective-permute-start | bytes 442376 | tf_op jit(solution)/shard_map/ppermute | solution.py:134
  277.4 5.2 %collective-permute-start.73 = (bf16[1,96,768]{2,1,0:T(8,128)(2,1)S(1)}, bf16[1,96,768]{2,1,0:T(8,128)(2,1)S(1)}, u32[]{:S(2)}, u32[]{:S(2)}) collective-permute-start(bf16[1,96,768]{2,1,0:T(8,128)(2,1)S(1)} %get-tuple-element.111), channel_id=1, source_target_pairs={{0,8},{4,12},{8,16},{12,20},{16,24},{20,28},{1,9},{5,13},{9,17},{1... | collective-permute-start | bytes 442376 | tf_op jit(solution)/shard_map/ppermute | solution.py:134
  285.5 5.0 %collective-permute-done.66 = bf16[1,96,768]{2,1,0:T(8,128)(2,1)S(1)} collective-permute-done((bf16[1,96,768]{2,1,0:T(8,128)(2,1)S(1)}, bf16[1,96,768]{2,1,0:T(8,128)(2,1)S(1)}, u32[]{:S(2)}, u32[]{:S(2)}) %collective-permute-start.66) | collective-permute-done | bytes 147488 | tf_op jit(solution)/shard_map/ppermute | solution.py:137
  293.9 3.3 multiply_reduce_fusion
  297.3 5.0 %fusion.113 = (f32[768]{0:T(1024)}, f32[1024,768]{0,1:T(8,128)S(1)}) fusion(f32[1024]{0:T(1024)S(1)} %broadcast_multiply_fusion.1, f32[1024,768]{0,1:T(8,128)S(1)} %copy-done.9, f32[1024]{0:T(1024)S(1)} %broadcast_multiply_fusion.3, f32[1024]{0:T(1024)S(1)} %broadcast_multiply_fusion.2, f32[768]{0:T(1024)S(1)} %copy-done.78, f32[1024,768]{0,1:T(8,128)S(1)} %copy-done.2, ...), kind=kLoop, calls=%fused_computation.320 | loop fusion | flops 16514304 | bytes 12605441 | tf_op jit(solution)/shard_map/reduce_sum | solution.py:521
  305.1 15.7 %attend_backward.1 = bf16[1024,1152]{1,0:T(8,128)(2,1)S(1)} custom-call(bf16[1024,1152]{1,0:T(8,128)(2,1)S(1)} %add_convert_fusion.q_ref.k_ref.v_ref, bf16[1024,1152]{1,0:T(8,128)(2,1)S(1)} %add_convert_fusion.q_ref.k_ref.v_ref, bf16[1024,1152]{1,0:T(8,128)(2,1)S(1)} %add_convert_fusion.q_ref.k_ref.v_ref, ...), custom_call_target="tpu_custom_call" | custom-call | flops 4026531840 | bytes 5505024 | tf_op jit(solution)/shard_map/attend_backward/pallas_call | solution.py:333
  320.8 4.5 fusion.132
  326.4 3.9 copy.96
  332.7 3.9 fusion.109
  338.7 2.9 copy.100
  341.6 2.9 reshape_reshape_squeeze.6
  344.5 3.0 slice_bitcast_fusion.1
  347.4 2.9 copy.102
  365.0 4.3 multiply_reduce_fusion.1
  397.3 4.1 collective-permute-start.51
  404.9 3.9 collective-permute-start.52
  412.0 4.1 collective-permute-done.81
  422.1 4.4 collective-permute-done.40
  428.3 5.2 %collective-permute-start.41 = (bf16[1,96,576]{2,1,0:T(8,128)(2,1)}, bf16[1,96,576]{2,1,0:T(8,128)(2,1)}, u32[]{:S(2)}, u32[]{:S(2)}) collective-permute-start(bf16[1,96,576]{2,1,0:T(8,128)(2,1)} %get-tuple-element.125), channel_id=1, source_target_pairs={{0,8},{4,12},{1,9},{5,13},{2,10},{6,14},{3,11},{7,15}} | collective-permute-start | bytes 331784 | tf_op jit(solution)/shard_map/ppermute | solution.py:134
  437.7 3.9 collective-permute-start.42
  444.9 5.0 %collective-permute-start.43 = (bf16[1,96,576]{2,1,0:T(8,128)(2,1)S(1)}, bf16[1,96,576]{2,1,0:T(8,128)(2,1)S(1)}, u32[]{:S(2)}, u32[]{:S(2)}) collective-permute-start(bf16[1,96,576]{2,1,0:T(8,128)(2,1)S(1)} %get-tuple-element.123), channel_id=1, source_target_pairs={{0,8},{4,12},{8,16},{12,20},{16,24},{20,28},{1,9},{5,13},{9,17},{1... | collective-permute-start | bytes 331784 | tf_op jit(solution)/shard_map/ppermute | solution.py:134
  451.4 2.9 multiply_add_fusion.1
  454.2 3.2 copy.129
  (544 shorter events, 223.1 us)
Async XLA Ops:
  10.5 58.5 %collective-permute-start = (bf16[512,768]{0,1:T(8,128)(2,1)S(1)}, bf16[512,768]{0,1:T(8,128)(2,1)S(1)}, u32[]{:S(2)}, u32[]{:S(2)}) collective-permute-start(bf16[512,768]{0,1:T(8,128)(2,1)S(1)} %copy.71), channel_id=1, source_target_pairs={{0,1},{1,0},{2,3},{3,2},{4,5},{5,4},{6,7},{7,6},{8,9},{9,8},{10,11... | collective-permute-start | bytes 2359304 | tf_op jit(solution)/shard_map/ppermute | solution.py:83
  15.3 8.7 %collective-permute-start.5 = (bf16[96,640]{0,1:T(8,128)(2,1)S(1)}, bf16[96,640]{0,1:T(8,128)(2,1)}, u32[]{:S(2)}, u32[]{:S(2)}) collective-permute-start(bf16[96,640]{0,1:T(8,128)(2,1)S(1)} %collective-permute-done.1), channel_id=1, source_target_pairs={{8,0},{12,4},{16,8},{20,12},{9,1},{13,5},{17,9},{21,13},{10,2},{14... | collective-permute-start | bytes 368648 | tf_op jit(solution)/shard_map/ppermute | solution.py:102
  17.6 9.5 %collective-permute-start.4 = (bf16[96,640]{0,1:T(8,128)(2,1)}, bf16[96,640]{0,1:T(8,128)(2,1)S(1)}, u32[]{:S(2)}, u32[]{:S(2)}) collective-permute-start(bf16[96,640]{0,1:T(8,128)(2,1)} %collective-permute-done.3), channel_id=1, source_target_pairs={{16,24},{20,28},{17,25},{21,29},{18,26},{22,30},{19,27},{23,31}} | collective-permute-start | bytes 368648 | tf_op jit(solution)/shard_map/ppermute | solution.py:99
  38.9 20.1 %collective-permute-start.8 = (bf16[4,48,640]{2,1,0:T(8,128)(2,1)}, bf16[4,48,640]{2,1,0:T(8,128)(2,1)}, u32[]{:S(2)}, u32[]{:S(2)}) collective-permute-start(bf16[4,48,640]{2,1,0:T(8,128)(2,1)} %get-tuple-element.145), channel_id=1, source_target_pairs={{0,2},{1,3},{2,0},{3,1},{4,6},{5,7},{6,4},{7,5},{8,10},{9,11},{10,... | collective-permute-start | bytes 737288 | tf_op jit(solution)/shard_map/ppermute | solution.py:83
  56.9 118.1 %collective-permute-start.34 = (bf16[512,768]{0,1:T(8,128)(2,1)}, bf16[512,768]{0,1:T(8,128)(2,1)}, u32[]{:S(2)}, u32[]{:S(2)}) collective-permute-start(bf16[512,768]{0,1:T(8,128)(2,1)} %copy.92), channel_id=1, source_target_pairs={{0,1},{1,0},{2,3},{3,2},{4,5},{5,4},{6,7},{7,6},{8,9},{9,8},{10,11... | collective-permute-start | bytes 2359304 | tf_op jit(solution)/shard_map/ppermute | solution.py:83
  59.0 9.3 %collective-permute-start.15 = (bf16[96,960]{1,0:T(8,128)(2,1)S(1)}, bf16[96,960]{1,0:T(8,128)(2,1)S(1)}, u32[]{:S(2)}, u32[]{:S(2)}) collective-permute-start(bf16[96,960]{1,0:T(8,128)(2,1)S(1)} %collective-permute-done.11), channel_id=1, source_target_pairs={{8,0},{12,4},{16,8},{20,12},{9,1},{13,5},{17,9},{21,13},{10,2},{14... | collective-permute-start | bytes 552968 | tf_op jit(solution)/shard_map/ppermute | solution.py:102
  61.6 22.7 %collective-permute-start.9 = (bf16[2,4,48,640]{3,2,1,0:T(8,128)(2,1)S(1)}, bf16[2,4,48,640]{3,2,1,0:T(8,128)(2,1)S(1)}, u32[]{:S(2)}, u32[]{:S(2)}) collective-permute-start(bf16[2,4,48,640]{3,2,1,0:T(8,128)(2,1)S(1)} %pad_maximum_fusion.17), channel_id=1, source_target_pairs={{0,4},{4,0},{8,12},{12,8},{16,20},{20,16},{24,28},{28,24},{1,5},{5... | collective-permute-start | bytes 1474568 | tf_op jit(solution)/shard_map/ppermute | solution.py:83
  63.2 26.9 %collective-permute-start.10 = (bf16[4,2,48,640]{3,2,1,0:T(8,128)(2,1)S(1)}, bf16[4,2,48,640]{3,2,1,0:T(8,128)(2,1)S(1)}, u32[]{:S(2)}, u32[]{:S(2)}) collective-permute-start(bf16[4,2,48,640]{3,2,1,0:T(8,128)(2,1)S(1)} %bitcast_dynamic-update-slice_fusion.5), channel_id=1, source_target_pairs={{0,2},{1,3},{2,0},{3,1},{4,6},{5,7},{6,4},{7,5},{8,10},{9,11},{10,... | collective-permute-start | bytes 1474568 | tf_op jit(solution)/shard_map/ppermute | solution.py:83
  76.6 10.6 %collective-permute-start.23 = (bf16[96,768]{1,0:T(8,128)(2,1)S(1)}, bf16[96,768]{1,0:T(8,128)(2,1)}, u32[]{:S(2)}, u32[]{:S(2)}) collective-permute-start(bf16[96,768]{1,0:T(8,128)(2,1)S(1)} %convert_bitcast_fusion.1), channel_id=1, source_target_pairs={{8,0},{12,4},{16,8},{20,12},{24,16},{28,20},{9,1},{13,5},{17,9},{2... | collective-permute-start | bytes 442376 | tf_op jit(solution)/shard_map/ppermute | solution.py:102
  78.0 10.9 %collective-permute-start.24 = (bf16[96,768]{1,0:T(8,128)(2,1)S(1)}, bf16[96,768]{1,0:T(8,128)(2,1)}, u32[]{:S(2)}, u32[]{:S(2)}) collective-permute-start(bf16[96,768]{1,0:T(8,128)(2,1)S(1)} %convert_bitcast_fusion.1), channel_id=1, source_target_pairs={{0,8},{4,12},{8,16},{12,20},{16,24},{20,28},{1,9},{5,13},{9,17},{1... | collective-permute-start | bytes 442376 | tf_op jit(solution)/shard_map/ppermute | solution.py:99
  84.3 32.1 %collective-permute-start.18 = (bf16[4,48,960]{2,1,0:T(8,128)(2,1)}, bf16[4,48,960]{2,1,0:T(8,128)(2,1)}, u32[]{:S(2)}, u32[]{:S(2)}) collective-permute-start(bf16[4,48,960]{2,1,0:T(8,128)(2,1)} %get-tuple-element.139), channel_id=1, source_target_pairs={{0,2},{1,3},{2,0},{3,1},{4,6},{5,7},{6,4},{7,5},{8,10},{9,11},{10,... | collective-permute-start | bytes 1105928 | tf_op jit(solution)/shard_map/ppermute | solution.py:83
  87.2 39.4 %collective-permute-start.17 = (bf16[4,48,960]{2,1,0:T(8,128)(2,1)}, bf16[4,48,960]{2,1,0:T(8,128)(2,1)}, u32[]{:S(2)}, u32[]{:S(2)}) collective-permute-start(bf16[4,48,960]{2,1,0:T(8,128)(2,1)} %get-tuple-element.137), channel_id=1, source_target_pairs={{0,4},{4,0},{8,12},{12,8},{16,20},{20,16},{24,28},{28,24},{1,5},{5... | collective-permute-start | bytes 1105928 | tf_op jit(solution)/shard_map/ppermute | solution.py:83
  88.8 26.0 %collective-permute-start.25 = (bf16[96,768]{1,0:T(8,128)(2,1)}, bf16[96,768]{1,0:T(8,128)(2,1)}, u32[]{:S(2)}, u32[]{:S(2)}) collective-permute-start(bf16[96,768]{1,0:T(8,128)(2,1)} %collective-permute-done.24), channel_id=1, source_target_pairs={{8,16},{12,20},{16,24},{20,28},{9,17},{13,21},{17,25},{21,29},{10,... | collective-permute-start | bytes 442376 | tf_op jit(solution)/shard_map/ppermute | solution.py:99
  90.2 26.2 %collective-permute-start.27 = (bf16[96,768]{1,0:T(8,128)(2,1)}, bf16[96,768]{1,0:T(8,128)(2,1)}, u32[]{:S(2)}, u32[]{:S(2)}) collective-permute-start(bf16[96,768]{1,0:T(8,128)(2,1)} %collective-permute-done.23), channel_id=1, source_target_pairs={{8,0},{12,4},{16,8},{20,12},{9,1},{13,5},{17,9},{21,13},{10,2},{14... | collective-permute-start | bytes 442376 | tf_op jit(solution)/shard_map/ppermute | solution.py:102
  116.3 49.1 %collective-permute-start.21 = (bf16[1024,384]{1,0:T(8,128)(2,1)S(1)}, bf16[1024,384]{1,0:T(8,128)(2,1)S(1)}, u32[]{:S(2)}, u32[]{:S(2)}) collective-permute-start(bf16[1024,384]{1,0:T(8,128)(2,1)S(1)} %get-tuple-element.24), channel_id=1, source_target_pairs={{0,1},{1,0},{2,3},{3,2},{4,5},{5,4},{6,7},{7,6},{8,9},{9,8},{10,11... | collective-permute-start | bytes 2359304 | tf_op jit(solution)/shard_map/ppermute | solution.py:83
  116.4 8.6 %collective-permute-start.28 = (bf16[96,768]{1,0:T(8,128)(2,1)}, bf16[96,768]{1,0:T(8,128)(2,1)S(1)}, u32[]{:S(2)}, u32[]{:S(2)}) collective-permute-start(bf16[96,768]{1,0:T(8,128)(2,1)} %collective-permute-done.27), channel_id=1, source_target_pairs={{8,0},{12,4},{9,1},{13,5},{10,2},{14,6},{11,3},{15,7}} | collective-permute-start | bytes 442376 | tf_op jit(solution)/shard_map/ppermute | solution.py:102
  118.9 26.9 %collective-permute-start.19 = (bf16[2,4,48,960]{3,2,1,0:T(8,128)(2,1)S(1)}, bf16[2,4,48,960]{3,2,1,0:T(8,128)(2,1)S(1)}, u32[]{:S(2)}, u32[]{:S(2)}) collective-permute-start(bf16[2,4,48,960]{3,2,1,0:T(8,128)(2,1)S(1)} %pad_maximum_fusion.14), channel_id=1, source_target_pairs={{0,4},{4,0},{8,12},{12,8},{16,20},{20,16},{24,28},{28,24},{1,5},{5... | collective-permute-start | bytes 2211848 | tf_op jit(solution)/shard_map/ppermute | solution.py:83
  125.1 8.9 %collective-permute-start.30 = (bf16[4,48,768]{2,1,0:T(8,128)(2,1)S(1)}, bf16[4,48,768]{2,1,0:T(8,128)(2,1)S(1)}, u32[]{:S(2)}, u32[]{:S(2)}) collective-permute-start(bf16[4,48,768]{2,1,0:T(8,128)(2,1)S(1)} %get-tuple-element.142), channel_id=1, source_target_pairs={{0,2},{1,3},{2,0},{3,1},{4,6},{5,7},{6,4},{7,5},{8,10},{9,11},{10,... | collective-permute-start | bytes 884744 | tf_op jit(solution)/shard_map/ppermute | solution.py:83
  126.7 18.5 %collective-permute-start.29 = (bf16[4,48,768]{2,1,0:T(8,128)(2,1)S(1)}, bf16[4,48,768]{2,1,0:T(8,128)(2,1)S(1)}, u32[]{:S(2)}, u32[]{:S(2)}) collective-permute-start(bf16[4,48,768]{2,1,0:T(8,128)(2,1)S(1)} %get-tuple-element.140), channel_id=1, source_target_pairs={{0,4},{4,0},{8,12},{12,8},{16,20},{20,16},{24,28},{28,24},{1,5},{5... | collective-permute-start | bytes 884744 | tf_op jit(solution)/shard_map/ppermute | solution.py:83
  134.0 20.5 %collective-permute-start.20 = (bf16[4,2,48,960]{3,2,1,0:T(8,128)(2,1)S(1)}, bf16[4,2,48,960]{3,2,1,0:T(8,128)(2,1)S(1)}, u32[]{:S(2)}, u32[]{:S(2)}) collective-permute-start(bf16[4,2,48,960]{3,2,1,0:T(8,128)(2,1)S(1)} %bitcast_dynamic-update-slice_fusion.3), channel_id=1, source_target_pairs={{0,2},{1,3},{2,0},{3,1},{4,6},{5,7},{6,4},{7,5},{8,10},{9,11},{10,... | collective-permute-start | bytes 2211848 | tf_op jit(solution)/shard_map/ppermute | solution.py:83
  145.2 14.9 %collective-permute-start.31 = (bf16[2,4,48,768]{3,2,1,0:T(8,128)(2,1)S(1)}, bf16[2,4,48,768]{3,2,1,0:T(8,128)(2,1)S(1)}, u32[]{:S(2)}, u32[]{:S(2)}) collective-permute-start(bf16[2,4,48,768]{3,2,1,0:T(8,128)(2,1)S(1)} %pad_maximum_fusion.16), channel_id=1, source_target_pairs={{0,4},{4,0},{8,12},{12,8},{16,20},{20,16},{24,28},{28,24},{1,5},{5... | collective-permute-start | bytes 1769480 | tf_op jit(solution)/shard_map/ppermute | solution.py:83
  145.8 19.3 %collective-permute-start.32 = (bf16[4,2,48,768]{3,2,1,0:T(8,128)(2,1)S(1)}, bf16[4,2,48,768]{3,2,1,0:T(8,128)(2,1)S(1)}, u32[]{:S(2)}, u32[]{:S(2)}) collective-permute-start(bf16[4,2,48,768]{3,2,1,0:T(8,128)(2,1)S(1)} %bitcast_dynamic-update-slice_fusion.4), channel_id=1, source_target_pairs={{0,2},{1,3},{2,0},{3,1},{4,6},{5,7},{6,4},{7,5},{8,10},{9,11},{10,... | collective-permute-start | bytes 1769480 | tf_op jit(solution)/shard_map/ppermute | solution.py:83
  156.2 9.3 %collective-permute-start.22 = (bf16[768,384]{1,0:T(8,128)(2,1)S(1)}, bf16[768,384]{1,0:T(8,128)(2,1)S(1)}, u32[]{:S(2)}, u32[]{:S(2)}) collective-permute-start(bf16[768,384]{1,0:T(8,128)(2,1)S(1)} %pad_maximum_fusion.15), channel_id=1, source_target_pairs={{0,1},{1,0},{2,3},{3,2},{4,5},{5,4},{6,7},{7,6},{8,9},{9,8},{10,11... | collective-permute-start | bytes 1769480 | tf_op jit(solution)/shard_map/ppermute | solution.py:83
  198.1 47.8 %collective-permute-start.33 = (bf16[512,768]{0,1:T(8,128)(2,1)}, bf16[512,768]{0,1:T(8,128)(2,1)}, u32[]{:S(2)}, u32[]{:S(2)}) collective-permute-start(bf16[512,768]{0,1:T(8,128)(2,1)} %dynamic-slice_convert_fusion.1), channel_id=1, source_target_pairs={{0,1},{1,0},{2,3},{3,2},{4,5},{5,4},{6,7},{7,6},{8,9},{9,8},{10,11... | collective-permute-start | bytes 2359304 | tf_op jit(solution)/shard_map/ppermute | solution.py:83
  205.2 88.7 %collective-permute-start.35 = (bf16[1024,768]{0,1:T(8,128)(2,1)}, bf16[1024,768]{0,1:T(8,128)(2,1)}, u32[]{:S(2)}, u32[]{:S(2)}) collective-permute-start(bf16[1024,768]{0,1:T(8,128)(2,1)} %convert_element_type.395), channel_id=1, source_target_pairs={{0,1},{1,0},{2,3},{3,2},{4,5},{5,4},{6,7},{7,6},{8,9},{9,8},{10,11... | collective-permute-start | bytes 4718600 | tf_op jit(solution)/shard_map/ppermute | solution.py:83
  209.5 16.5 %collective-permute-start.59 = (bf16[2,4,48,768]{3,2,1,0:T(8,128)(2,1)}, bf16[2,4,48,768]{3,2,1,0:T(8,128)(2,1)}, u32[]{:S(2)}, u32[]{:S(2)}) collective-permute-start(bf16[2,4,48,768]{3,2,1,0:T(8,128)(2,1)} %fusion.38), channel_id=1, source_target_pairs={{0,4},{4,0},{8,12},{12,8},{16,20},{20,16},{24,28},{28,24},{1,5},{5... | collective-permute-start | bytes 1769480 | tf_op jit(solution)/shard_map/ppermute | solution.py:83
  210.3 19.5 %collective-permute-start.57 = (bf16[4,2,48,768]{3,2,0,1:T(8,128)(2,1)}, bf16[4,2,48,768]{3,2,0,1:T(8,128)(2,1)}, u32[]{:S(2)}, u32[]{:S(2)}) collective-permute-start(bf16[4,2,48,768]{3,2,0,1:T(8,128)(2,1)} %fusion.36), channel_id=1, source_target_pairs={{0,2},{1,3},{2,0},{3,1},{4,6},{5,7},{6,4},{7,5},{8,10},{9,11},{10,... | collective-permute-start | bytes 1769480 | tf_op jit(solution)/shard_map/ppermute | solution.py:83
  221.2 16.5 %collective-permute-start.69 = (bf16[2,4,48,768]{3,2,1,0:T(8,128)(2,1)}, bf16[2,4,48,768]{3,2,1,0:T(8,128)(2,1)}, u32[]{:S(2)}, u32[]{:S(2)}) collective-permute-start(bf16[2,4,48,768]{3,2,1,0:T(8,128)(2,1)} %fusion.39), channel_id=1, source_target_pairs={{0,4},{4,0},{8,12},{12,8},{16,20},{20,16},{24,28},{28,24},{1,5},{5... | collective-permute-start | bytes 1769480 | tf_op jit(solution)/shard_map/ppermute | solution.py:83
  226.0 16.5 %collective-permute-start.67 = (bf16[4,2,48,768]{3,2,0,1:T(8,128)(2,1)}, bf16[4,2,48,768]{3,2,0,1:T(8,128)(2,1)S(1)}, u32[]{:S(2)}, u32[]{:S(2)}) collective-permute-start(bf16[4,2,48,768]{3,2,0,1:T(8,128)(2,1)} %fusion.37), channel_id=1, source_target_pairs={{0,2},{1,3},{2,0},{3,1},{4,6},{5,7},{6,4},{7,5},{8,10},{9,11},{10,... | collective-permute-start | bytes 1769480 | tf_op jit(solution)/shard_map/ppermute | solution.py:83
  229.8 22.2 %collective-permute-start.60 = (bf16[4,48,768]{2,1,0:T(8,128)(2,1)}, bf16[4,48,768]{2,1,0:T(8,128)(2,1)}, u32[]{:S(2)}, u32[]{:S(2)}) collective-permute-start(bf16[4,48,768]{2,1,0:T(8,128)(2,1)} %fusion.56), channel_id=1, source_target_pairs={{0,2},{1,3},{2,0},{3,1},{4,6},{5,7},{6,4},{7,5},{8,10},{9,11},{10,... | collective-permute-start | bytes 884744 | tf_op jit(solution)/shard_map/ppermute | solution.py:83
  237.7 15.7 %collective-permute-start.58 = (bf16[4,48,768]{2,1,0:T(8,128)(2,1)}, bf16[4,48,768]{2,1,0:T(8,128)(2,1)}, u32[]{:S(2)}, u32[]{:S(2)}) collective-permute-start(bf16[4,48,768]{2,1,0:T(8,128)(2,1)} %fusion.54), channel_id=1, source_target_pairs={{0,4},{4,0},{8,12},{12,8},{16,20},{20,16},{24,28},{28,24},{1,5},{5... | collective-permute-start | bytes 884744 | tf_op jit(solution)/shard_map/ppermute | solution.py:83
  242.5 17.9 %collective-permute-start.70 = (bf16[4,48,768]{2,1,0:T(8,128)(2,1)}, bf16[4,48,768]{2,1,0:T(8,128)(2,1)}, u32[]{:S(2)}, u32[]{:S(2)}) collective-permute-start(bf16[4,48,768]{2,1,0:T(8,128)(2,1)} %fusion.57), channel_id=1, source_target_pairs={{0,2},{1,3},{2,0},{3,1},{4,6},{5,7},{6,4},{7,5},{8,10},{9,11},{10,... | collective-permute-start | bytes 884744 | tf_op jit(solution)/shard_map/ppermute | solution.py:83
  245.9 15.5 %collective-permute-start.68 = (bf16[4,48,768]{2,1,0:T(8,128)(2,1)}, bf16[4,48,768]{2,1,0:T(8,128)(2,1)}, u32[]{:S(2)}, u32[]{:S(2)}) collective-permute-start(bf16[4,48,768]{2,1,0:T(8,128)(2,1)} %fusion.55), channel_id=1, source_target_pairs={{0,4},{4,0},{8,12},{12,8},{16,20},{20,16},{24,28},{28,24},{1,5},{5... | collective-permute-start | bytes 884744 | tf_op jit(solution)/shard_map/ppermute | solution.py:83
  254.7 9.8 %collective-permute-start.61 = (bf16[1,96,768]{2,1,0:T(8,128)(2,1)S(1)}, bf16[1,96,768]{2,1,0:T(8,128)(2,1)S(1)}, u32[]{:S(2)}, u32[]{:S(2)}) collective-permute-start(bf16[1,96,768]{2,1,0:T(8,128)(2,1)S(1)} %get-tuple-element.117), channel_id=1, source_target_pairs={{0,8},{4,12},{1,9},{5,13},{2,10},{6,14},{3,11},{7,15}} | collective-permute-start | bytes 442376 | tf_op jit(solution)/shard_map/ppermute | solution.py:134
  259.2 11.7 %collective-permute-start.64 = (bf16[1,96,768]{2,1,0:T(8,128)(2,1)S(1)}, bf16[1,96,768]{2,1,0:T(8,128)(2,1)S(1)}, u32[]{:S(2)}, u32[]{:S(2)}) collective-permute-start(bf16[1,96,768]{2,1,0:T(8,128)(2,1)S(1)} %get-tuple-element.118), channel_id=1, source_target_pairs={{24,16},{28,20},{25,17},{29,21},{26,18},{30,22},{27,19},{31,23}} | collective-permute-start | bytes 442376 | tf_op jit(solution)/shard_map/ppermute | solution.py:137
  263.8 12.9 %collective-permute-start.74 = (bf16[1,96,768]{2,1,0:T(8,128)(2,1)S(1)}, bf16[1,96,768]{2,1,0:T(8,128)(2,1)S(1)}, u32[]{:S(2)}, u32[]{:S(2)}) collective-permute-start(bf16[1,96,768]{2,1,0:T(8,128)(2,1)S(1)} %get-tuple-element.114), channel_id=1, source_target_pairs={{24,16},{28,20},{25,17},{29,21},{26,18},{30,22},{27,19},{31,23}} | collective-permute-start | bytes 442376 | tf_op jit(solution)/shard_map/ppermute | solution.py:137
  267.9 8.8 %collective-permute-start.72 = (bf16[1,96,768]{2,1,0:T(8,128)(2,1)S(1)}, bf16[1,96,768]{2,1,0:T(8,128)(2,1)S(1)}, u32[]{:S(2)}, u32[]{:S(2)}) collective-permute-start(bf16[1,96,768]{2,1,0:T(8,128)(2,1)S(1)} %add_convert_fusion.6), channel_id=1, source_target_pairs={{0,8},{4,12},{8,16},{12,20},{1,9},{5,13},{9,17},{13,21},{2,10},{6,... | collective-permute-start | bytes 442376 | tf_op jit(solution)/shard_map/ppermute | solution.py:134
  270.9 11.7 %collective-permute-start.65 = (bf16[1,96,768]{2,1,0:T(8,128)(2,1)S(1)}, bf16[1,96,768]{2,1,0:T(8,128)(2,1)S(1)}, u32[]{:S(2)}, u32[]{:S(2)}) collective-permute-start(bf16[1,96,768]{2,1,0:T(8,128)(2,1)S(1)} %get-tuple-element.116), channel_id=1, source_target_pairs={{16,8},{20,12},{24,16},{28,20},{17,9},{21,13},{25,17},{29,21},{18,... | collective-permute-start | bytes 442376 | tf_op jit(solution)/shard_map/ppermute | solution.py:137
  271.6 13.8 %collective-permute-start.63 = (bf16[1,96,768]{2,1,0:T(8,128)(2,1)S(1)}, bf16[1,96,768]{2,1,0:T(8,128)(2,1)S(1)}, u32[]{:S(2)}, u32[]{:S(2)}) collective-permute-start(bf16[1,96,768]{2,1,0:T(8,128)(2,1)S(1)} %get-tuple-element.115), channel_id=1, source_target_pairs={{0,8},{4,12},{8,16},{12,20},{16,24},{20,28},{1,9},{5,13},{9,17},{1... | collective-permute-start | bytes 442376 | tf_op jit(solution)/shard_map/ppermute | solution.py:134
  277.4 14.2 %collective-permute-start.73 = (bf16[1,96,768]{2,1,0:T(8,128)(2,1)S(1)}, bf16[1,96,768]{2,1,0:T(8,128)(2,1)S(1)}, u32[]{:S(2)}, u32[]{:S(2)}) collective-permute-start(bf16[1,96,768]{2,1,0:T(8,128)(2,1)S(1)} %get-tuple-element.111), channel_id=1, source_target_pairs={{0,8},{4,12},{8,16},{12,20},{16,24},{20,28},{1,9},{5,13},{9,17},{1... | collective-permute-start | bytes 442376 | tf_op jit(solution)/shard_map/ppermute | solution.py:134
  284.2 8.6 %collective-permute-start.76 = (bf16[1,96,768]{2,1,0:T(8,128)(2,1)S(1)}, bf16[1,96,768]{2,1,0:T(8,128)(2,1)S(1)}, u32[]{:S(2)}, u32[]{:S(2)}) collective-permute-start(bf16[1,96,768]{2,1,0:T(8,128)(2,1)S(1)} %add_convert_fusion.3), channel_id=1, source_target_pairs={{8,0},{12,4},{16,8},{20,12},{24,16},{28,20},{9,1},{13,5},{17,9},{2... | collective-permute-start | bytes 442376 | tf_op jit(solution)/shard_map/ppermute | solution.py:137
  332.6 109.0 %collective-permute-start.36 = (bf16[512,768]{0,1:T(8,128)(2,1)}, bf16[512,768]{0,1:T(8,128)(2,1)}, u32[]{:S(2)}, u32[]{:S(2)}) collective-permute-start(bf16[512,768]{0,1:T(8,128)(2,1)} %dynamic-slice_convert_fusion), channel_id=1, source_target_pairs={{0,1},{1,0},{2,3},{3,2},{4,5},{5,4},{6,7},{7,6},{8,9},{9,8},{10,11... | collective-permute-start | bytes 2359304 | tf_op jit(solution)/shard_map/ppermute | solution.py:83
  388.4 15.7 %collective-permute-start.79 = (f32[12,768]{1,0:T(8,128)S(1)}, f32[12,768]{1,0:T(8,128)S(1)}, u32[]{:S(2)}, u32[]{:S(2)}) collective-permute-start(f32[12,768]{1,0:T(8,128)S(1)} %add.720), channel_id=1, source_target_pairs={{0,4},{4,0},{8,12},{12,8},{16,20},{20,16},{24,28},{28,24},{1,5},{5... | collective-permute-start | bytes 110600 | tf_op jit(solution)/shard_map/ppermute | solution.py:83
  402.6 18.3 %collective-permute-start.37 = (bf16[4,2,48,576]{3,2,0,1:T(8,128)(2,1)S(1)}, bf16[4,2,48,576]{3,2,0,1:T(8,128)(2,1)S(1)}, u32[]{:S(2)}, u32[]{:S(2)}) collective-permute-start(bf16[4,2,48,576]{3,2,0,1:T(8,128)(2,1)S(1)} %fusion.42), channel_id=1, source_target_pairs={{0,2},{1,3},{2,0},{3,1},{4,6},{5,7},{6,4},{7,5},{8,10},{9,11},{10,... | collective-permute-start | bytes 1327112 | tf_op jit(solution)/shard_map/ppermute | solution.py:83
  409.0 11.1 %collective-permute-start.39 = (bf16[2,4,48,576]{3,2,1,0:T(8,128)(2,1)S(1)}, bf16[2,4,48,576]{3,2,1,0:T(8,128)(2,1)S(1)}, u32[]{:S(2)}, u32[]{:S(2)}) collective-permute-start(bf16[2,4,48,576]{3,2,1,0:T(8,128)(2,1)S(1)} %fusion.43), channel_id=1, source_target_pairs={{0,4},{4,0},{8,12},{12,8},{16,20},{20,16},{24,28},{28,24},{1,5},{5... | collective-permute-start | bytes 1327112 | tf_op jit(solution)/shard_map/ppermute | solution.py:83
  416.8 16.6 %collective-permute-start.53 = (bf16[1,96,192]{2,1,0:T(8,128)(2,1)S(1)}, bf16[1,96,192]{2,1,0:T(8,128)(2,1)S(1)}, u32[]{:S(2)}, u32[]{:S(2)}) collective-permute-start(bf16[1,96,192]{2,1,0:T(8,128)(2,1)S(1)} %get-tuple-element.146), channel_id=1, source_target_pairs={{0,8},{4,12},{8,16},{12,20},{16,24},{20,28},{1,9},{5,13},{9,17},{1... | collective-permute-start | bytes 110600 | tf_op jit(solution)/shard_map/ppermute | solution.py:134
  418.8 14.7 %collective-permute-start.56 = (bf16[1,96,192]{2,1,0:T(8,128)(2,1)S(1)}, bf16[1,96,192]{2,1,0:T(8,128)(2,1)S(1)}, u32[]{:S(2)}, u32[]{:S(2)}) collective-permute-start(bf16[1,96,192]{2,1,0:T(8,128)(2,1)S(1)} %add_convert_fusion.15), channel_id=1, source_target_pairs={{8,0},{12,4},{16,8},{20,12},{24,16},{28,20},{9,1},{13,5},{17,9},{2... | collective-permute-start | bytes 110600 | tf_op jit(solution)/shard_map/ppermute | solution.py:137
  444.9 12.4 %collective-permute-start.43 = (bf16[1,96,576]{2,1,0:T(8,128)(2,1)S(1)}, bf16[1,96,576]{2,1,0:T(8,128)(2,1)S(1)}, u32[]{:S(2)}, u32[]{:S(2)}) collective-permute-start(bf16[1,96,576]{2,1,0:T(8,128)(2,1)S(1)} %get-tuple-element.123), channel_id=1, source_target_pairs={{0,8},{4,12},{8,16},{12,20},{16,24},{20,28},{1,9},{5,13},{9,17},{1... | collective-permute-start | bytes 331784 | tf_op jit(solution)/shard_map/ppermute | solution.py:134
  (133 other events, 1313.9 us)

commit v2 on v1

v2 whole, which is shorter than its diff:
```python
import math

import jax
import jax.numpy as jnp
from jax import lax
from jax.experimental import pallas as pl
from jax.experimental.pallas import tpu as pltpu
from jax.sharding import PartitionSpec as P

HEAD_DIM = 64
LENGTH = 1024
STEP_NUMBER = 10
VEC_ROWS = 12
PAIR = 2 * HEAD_DIM
QUERY_BLOCK = 256
ROW_BLOCK = 256


EPS = 1e-05
BETA_ONE = 0.9
BETA_TWO = 0.999
ADAM_EPS = 1e-08
DECAY = 0.1
RATE_MATRIX = 0.04
RATE_VECTOR = 0.3

F32 = jnp.float32
BF16 = jnp.bfloat16


def normalize_rows(values_in):
    row_mean = jnp.mean(values_in, axis=-1, keepdims=True)
    centred = values_in - row_mean
    row_var = jnp.mean(centred * centred, axis=-1, keepdims=True)
    inv_std = lax.rsqrt(row_var + EPS)
    return (centred * inv_std, inv_std)


def norm_back(grad_in, normed, inv_std):
    mean_grad = jnp.mean(grad_in, axis=-1, keepdims=True)
    mean_cross = jnp.mean(grad_in * normed, axis=-1, keepdims=True)
    return inv_std * (grad_in - mean_grad - normed * mean_cross)


def adamw(weight, moment_one, moment_two, gradient, rate):
    first = BETA_ONE * moment_one + (1 - BETA_ONE) * gradient
    second = BETA_TWO * moment_two + (1 - BETA_TWO) * gradient * gradient
    first_hat = first / (1 - BETA_ONE**STEP_NUMBER)
    second_hat = second / (1 - BETA_TWO**STEP_NUMBER)
    updated = weight - rate * (first_hat / (jnp.sqrt(second_hat) + ADAM_EPS) + DECAY * weight)
    return (updated, first, second)


def bit_strides(high, low):
    strides = []
    while high > low:
        high //= 2
        strides.append(high)
    return strides


def place_on(line):
    name, stride = line
    return lax.axis_index(name) // stride % 2


def swap_over(value, line):
    name, stride = line
    pairs = [(index, index ^ stride) for index in range(lax.axis_size(name))]
    return lax.ppermute(value, name, pairs)


def gather_bit(block, line, dim):
    other = jnp.expand_dims(swap_over(block, line), dim)
    shape = block.shape[:dim] + (2,) + block.shape[dim:]
    both = jnp.broadcast_to(jnp.expand_dims(block, dim), shape)
    return lax.dynamic_update_slice_in_dim(both, other, 1 - place_on(line), dim)


def gather_bits(block, lines, dim):
    for line in lines:
        block = gather_bit(block, line, dim)
        dim += 1
    return block


def reduce_bit(parts, line, dim):
    place = place_on(line)

    def part(index):
        return lax.dynamic_index_in_dim(parts, index, dim, keepdims=False)

    sent = swap_over(part(1 - place).astype(BF16), line)
    return part(place).astype(F32) + sent.astype(F32)


def reduce_bits(parts, lines, dim):
    for line in reversed(lines):
        parts = reduce_bit(parts, line, dim + len(lines) - 1)
        lines = lines[:-1]
    return parts


class Grid:
    def __init__(self, row_count):
        near_size = {8: 2, 64: 4}.get(row_count, 1)
        self.row_count = row_count
        self.far = [("row", stride) for stride in bit_strides(row_count, near_size)]
        self.near = [("row", stride) for stride in bit_strides(near_size, 1)]
        self.x_line = ("col", 2)

    def gather_far(self, block):
        rows, cols = block.shape
        return gather_bits(block, self.far, 0).reshape(-1, rows, cols)

    def gather_near(self, stacked, keep_cols):
        far, _, cols = stacked.shape
        front, back = stacked[: far // 2], stacked[far // 2 :]
        front_own = gather_bits(front, self.near, 1).reshape(-1, cols)
        front_other = swap_over(front_own[:, :keep_cols], self.x_line)
        back_other = swap_over(back[:, :, :keep_cols], self.x_line)
        back_pair = gather_bits(jnp.concatenate([back, back_other], axis=2), self.near, 1)
        back_pair = back_pair.reshape(-1, cols + keep_cols)
        own = jnp.concatenate([front_own, back_pair[:, :cols]], axis=0)
        other = jnp.concatenate([front_other, back_pair[:, cols:]], axis=0)
        return own, other

    def reduce_all(self, pair):
        _, all_rows, cols = pair.shape
        rows = all_rows // self.row_count
        middle = all_rows // 2
        bits = (2,) * len(self.near)
        front = pair[0, :middle].astype(F32) + swap_over(pair[1, :middle], self.x_line).astype(F32)
        front = reduce_bits(front.reshape((-1,) + bits + (rows, cols)), self.near, 1)
        back = pair[:, middle:].reshape((2, -1) + bits + (rows, cols))
        back = reduce_bits(back, self.near, 2)
        back = back[0].astype(F32) + swap_over(back[1].astype(BF16), self.x_line).astype(F32)
        total = jnp.concatenate([front, back], axis=0)
        total = total.reshape((2,) * len(self.far) + (rows, cols))
        return reduce_bits(total, self.far, 0)


def sum_everywhere(value):
    for name in ("col", "row"):
        for stride in bit_strides(lax.axis_size(name), 1):
            value = value + swap_over(value, (name, stride))
    return value


def dot_nt(left, right):
    return lax.dot_general(left, right, (((1,), (1,)), ((), ())), preferred_element_type=F32)


def dot_nn(left, right):
    return lax.dot_general(left, right, (((1,), (0,)), ((), ())), preferred_element_type=F32)


def lane_pick(half):
    lanes = lax.broadcasted_iota(jnp.int32, (1, PAIR), 1)
    return jnp.where((lanes // HEAD_DIM) == half, 1.0, 0.0).astype(BF16)


def causal_block(size):
    key_at = lax.broadcasted_iota(jnp.int32, (size, size), 0)
    query_at = lax.broadcasted_iota(jnp.int32, (size, size), 1)
    return key_at <= query_at


def attend_kernel(q_ref, k_ref, v_ref, out_ref, lse_ref):
    length = q_ref.shape[0]
    block = min(QUERY_BLOCK, length)
    allowed = causal_block(block)
    values_t = v_ref[...].T
    scaling = jnp.asarray(HEAD_DIM**-0.5, BF16)
    for first in range(0, length, block):
        last = first + block
        query = q_ref[first:last, :] * scaling
        outs = []
        for half in range(2):
            rows = slice(half * HEAD_DIM, (half + 1) * HEAD_DIM)
            query_half = query * lane_pick(half)
            diag = dot_nt(k_ref[first:last, :], query_half)
            diag = jnp.where(allowed, diag, -1e30)
            top = jnp.max(diag, axis=0, keepdims=True)
            if first:
                rest = dot_nt(k_ref[0:first, :], query_half)
                top = jnp.maximum(top, jnp.max(rest, axis=0, keepdims=True))
            diag = jnp.exp(diag - top)
            total = jnp.sum(diag, axis=0, keepdims=True)
            if first:
                rest = jnp.exp(rest - top)
                total = total + jnp.sum(rest, axis=0, keepdims=True)
            inverse = 1.0 / total
            result = dot_nn(values_t[rows, first:last], (diag * inverse).astype(BF16))
            if first:
                result = result + dot_nn(values_t[rows, 0:first], (rest * inverse).astype(BF16))
            outs.append(result)
            lse_ref[0, half : half + 1, first:last] = top + jnp.log(total)
        out_ref[first:last, :] = jnp.concatenate(outs, axis=0).T.astype(BF16)


def attend_forward(qkv):
    length, width = qkv.shape
    pairs = width // (3 * PAIR)

    def lanes(part):
        return pl.BlockSpec((length, PAIR), lambda pair: (0, part * pairs + pair))

    return pl.pallas_call(
        attend_kernel,
        grid=(pairs,),
        in_specs=[lanes(0), lanes(1), lanes(2)],
        out_specs=[lanes(0), pl.BlockSpec((1, 8, length), lambda pair: (pair, 0, 0))],
        out_shape=[
            jax.ShapeDtypeStruct((length, pairs * PAIR), BF16),
            jax.ShapeDtypeStruct((pairs, 8, length), F32),
        ],
        compiler_params=pltpu.CompilerParams(vmem_limit_bytes=40 * 2**20),
        cost_estimate=pl.CostEstimate(
            flops=pairs * 2 * 4 * length * length * HEAD_DIM,
            bytes_accessed=4 * length * pairs * PAIR * 2,
            transcendentals=pairs * length * length,
        ),
        name="attend_forward",
    )(qkv, qkv, qkv)


def attend_back_kernel(q_ref, k_ref, v_ref, go_ref, lse_ref, grad_ref, gk_sum, gv_sum):
    length = q_ref.shape[0]
    pairs = grad_ref.shape[1] // (3 * PAIR)
    block = min(QUERY_BLOCK, length)
    allowed = causal_block(block)
    keys_t = k_ref[...].T
    scaling = jnp.asarray(HEAD_DIM**-0.5, BF16)
    pair = pl.program_id(0)

    def lanes(part):
        return pl.ds(pl.multiple_of((part * pairs + pair) * PAIR, PAIR), PAIR)

    gk_sum[...] = jnp.zeros_like(gk_sum)
    gv_sum[...] = jnp.zeros_like(gv_sum)
    for first in range(0, length, block):
        last = first + block
        query = q_ref[first:last, :] * scaling
        grad_out = go_ref[first:last, :]
        outs = []
        for half in range(2):
            rows = slice(half * HEAD_DIM, (half + 1) * HEAD_DIM)
            pick = lane_pick(half)
            query_half = query * pick
            grad_half = grad_out * pick
            lse = lse_ref[0, half : half + 1, first:last]
            spans = [(first, last)] if first == 0 else [(0, first), (first, last)]
            probs, grads, inner = [], [], None
            for low, high in spans:
                scores = dot_nt(k_ref[low:high, :], query_half)
                if low == first:
                    scores = jnp.where(allowed, scores, -1e30)
                prob = jnp.exp(scores - lse)
                grad_prob = dot_nt(v_ref[low:high, :], grad_half)
                part = jnp.sum(prob * grad_prob, axis=0, keepdims=True)
                inner = part if inner is None else inner + part
                probs.append(prob)
                grads.append(grad_prob)
            result = None
            for (low, high), prob, grad_prob in zip(spans, probs, grads):
                grad_score = (prob * (grad_prob - inner)).astype(BF16)
                gk_sum[low:high, :] += dot_nn(grad_score, query_half)
                gv_sum[low:high, :] += dot_nn(prob.astype(BF16), grad_half)
                part = dot_nn(keys_t[rows, low:high], grad_score)
                result = part if result is None else result + part
            outs.append(result)
        grad_query = jnp.concatenate(outs, axis=0).T * (HEAD_DIM**-0.5)
        grad_ref[first:last, lanes(0)] = grad_query.astype(BF16)
    grad_ref[:, lanes(1)] = gk_sum[...].astype(BF16)
    grad_ref[:, lanes(2)] = gv_sum[...].astype(BF16)


def attend_backward(qkv, grad_heads, lse):
    length, width = qkv.shape
    pairs = width // (3 * PAIR)

    def lanes(part):
        return pl.BlockSpec((length, PAIR), lambda pair: (0, part * pairs + pair))

    return pl.pallas_call(
        attend_back_kernel,
        grid=(pairs,),
        in_specs=[
            lanes(0),
            lanes(1),
            lanes(2),
            lanes(0),
            pl.BlockSpec((1, 8, length), lambda pair: (pair, 0, 0)),
        ],
        out_specs=pl.BlockSpec((length, width), lambda pair: (0, 0)),
        out_shape=jax.ShapeDtypeStruct((length, width), BF16),
        scratch_shapes=[pltpu.VMEM((length, PAIR), F32), pltpu.VMEM((length, PAIR), F32)],
        compiler_params=pltpu.CompilerParams(vmem_limit_bytes=40 * 2**20),
        cost_estimate=pl.CostEstimate(
            flops=pairs * 2 * 10 * length * length * HEAD_DIM,
            bytes_accessed=7 * length * pairs * PAIR * 2,
            transcendentals=pairs * length * length,
        ),
        name="attend_backward",
    )(qkv, qkv, qkv, grad_heads, lse)


def rows_of(block, width):
    return pl.BlockSpec((block, width), lambda step: (step, 0))


def whole(shape):
    return pl.BlockSpec(shape, lambda *step: (0,) * len(shape))


def shaped(shape, dtype):
    return jax.ShapeDtypeStruct(shape, dtype)


def cost(flops, arrays):
    return pl.CostEstimate(flops=flops, bytes_accessed=arrays, transcendentals=0)


PARAMS = pltpu.CompilerParams(vmem_limit_bytes=48 * 2**20)


def first_norm_kernel(tokens_ref, vec_ref, weight_ref, bias_ref, norm_ref, qkv_ref):
    normed, _ = normalize_rows(tokens_ref[...].astype(F32))
    first_in = (normed * vec_ref[0:1, :] + vec_ref[1:2, :]).astype(BF16)
    norm_ref[...] = first_in
    qkv_ref[...] = (dot_nn(first_in, weight_ref[...]) + bias_ref[...]).astype(BF16)


def first_norm(tokens, vec_all, weight, bias):
    length, width = tokens.shape
    cols = weight.shape[1]
    return pl.pallas_call(
        first_norm_kernel,
        grid=(length // ROW_BLOCK,),
        in_specs=[
            rows_of(ROW_BLOCK, width),
            whole(vec_all.shape),
            whole(weight.shape),
            whole(bias.shape),
        ],
        out_specs=[rows_of(ROW_BLOCK, width), rows_of(ROW_BLOCK, cols)],
        out_shape=[shaped((length, width), BF16), shaped((length, cols), BF16)],
        compiler_params=PARAMS,
        cost_estimate=cost(2 * length * width * cols, 2 * length * (2 * width + cols)),
        name="first_norm",
    )(tokens, vec_all, weight, bias)


def attended_kernel(
    heads_ref, partner_ref, own_ref, other_ref, tokens_ref, vec_ref, hidden_ref, norm_ref
):
    attended = dot_nt(heads_ref[...], own_ref[...]) + dot_nt(partner_ref[...], other_ref[...])
    hidden = tokens_ref[...].astype(F32) + attended + vec_ref[4:5, :]
    hidden_ref[...] = hidden
    normed, _ = normalize_rows(hidden)
    norm_ref[...] = (normed * vec_ref[5:6, :] + vec_ref[6:7, :]).astype(BF16)


def attended_norm(heads, partner_heads, own_out, partner_out, tokens, vec_all):
    length, width = tokens.shape
    cols = heads.shape[1]
    return pl.pallas_call(
        attended_kernel,
        grid=(length // ROW_BLOCK,),
        in_specs=[
            rows_of(ROW_BLOCK, cols),
            rows_of(ROW_BLOCK, cols),
            whole(own_out.shape),
            whole(partner_out.shape),
            rows_of(ROW_BLOCK, width),
            whole(vec_all.shape),
        ],
        out_specs=[rows_of(ROW_BLOCK, width), rows_of(ROW_BLOCK, width)],
        out_shape=[shaped((length, width), F32), shaped((length, width), BF16)],
        compiler_params=PARAMS,
        cost_estimate=cost(4 * length * width * cols, length * width * 10),
        name="attended_norm",
    )(heads, partner_heads, own_out, partner_out, tokens, vec_all)


def feed_kernel(
    norm_ref, cot_ref, up_ref, down_ref, bias_ref, act_ref, gup_ref, bias_sum_ref, out_ref, back_ref,
    back_low_ref,
):
    step = pl.program_id(0)
    length = norm_ref.shape[0]
    curve, cubic = math.sqrt(2 / math.pi), 0.044715

    @pl.when(step == 0)
    def _():
        out_ref[...] = jnp.zeros_like(out_ref)
        back_ref[...] = jnp.zeros_like(back_ref)

    bias_sum = jnp.zeros(bias_ref.shape, F32)
    for first in range(0, length, ROW_BLOCK):
        rows = slice(first, first + ROW_BLOCK)
        up = dot_nn(norm_ref[rows, :], up_ref[...]) + bias_ref[...]
        square = up * up
        tanh = jnp.tanh(curve * up * (1.0 + cubic * square))
        act = (0.5 * up * (1.0 + tanh)).astype(BF16)
        act_ref[rows, :] = act
        slope = 0.5 * (1.0 + tanh) + 0.5 * up * (1.0 - tanh * tanh) * (
            curve * (1.0 + 3.0 * cubic * square)
        )
        grad_up = (dot_nn(cot_ref[rows, :], down_ref[...]) * slope).astype(BF16)
        gup_ref[rows, :] = grad_up
        bias_sum = bias_sum + jnp.sum(grad_up.astype(F32), axis=0, keepdims=True)
        out_ref[rows, :] += dot_nt(act, down_ref[...])
        back_ref[rows, :] += dot_nt(grad_up, up_ref[...])
    bias_sum_ref[...] = bias_sum

    @pl.when(step == pl.num_programs(0) - 1)
    def _():
        back_low_ref[...] = back_ref[...].astype(BF16)


def feed(norm, cot, up, down, bias):
    length, width = norm.shape
    hidden = up.shape[1]
    block = 512
    cols = pl.BlockSpec((width, block), lambda step: (0, step))
    tall = pl.BlockSpec((length, block), lambda step: (0, step))
    flat = pl.BlockSpec((1, block), lambda step: (0, step))
    full = whole((length, width))
    return pl.pallas_call(
        feed_kernel,
        grid=(hidden // block,),
        in_specs=[full, full, cols, cols, flat],
        out_specs=[tall, tall, flat, full, full, full],
        out_shape=[
            shaped((length, hidden), BF16),
            shaped((length, hidden), BF16),
            shaped((1, hidden), F32),
            shaped((length, width), F32),
            shaped((length, width), F32),
            shaped((length, width), BF16),
        ],
        compiler_params=PARAMS,
        cost_estimate=cost(8 * length * width * hidden, 4 * length * (width + hidden)),
        name="feed",
    )(norm, cot, up, down, bias)


def feed_grads_kernel(cot_ref, norm_ref, act_ref, gup_ref, out_ref, turned):
    kind = pl.program_id(0)
    first = (pl.program_id(1) == 0) & (pl.program_id(2) == 0)

    @pl.when(first & (kind == 0))
    def _():
        turned[...] = cot_ref[...].T

    @pl.when(first & (kind == 1))
    def _():
        turned[...] = norm_ref[...].T

    @pl.when(kind == 0)
    def _():
        out_ref[0] = dot_nn(turned[...], act_ref[...]).astype(BF16)

    @pl.when(kind == 1)
    def _():
        out_ref[0] = dot_nn(turned[...], gup_ref[...]).astype(BF16)


def feed_grads(cot, norm, act, grad_up):
    length, width = norm.shape
    hidden = act.shape[1]
    block = hidden // 4
    return pl.pallas_call(
        feed_grads_kernel,
        grid=(2, 2, 2),
        in_specs=[
            whole((length, width)),
            whole((length, width)),
            pl.BlockSpec((length, block), lambda kind, x, n: (0, jnp.where(kind == 0, 2 * x + n, 3))),
            pl.BlockSpec((length, block), lambda kind, x, n: (0, jnp.where(kind == 1, 2 * x + n, 0))),
        ],
        out_specs=pl.BlockSpec((1, width, block), lambda kind, x, n: (x, 0, 2 * kind + n)),
        out_shape=shaped((2, width, hidden), BF16),
        scratch_shapes=[pltpu.VMEM((width, length), BF16)],
        compiler_params=PARAMS,
        cost_estimate=cost(4 * length * width * hidden, 4 * length * (width + hidden)),
        name="feed_grads",
    )(cot, norm, act, grad_up)


def second_back_kernel(
    part_ref, other_ref, hidden_ref, cot_ref, vec_ref, out_w_ref, grad_ref, low_ref, heads_ref, sum_ref
):
    normed, inv_std = normalize_rows(hidden_ref[...])
    part = part_ref[...]
    cot = cot_ref[...].astype(F32)
    grad_second = part + other_ref[...].astype(F32)
    grad = cot + norm_back(grad_second * vec_ref[5:6, :], normed, inv_std)
    grad_ref[...] = grad
    low = grad.astype(BF16)
    low_ref[...] = low
    heads_ref[...] = dot_nn(low, out_w_ref[...]).astype(BF16)

    @pl.when(pl.program_id(0) == 0)
    def _():
        sum_ref[...] = jnp.zeros_like(sum_ref)

    for row, value in enumerate((grad, part * normed, part, cot)):
        sum_ref[row : row + 1, :] += jnp.sum(value, axis=0, keepdims=True)


def second_back(part, other, hidden, cot, vec_all, out_w):
    length, width = part.shape
    cols = out_w.shape[1]
    full = rows_of(ROW_BLOCK, width)
    return pl.pallas_call(
        second_back_kernel,
        grid=(length // ROW_BLOCK,),
        in_specs=[full, full, full, full, whole(vec_all.shape), whole(out_w.shape)],
        out_specs=[full, full, rows_of(ROW_BLOCK, cols), whole((8, width))],
        out_shape=[
            shaped((length, width), F32),
            shaped((length, width), BF16),
            shaped((length, cols), BF16),
            shaped((8, width), F32),
        ],
        compiler_params=PARAMS,
        cost_estimate=cost(2 * length * width * cols, length * width * 20),
        name="second_back",
    )(part, other, hidden, cot, vec_all, out_w)


def qkv_grads_kernel(norm_ref, low_ref, grad_ref, heads_ref, out_ref, turned):
    part = pl.program_id(0)
    cols = heads_ref.shape[1]
    half = cols // 2

    @pl.when(part == 0)
    def _():
        turned[...] = norm_ref[...].T

    @pl.when(part == 3)
    def _():
        turned[...] = low_ref[...].T

    for index in range(4):

        @pl.when(part == index)
        def _():
            right = heads_ref if index == 3 else grad_ref
            grads = dot_nn(turned[...], right[...]).astype(BF16)
            for x in range(2):
                out_ref[x, :, index * half : (index + 1) * half] = grads[:, x * half : (x + 1) * half]


def qkv_grads(norm, low, grad_qkv, heads):
    length, width = norm.shape
    cols = heads.shape[1]
    return pl.pallas_call(
        qkv_grads_kernel,
        grid=(4,),
        in_specs=[
            whole((length, width)),
            whole((length, width)),
            pl.BlockSpec((length, cols), lambda part: (0, jnp.minimum(part, 2))),
            whole((length, cols)),
        ],
        out_specs=whole((2, width, 2 * cols)),
        out_shape=shaped((2, width, 2 * cols), BF16),
        scratch_shapes=[pltpu.VMEM((width, length), BF16)],
        compiler_params=PARAMS,
        cost_estimate=cost(8 * length * width * cols, 4 * length * (2 * width + 2 * cols)),
        name="qkv_grads",
    )(norm, low, grad_qkv, heads)


def first_back_kernel(grad_ref, weight_ref, tokens_ref, part_ref, sum_ref, bias_ref):
    part = dot_nt(grad_ref[...], weight_ref[...])
    part_ref[...] = part
    normed, _ = normalize_rows(tokens_ref[...].astype(F32))

    @pl.when(pl.program_id(0) == 0)
    def _():
        sum_ref[...] = jnp.zeros_like(sum_ref)
        bias_ref[...] = jnp.zeros_like(bias_ref)

    for row, value in enumerate((part * normed, part)):
        sum_ref[row : row + 1, :] += jnp.sum(value, axis=0, keepdims=True)
    bias_ref[0:1, :] += jnp.sum(grad_ref[...].astype(F32), axis=0, keepdims=True)


def first_back(grad_qkv, weight, tokens):
    length, width = tokens.shape
    cols = grad_qkv.shape[1]
    return pl.pallas_call(
        first_back_kernel,
        grid=(length // ROW_BLOCK,),
        in_specs=[rows_of(ROW_BLOCK, cols), whole(weight.shape), rows_of(ROW_BLOCK, width)],
        out_specs=[rows_of(ROW_BLOCK, width), whole((8, width)), whole((8, cols))],
        out_shape=[
            shaped((length, width), F32),
            shaped((8, width), F32),
            shaped((8, cols), F32),
        ],
        compiler_params=PARAMS,
        cost_estimate=cost(2 * length * width * cols, length * (6 * width + 2 * cols)),
        name="first_back",
    )(grad_qkv, weight, tokens)


def token_back_kernel(core_ref, part_ref, other_ref, tokens_ref, grad_ref, vec_ref, out_ref):
    normed, inv_std = normalize_rows(tokens_ref[...].astype(F32))
    grad_first = part_ref[...] + other_ref[...].astype(F32)
    out_ref[...] = grad_ref[...] + norm_back(grad_first * vec_ref[0:1, :], normed, inv_std)


def token_back(core, part, other, tokens, grad_hidden, vec_all):
    rows, width = tokens.shape
    steps = rows // ROW_BLOCK
    own = pl.BlockSpec((ROW_BLOCK, width), lambda step, core_ref: (core_ref[0] * steps + step, 0))
    here = pl.BlockSpec((ROW_BLOCK, width), lambda step, core_ref: (step, 0))
    return pl.pallas_call(
        token_back_kernel,
        grid_spec=pltpu.PrefetchScalarGridSpec(
            num_scalar_prefetch=1,
            grid=(steps,),
            in_specs=[own, here, here, own, whole(vec_all.shape)],
            out_specs=here,
        ),
        out_shape=shaped((rows, width), F32),
        compiler_params=PARAMS,
        cost_estimate=cost(rows * width * 20, rows * width * 16),
        name="token_back",
    )(core.reshape(1), part, other, tokens, grad_hidden, vec_all)


def shards(
    tokens,
    cotangent,
    w_qkv,
    w_out,
    w_up,
    w_down,
    vectors,
    first_qkv,
    first_out,
    first_up,
    first_down,
    first_vectors,
    second_qkv,
    second_out,
    second_up,
    second_down,
    second_vectors,
):
    row_index = lax.axis_index("row")
    col_index = lax.axis_index("col")
    col_count = lax.axis_size("col")
    grid = Grid(lax.axis_size("row"))
    core_line = ("col", 1)
    core = col_index % 2
    other_col = col_index ^ 2
    rows_loc, width = tokens.shape
    width_loc = w_qkv.shape[2]
    width_core = 2 * width_loc
    hidden_loc = w_up.shape[1]
    shard_rows = w_up.shape[0]

    pad = -VEC_ROWS % 128
    pack_qkv = jnp.concatenate(
        [w_qkv[:, part].astype(BF16) for part in range(3)]
        + [w_out.T.astype(BF16), vectors.T.astype(BF16), jnp.zeros((shard_rows, pad), BF16)],
        axis=1,
    )
    pack_feed = jnp.concatenate([w_up.astype(BF16), w_down.T.astype(BF16)], axis=1)

    def both_halves(mine):
        return gather_bit(mine, core_line, 0).reshape(-1, width)

    def own_rows(value):
        return lax.dynamic_slice_in_dim(value, core * rows_loc, rows_loc, 0)

    def partner_rows(value):
        return lax.dynamic_slice_in_dim(value, (1 - core) * rows_loc, rows_loc, 0)

    far_qkv = grid.gather_far(pack_qkv)
    pack_feed, far_qkv = lax.optimization_barrier((pack_feed, far_qkv))
    own_qkv, other_qkv = grid.gather_near(far_qkv, 4 * width_loc)
    far_feed = grid.gather_far(pack_feed)
    own_feed, other_feed = grid.gather_near(far_feed, 2 * hidden_loc)

    all_tokens = both_halves(tokens)
    all_cot = both_halves(cotangent)

    vec_all = own_qkv[:, 4 * width_loc : 4 * width_loc + VEC_ROWS].T.astype(F32)

    def cat_blocks(vec_row, size):
        return jnp.concatenate(
            [
                lax.dynamic_slice_in_dim(vec_row, col_index * size, size, 0),
                lax.dynamic_slice_in_dim(vec_row, other_col * size, size, 0),
            ]
        )

    def joined(own, other, size, parts):
        return jnp.concatenate(
            [
                block[:, part * size : (part + 1) * size]
                for part in parts
                for block in (own, other)
            ],
            axis=1,
        )

    full_qkv = joined(own_qkv, other_qkv, width_loc, range(3))
    full_out = joined(own_qkv, other_qkv, width_loc, (3,))
    full_up = joined(own_feed, other_feed, hidden_loc, (0,))
    full_down = joined(own_feed, other_feed, hidden_loc, (1,))
    partner_out = swap_over(full_out, core_line)

    bias_qkv = jnp.concatenate(
        [
            cat_blocks(vec_all[2], width_loc),
            jnp.zeros((width_core,), F32),
            cat_blocks(vec_all[3], width_loc),
        ]
    )
    first_in, qkv = first_norm(all_tokens, vec_all, full_qkv, bias_qkv[None])
    heads_low, lse = attend_forward(qkv)
    partner_heads = swap_over(heads_low, core_line)
    hidden_state, second_in = attended_norm(
        heads_low, partner_heads, full_out, partner_out, all_tokens, vec_all
    )
    bias_up = cat_blocks(vec_all[8:].reshape(-1), hidden_loc)
    activated, grad_upper, grad_bias_up, down_part, second_part, second_low = feed(
        second_in, all_cot, full_up, full_down, bias_up[None]
    )

    second_other = swap_over(second_low, core_line)
    pair_feed = feed_grads(all_cot, second_in, activated, grad_upper)
    grad_hidden, grad_hidden_low, grad_heads, second_sums = second_back(
        second_part, second_other, hidden_state, all_cot, vec_all, full_out
    )
    down_other = swap_over(partner_rows(down_part).astype(BF16), core_line).astype(F32)
    mixed_out = own_rows(hidden_state) + own_rows(down_part) + down_other + vec_all[7]
    grad_qkv_low = attend_backward(qkv, grad_heads, lse)
    pair_qkv = qkv_grads(first_in, grad_hidden_low, grad_qkv_low, heads_low)
    first_part, first_sums, bias_sums = first_back(grad_qkv_low, full_qkv, all_tokens)
    first_other = swap_over(partner_rows(first_part).astype(BF16), core_line)
    token_grad = token_back(core, first_part, first_other, tokens, grad_hidden, vec_all)

    owned_feed = grid.reduce_all(pair_feed)
    owned_down, owned_up = owned_feed[:, :hidden_loc], owned_feed[:, hidden_loc:]
    owned_pack = grid.reduce_all(pair_qkv)
    owned_qkv = jnp.stack(
        [owned_pack[:, part * width_loc : (part + 1) * width_loc] for part in range(3)], axis=1
    )
    owned_out = owned_pack[:, 3 * width_loc :]

    def placed(part_row, length):
        size = part_row.shape[0] // 2
        start = jnp.zeros((length,), F32)
        start = lax.dynamic_update_slice_in_dim(start, part_row[:size], col_index * size, 0)
        return lax.dynamic_update_slice_in_dim(start, part_row[size:], other_col * size, 0)

    front_rows = jnp.stack(
        [
            first_sums[0],
            first_sums[1],
            placed(bias_sums[0, :width_core], width),
            placed(bias_sums[0, 2 * width_core :], width),
            0.5 * second_sums[0],
            second_sums[1],
            second_sums[2],
            0.5 * second_sums[3],
        ]
    )
    up_rows = placed(grad_bias_up[0], hidden_loc * col_count).reshape(-1, width)
    grad_vec = sum_everywhere(jnp.concatenate([front_rows, up_rows], axis=0))
    owned_vec = lax.dynamic_slice_in_dim(grad_vec, row_index * shard_rows, shard_rows, 1)

    new_qkv, new_first_qkv, new_second_qkv = adamw(
        w_qkv, first_qkv, second_qkv, owned_qkv, RATE_MATRIX
    )
    new_out, new_first_out, new_second_out = adamw(
        w_out, first_out, second_out, owned_out.T, RATE_MATRIX
    )
    new_up, new_first_up, new_second_up = adamw(w_up, first_up, second_up, owned_up, RATE_MATRIX)
    new_down, new_first_down, new_second_down = adamw(
        w_down, first_down, second_down, owned_down.T, RATE_MATRIX
    )
    new_vectors, new_first_vectors, new_second_vectors = adamw(
        vectors, first_vectors, second_vectors, owned_vec, RATE_VECTOR
    )
    return (
        mixed_out,
        token_grad,
        new_qkv,
        new_out,
        new_up,
        new_down,
        new_vectors,
        new_first_qkv,
        new_first_out,
        new_first_up,
        new_first_down,
        new_first_vectors,
        new_second_qkv,
        new_second_out,
        new_second_up,
        new_second_down,
        new_second_vectors,
    )


def solution(mesh):
    by_token = P(("row", "col"), None)
    weights = (
        P("row", None, "col"),
        P("col", "row"),
        P("row", "col"),
        P("col", "row"),
        P(None, "row"),
    )
    return jax.shard_map(
        shards,
        mesh=mesh,
        in_specs=(by_token, by_token) + weights * 3,
        out_specs=(by_token, by_token) + weights * 3,
        check_vma=False,
    )
```

time: 472 us -> 336 us (0.71)
  starting transfers between devices: 126 us -> 42.2 us
  Pallas kernels: 28.1 us -> 93.3 us
  local copies, waits for them, and re-layouts: 113 us -> 58.4 us
  matrix products: 49.3 us -> 0 us
  other arithmetic: 57 us -> 40 us
  waiting for transfers between devices: 86.7 us -> 94.1 us
    ppermute x42 -> x0, starting transfers between devices: 89.8 us -> none  [the longest x12 46.2 us: reduce_line(): lax.ppermute(up_send.astype(BF16), name, hop_pairs(line, 1, lambda at: at...]
    pallas_call x0 -> x8, Pallas kernels: none -> 64.4 us  [the longest x1 18 us: feed(): pl.pallas_call(feed_kernel, grid=(hidden // block,), in_specs=[full, full...]
    dot_general x13 -> x0, matrix products: 49.3 us -> none  [the longest x4 19 us: dot_nn(): lax.dot_general(left, right, (((1,), (0,)), ((), ())), preferred_element_...]
    ppermute x40 -> x36, waiting for transfers between devices: 51.7 us -> 94.1 us  [swap_over(): return lax.ppermute(value, name, pairs)]
    ppermute x42 -> x0, waiting for transfers between devices: 35.1 us -> none  [the longest x9 25.5 us: gather_line(): lax.ppermute(above[-1], name, hop_pairs(line, -1, lambda at: at <= size -...]
    another operation x22 -> x3, local copies, waits for them, and re-layouts: 21.4 us -> 0.1 us  [the longest x1 0.09 us: shards(): jnp.stack([owned_pack[:, part * width_loc:(part + 1) * width_loc] for par...]
    reduce_sum x9 -> x0, other arithmetic: 17.4 us -> none  [the longest x1 4.99 us: shards(): jnp.sum(grad_hidden, axis=0)]
    slice x18 -> x11, local copies, waits for them, and re-layouts: 20.9 us -> 5.87 us  [the longest x2 1.9 us: reduce_all(): back = pair[:, middle:].reshape((2, -1) + bits + (rows, cols))]
  transfers between devices with their start and end apart: 82 -> 36, of which waited for: 29 -> 17; matrix products, arithmetic and copies ran while one was open for 35% -> 22% of each run, Pallas kernels for 3% -> 19%
where the time goes in v2:
time: 336 us; the launch traced here: 330 us
  waiting for transfers between devices  94.1 us (28%)
  Pallas kernels  93.3 us (28%)
  local copies, waits for them, and re-layouts  58.4 us (17%)
  starting transfers between devices  42.2 us (13%)
  other arithmetic  40 us (12%)
    ppermute x36, waiting for transfers between devices, swap_over(): return lax.ppermute(value, name, pairs)  94.1 us
    ppermute x36, starting transfers between devices, swap_over(): return lax.ppermute(value, name, pairs)  42.2 us
    pallas_call x1, Pallas kernels, feed(): pl.pallas_call(feed_kernel, grid=(hidden // block,), in_specs=[full, full...  18 us
    unnamed x110, local copies, waits for them, and re-layouts  17.2 us
    pallas_call x1, Pallas kernels, attend_backward(): pl.pallas_call(attend_back_kernel, grid=(pairs,), in_specs=[lanes(0), lan...  15.9 us
    pallas_call x1, Pallas kernels, attend_forward(): pl.pallas_call(attend_kernel, grid=(pairs,), in_specs=[lanes(0), lanes(1)...  13 us
    pallas_call x1, Pallas kernels, feed_grads(): pl.pallas_call(feed_grads_kernel, grid=(2, 2, 2), in_specs=[whole((length...  12.7 us
    concatenate x3, other arithmetic, joined(): jnp.concatenate([block[:, part * size:(part + 1) * size] for part in part...  9.36 us
  transfers between devices with their start and end apart: 36, of which 17 were waited for; matrix products, arithmetic and copies ran while one was open for 22% of the time, Pallas kernels for 19%

profile of v2, /device:TPU:0, one launch (start us, length us, event | category | flops | bytes accessed | tf_op | source)
XLA Modules:
  0.0 330.1 jit_solution(14601074502209293998)
XLA Ops:
  3.8 4.1 %collective-permute-start.1 = (bf16[96,896]{1,0:T(8,128)(2,1)S(1)}, bf16[96,896]{1,0:T(8,128)(2,1)S(1)}, u32[]{:S(2)}, u32[]{:S(2)}) collective-permute-start(bf16[96,896]{1,0:T(8,128)(2,1)S(1)} %concatenate.53), channel_id=1, source_target_pairs={{0,16},{4,20},{8,24},{12,28},{16,0},{20,4},{24,8},{28,12},{1,17},{... | collective-permute-start | bytes 516104 | tf_op jit(solution)/shard_map/ppermute | solution.py:70
  8.4 7.5 %collective-permute-done.1 = bf16[96,896]{1,0:T(8,128)(2,1)S(1)} collective-permute-done((bf16[96,896]{1,0:T(8,128)(2,1)S(1)}, bf16[96,896]{1,0:T(8,128)(2,1)S(1)}, u32[]{:S(2)}, u32[]{:S(2)}) %collective-permute-start.1) | collective-permute-done | bytes 172064 | tf_op jit(solution)/shard_map/ppermute | solution.py:70
  17.0 8.3 %collective-permute-done.2 = bf16[2,96,896]{2,1,0:T(8,128)(2,1)S(1)} collective-permute-done((bf16[2,96,896]{2,1,0:T(8,128)(2,1)S(1)}, bf16[2,96,896]{2,1,0:T(8,128)(2,1)S(1)}, u32[]{:S(2)}, u32[]{:S(2)}) %collective-permute-start.2) | collective-permute-done | bytes 344096 | tf_op jit(solution)/shard_map/ppermute | solution.py:70
  25.5 3.2 collective-permute-start.10
  33.2 8.4 %collective-permute-done.10 = bf16[96,1536]{1,0:T(8,128)(2,1)S(1)} collective-permute-done((bf16[96,1536]{1,0:T(8,128)(2,1)S(1)}, bf16[96,1536]{1,0:T(8,128)(2,1)S(1)}, u32[]{:S(2)}, u32[]{:S(2)}) %collective-permute-start.10) | collective-permute-done | bytes 294944 | tf_op jit(solution)/shard_map/ppermute | solution.py:70
  51.3 6.6 %collective-permute-done.11 = bf16[2,96,1536]{2,1,0:T(8,128)(2,1)} collective-permute-done((bf16[2,96,1536]{2,1,0:T(8,128)(2,1)}, bf16[2,96,1536]{2,1,0:T(8,128)(2,1)}, u32[]{:S(2)}, u32[]{:S(2)}) %collective-permute-start.11) | collective-permute-done | bytes 589856 | tf_op jit(solution)/shard_map/ppermute | solution.py:70
  68.4 2.2 copy.78
  70.6 2.1 copy.79
  73.7 1.7 maximum_dynamic-update-slice_fusion.2
  75.4 1.7 fusion.28
  81.8 4.4 %copy.61.weight_ref = bf16[768,1152]{1,0:T(8,128)(2,1)} copy(bf16[768,1152]{0,1:T(8,128)(2,1)} %fusion.26) | data formatting | bytes 3538944 | tf_op jit(solution)/shard_map/concatenate | solution.py:708
  86.3 2.5 pad_maximum_fusion.3
  90.7 4.5 %first_norm.1 = (bf16[1024,768]{1,0:T(8,128)(2,1)S(1)}, bf16[1024,1152]{1,0:T(8,128)(2,1)}) custom-call(bf16[1024,768]{1,0:T(8,128)(2,1)S(1)} %bitcast.158, f32[12,768]{1,0:T(8,128)S(1)} %convert_bitcast_fusion.1.vec_ref, bf16[768,1152]{1,0:T(8,128)(2,1)S(1)} %copy-done.4, f32[1,1152]{1,0:T(1,128)S(1)} %broadcast_in_dim.119.bias_ref), custom_call_target="tpu_custom_call" | custom-call | flops 1811939328 | bytes 5505024 | tf_op jit(solution)/shard_map/first_norm/pallas_call | solution.py:338
  95.1 2.2 copy-done
  97.4 13.0 %attend_forward.1 = (bf16[1024,384]{1,0:T(8,128)(2,1)}, f32[3,8,1024]{2,1,0:T(8,128)S(1)}) custom-call(bf16[1024,1152]{1,0:T(8,128)(2,1)S(1)} %copy-done, bf16[1024,1152]{1,0:T(8,128)(2,1)S(1)} %copy-done, bf16[1024,1152]{1,0:T(8,128)(2,1)S(1)} %copy-done), custom_call_target="tpu_custom_call" | custom-call | flops 1610612736 | bytes 3145728 | tf_op jit(solution)/shard_map/attend_forward/pallas_call | solution.py:209
  110.5 1.8 fusion.14
  114.2 2.2 broadcast_in_dim.127
  116.4 1.9 bitcast_dynamic-update-slice_fusion.4
  122.5 5.6 %attended_norm.1 = (f32[1024,768]{1,0:T(8,128)}, bf16[1024,768]{1,0:T(8,128)(2,1)S(1)}) custom-call(bf16[1024,384]{1,0:T(8,128)(2,1)} %get-tuple-element.40.heads_ref, bf16[1024,384]{1,0:T(8,128)(2,1)} %collective-permute-done.7.partner_ref, bf16[768,384]{1,0:T(8,128)(2,1)S(1)} %copy.62.own_ref.out_w_ref, bf16[768,384]{1,0:T(8,128)(2,1)S(1)} %copy.63.other_ref, ...), custom_call_target="tpu_custom_call" | custom-call | flops 1207959552 | bytes 7864320 | tf_op jit(solution)/shard_map/attended_norm/pallas_call | solution.py:368
  132.3 14.2 %collective-permute-done.15 = bf16[384,1536]{1,0:T(8,128)(2,1)} collective-permute-done((bf16[384,1536]{1,0:T(8,128)(2,1)}, bf16[384,1536]{1,0:T(8,128)(2,1)}, u32[]{:S(2)}, u32[]{:S(2)}) %collective-permute-start.15) | collective-permute-done | bytes 1179680 | tf_op jit(solution)/shard_map/ppermute | solution.py:70
  147.7 5.9 %fusion.3 = (bf16[768,1536]{1,0:T(8,128)(2,1)}, bf16[768,1536]{1,0:T(8,128)(2,1)}) fusion(bf16[384,1536]{1,0:T(8,128)(2,1)} %collective-permute-done.15, bf16[384,1536]{1,0:T(8,128)(2,1)S(1)} %get-tuple-element.111, bf16[384,1536]{1,0:T(8,128)(2,1)S(1)} %get-tuple-element.110, bf16[384,1536]{1,0:T(8,128)(2,1)} %bitcast.29, bf16[768,768]{1,0:T(8,128)(2,1)S(1)} %fusion.5, ...), kind=kLoop, calls=%fused_computation.6 | loop fusion | flops 17694720 | bytes 11796480 | tf_op jit(solution)/shard_map/concatenate | solution.py:708
  153.5 18.0 %feed.1 = (bf16[1024,1536]{1,0:T(8,128)(2,1)}, bf16[1024,1536]{1,0:T(8,128)(2,1)}, f32[1,1536]{1,0:T(1,128)S(1)}, f32[1024,768]{1,0:T(8,128)}, f32[1024,768]{1,0:T(8,128)}, /*index=5*/bf16[1024,768]{1,0:T(8,128)(2,1)S(1)}) custom-call(bf16[1024,768]{1,0:T(8,128)(2,1)S(1)} %get-tuple-element.42.norm_ref, bf16[1024,768]{1,0:T(8,128)(2,1)S(1)} %bitcast.155, ...), custom_call_target="tpu_custom_call" | custom-call | flops 9663676416 | bytes 9437184 | tf_op jit(solution)/shard_map/feed/pallas_call | solution.py:431
  171.5 12.7 %feed_grads.1 = bf16[2,768,1536]{2,1,0:T(8,128)(2,1)} custom-call(bf16[1024,768]{1,0:T(8,128)(2,1)S(1)} %bitcast.156, bf16[1024,768]{1,0:T(8,128)(2,1)S(1)} %get-tuple-element.42.norm_ref, bf16[1024,1536]{1,0:T(8,128)(2,1)} %get-tuple-element.53.act_ref, bf16[1024,1536]{1,0:T(8,128)(2,1)} %get-tuple-element.54.gup_ref), custom_call_target="tpu_custom_call" | custom-call | flops 4831838208 | bytes 9437184 | tf_op jit(solution)/shard_map/feed_grads/pallas_call | solution.py:475
  184.3 1.8 slice.292
  188.8 2.4 dynamic-slice_convert_fusion.1
  191.9 2.4 slice_bitcast_fusion.1
  195.5 3.7 %add_add_fusion = f32[512,768]{1,0:T(8,128)} fusion(bf16[512,768]{1,0:T(8,128)(2,1)} %collective-permute-done.16, f32[1024,768]{1,0:T(8,128)} %get-tuple-element.44, s32[]{:T(128)S(6)} %select_n.161, f32[1024,768]{1,0:T(8,128)} %get-tuple-element.41.hidden_ref, f32[768]{0:T(1024)S(1)} %get-tuple-element.122), kind=kLoop, calls=%fused_computation.15 | loop fusion | flops 1572864 | bytes 5508100 | tf_op jit(solution)/shard_map/add | solution.py:747
  199.1 15.5 %collective-permute-done.27 = bf16[2,2,96,1536]{3,2,1,0:T(8,128)(2,1)} collective-permute-done((bf16[2,2,96,1536]{3,2,1,0:T(8,128)(2,1)}, bf16[2,2,96,1536]{3,2,1,0:T(8,128)(2,1)}, u32[]{:S(2)}, u32[]{:S(2)}) %collective-permute-start.27) | collective-permute-done | bytes 1179680 | tf_op jit(solution)/shard_map/ppermute | solution.py:70
  217.8 5.6 %collective-permute-done.25 = bf16[384,1536]{1,0:T(8,128)(2,1)} collective-permute-done((bf16[384,1536]{1,0:T(8,128)(2,1)}, bf16[384,1536]{1,0:T(8,128)(2,1)}, u32[]{:S(2)}, u32[]{:S(2)}) %collective-permute-start.25) | collective-permute-done | bytes 1179680 | tf_op jit(solution)/shard_map/ppermute | solution.py:70
  223.4 3.3 %convert_add_fusion.1 = f32[384,1536]{1,0:T(8,128)} fusion(bf16[384,1536]{1,0:T(8,128)(2,1)} %collective-permute-done.25, bf16[2,768,1536]{2,1,0:T(8,128)(2,1)} %feed_grads.1), kind=kLoop, calls=%fused_computation.13 | loop fusion | flops 1769472 | bytes 4718592 | tf_op jit(solution)/shard_map/add | solution.py:133
  226.8 7.2 %second_back.1 = (f32[1024,768]{1,0:T(8,128)}, bf16[1024,768]{1,0:T(8,128)(2,1)S(1)}, bf16[1024,384]{1,0:T(8,128)(2,1)S(1)}, f32[8,768]{1,0:T(8,128)S(1)}) custom-call(f32[1024,768]{1,0:T(8,128)} %get-tuple-element.45.part_ref, bf16[1024,768]{1,0:T(8,128)(2,1)} %collective-permute-done.17.other_ref, f32[1024,768]{1,0:T(8,128)} %get-tuple-element.41.hidden_ref, ...), custom_call_target="tpu_custom_call" | custom-call | flops 603979776 | bytes 15728640 | tf_op jit(solution)/shard_map/second_back/pallas_call | solution.py:518
  235.2 15.9 %attend_backward.1.grad_ref = bf16[1024,1152]{1,0:T(8,128)(2,1)S(1)} custom-call(bf16[1024,1152]{1,0:T(8,128)(2,1)S(1)} %copy-done.1, bf16[1024,1152]{1,0:T(8,128)(2,1)S(1)} %copy-done.1, bf16[1024,1152]{1,0:T(8,128)(2,1)S(1)} %copy-done.1, bf16[1024,384]{1,0:T(8,128)(2,1)S(1)} %get-tuple-element.47.go_ref, f32[3,8,1024]{2,1,0:T(8,128)S(1)} %copy-done.17), custom_call_target="tpu_custom_call" | custom-call | flops 4026531840 | bytes 5505024 | tf_op jit(solution)/shard_map/attend_backward/pallas_call | solution.py:286
  251.2 4.8 %first_back.1 = (f32[1024,768]{1,0:T(8,128)}, f32[8,768]{1,0:T(8,128)S(1)}, f32[8,1152]{1,0:T(8,128)S(1)}) custom-call(bf16[1024,1152]{1,0:T(8,128)(2,1)S(1)} %attend_backward.1.grad_ref, bf16[768,1152]{1,0:T(8,128)(2,1)S(1)} %copy-done.5, bf16[1024,768]{1,0:T(8,128)(2,1)S(1)} %bitcast.160), custom_call_target="tpu_custom_call" | custom-call | flops 1811939328 | bytes 7077888 | tf_op jit(solution)/shard_map/first_back/pallas_call | solution.py:597
  259.3 1.7 collective-permute-done.31
  262.5 8.5 %qkv_grads.1 = bf16[2,768,768]{2,1,0:T(8,128)(2,1)} custom-call(bf16[1024,768]{1,0:T(8,128)(2,1)S(1)} %copy-done.20, bf16[1024,768]{1,0:T(8,128)(2,1)S(1)} %copy-done.15, bf16[1024,1152]{1,0:T(8,128)(2,1)} %copy-done.18, bf16[1024,384]{1,0:T(8,128)(2,1)} %get-tuple-element.40.heads_ref), custom_call_target="tpu_custom_call" | custom-call | flops 2415919104 | bytes 9437184 | tf_op jit(solution)/shard_map/qkv_grads/pallas_call | solution.py:561
  271.0 3.2 collective-permute-start.33
  276.6 1.8 collective-permute-start.34
  278.7 2.0 collective-permute-done.34
  283.0 2.5 collective-permute-done.35
  289.4 1.8 collective-permute-start.29
  291.3 4.7 %collective-permute-done.21 = bf16[2,2,96,768]{3,2,1,0:T(8,128)(2,1)S(1)} collective-permute-done((bf16[2,2,96,768]{3,2,1,0:T(8,128)(2,1)S(1)}, bf16[2,2,96,768]{3,2,1,0:T(8,128)(2,1)S(1)}, u32[]{:S(2)}, u32[]{:S(2)}) %collective-permute-start.21) | collective-permute-done | bytes 589856 | tf_op jit(solution)/shard_map/ppermute | solution.py:70
  296.9 2.0 collective-permute-done.19
  299.1 2.5 collective-permute-done.29
  301.8 4.6 %collective-permute-start.30 = (bf16[96,1536]{1,0:T(8,128)(2,1)S(1)}, bf16[96,1536]{1,0:T(8,128)(2,1)S(1)}, u32[]{:S(2)}, u32[]{:S(2)}) collective-permute-start(bf16[96,1536]{1,0:T(8,128)(2,1)S(1)} %fusion.22), channel_id=1, source_target_pairs={{0,16},{4,20},{8,24},{12,28},{16,0},{20,4},{24,8},{28,12},{1,17},{... | collective-permute-start | bytes 884744 | tf_op jit(solution)/shard_map/ppermute | solution.py:70
  306.4 3.1 token_back.1
  310.6 4.5 %collective-permute-done.30 = bf16[96,1536]{1,0:T(8,128)(2,1)S(1)} collective-permute-done((bf16[96,1536]{1,0:T(8,128)(2,1)S(1)}, bf16[96,1536]{1,0:T(8,128)(2,1)S(1)}, u32[]{:S(2)}, u32[]{:S(2)}) %collective-permute-start.30) | collective-permute-done | bytes 294944 | tf_op jit(solution)/shard_map/ppermute | solution.py:70
  317.9 2.1 collective-permute-start.24
  321.1 5.2 %collective-permute-done.24 = bf16[96,768]{1,0:T(8,128)(2,1)S(1)} collective-permute-done((bf16[96,768]{1,0:T(8,128)(2,1)S(1)}, bf16[96,768]{1,0:T(8,128)(2,1)S(1)}, u32[]{:S(2)}, u32[]{:S(2)}) %collective-permute-start.24) | collective-permute-done | bytes 147488 | tf_op jit(solution)/shard_map/ppermute | solution.py:70
  (265 shorter events, 80.4 us)
Async XLA Ops:
  0.7 16.2 %copy-start.34 = (f32[768,96]{0,1:T(8,128)S(1)}, f32[768,96]{0,1:T(8,128)}, u32[]{:S(2)}) copy-start(f32[768,96]{0,1:T(8,128)} %param.22) | copy-start | bytes 884740
  0.7 16.2 %copy-start.32 = (f32[96,768]{1,0:T(8,128)S(1)}, f32[96,768]{1,0:T(8,128)}, u32[]{:S(2)}) copy-start(f32[96,768]{1,0:T(8,128)} %param.21) | copy-start | bytes 884740
  3.8 12.2 %collective-permute-start.1 = (bf16[96,896]{1,0:T(8,128)(2,1)S(1)}, bf16[96,896]{1,0:T(8,128)(2,1)S(1)}, u32[]{:S(2)}, u32[]{:S(2)}) collective-permute-start(bf16[96,896]{1,0:T(8,128)(2,1)S(1)} %concatenate.53), channel_id=1, source_target_pairs={{0,16},{4,20},{8,24},{12,28},{16,0},{20,4},{24,8},{28,12},{1,17},{... | collective-permute-start | bytes 516104 | tf_op jit(solution)/shard_map/ppermute | solution.py:70
  7.9 23.9 %collective-permute-start = (bf16[512,768]{1,0:T(8,128)(2,1)S(1)}, bf16[512,768]{1,0:T(8,128)(2,1)}, u32[]{:S(2)}, u32[]{:S(2)}) collective-permute-start(bf16[512,768]{1,0:T(8,128)(2,1)S(1)} %copy-done.3), channel_id=1, source_target_pairs={{0,1},{1,0},{2,3},{3,2},{4,5},{5,4},{6,7},{7,6},{8,9},{9,8},{10,11... | collective-permute-start | bytes 2359304 | tf_op jit(solution)/shard_map/ppermute | solution.py:70
  7.9 36.0 %collective-permute-start.9 = (bf16[512,768]{1,0:T(8,128)(2,1)}, bf16[512,768]{1,0:T(8,128)(2,1)S(1)}, u32[]{:S(2)}, u32[]{:S(2)}) collective-permute-start(bf16[512,768]{1,0:T(8,128)(2,1)} %param.18), channel_id=1, source_target_pairs={{0,1},{1,0},{2,3},{3,2},{4,5},{5,4},{6,7},{7,6},{8,9},{9,8},{10,11... | collective-permute-start | bytes 2359304 | tf_op jit(solution)/shard_map/ppermute | solution.py:70
  16.0 9.3 %collective-permute-start.2 = (bf16[2,96,896]{2,1,0:T(8,128)(2,1)S(1)}, bf16[2,96,896]{2,1,0:T(8,128)(2,1)S(1)}, u32[]{:S(2)}, u32[]{:S(2)}) collective-permute-start(bf16[2,96,896]{2,1,0:T(8,128)(2,1)S(1)} %bitcast_dynamic-update-slice_fusion.9), channel_id=1, source_target_pairs={{0,8},{4,12},{8,0},{12,4},{16,24},{20,28},{24,16},{28,20},{1,9},{5... | collective-permute-start | bytes 1032200 | tf_op jit(solution)/shard_map/ppermute | solution.py:70
  25.5 16.1 %collective-permute-start.10 = (bf16[96,1536]{1,0:T(8,128)(2,1)S(1)}, bf16[96,1536]{1,0:T(8,128)(2,1)S(1)}, u32[]{:S(2)}, u32[]{:S(2)}) collective-permute-start(bf16[96,1536]{1,0:T(8,128)(2,1)S(1)} %pad_maximum_fusion.6), channel_id=1, source_target_pairs={{0,16},{4,20},{8,24},{12,28},{16,0},{20,4},{24,8},{28,12},{1,17},{... | collective-permute-start | bytes 884744 | tf_op jit(solution)/shard_map/ppermute | solution.py:70
  28.7 15.4 %collective-permute-start.4 = (bf16[2,96,768]{2,1,0:T(8,128)(2,1)S(1)}, bf16[2,96,768]{2,1,0:T(8,128)(2,1)S(1)}, u32[]{:S(2)}, u32[]{:S(2)}) collective-permute-start(bf16[2,96,768]{2,1,0:T(8,128)(2,1)S(1)} %slice.203), channel_id=1, source_target_pairs={{0,2},{1,3},{2,0},{3,1},{4,6},{5,7},{6,4},{7,5},{8,10},{9,11},{10,... | collective-permute-start | bytes 884744 | tf_op jit(solution)/shard_map/ppermute | solution.py:70
  30.3 16.3 %collective-permute-start.3 = (bf16[2,96,896]{2,1,0:T(8,128)(2,1)S(1)}, bf16[2,96,896]{2,1,0:T(8,128)(2,1)S(1)}, u32[]{:S(2)}, u32[]{:S(2)}) collective-permute-start(bf16[2,96,896]{2,1,0:T(8,128)(2,1)S(1)} %get-tuple-element.114), channel_id=1, source_target_pairs={{0,4},{4,0},{8,12},{12,8},{16,20},{20,16},{24,28},{28,24},{1,5},{5... | collective-permute-start | bytes 1032200 | tf_op jit(solution)/shard_map/ppermute | solution.py:70
  31.9 12.0 %copy-start.39 = (bf16[512,768]{1,0:T(8,128)(2,1)S(1)}, bf16[512,768]{1,0:T(8,128)(2,1)}, u32[]{:S(2)}) copy-start(bf16[512,768]{1,0:T(8,128)(2,1)} %param.18) | copy-start | bytes 2359300
  43.2 14.7 %collective-permute-start.11 = (bf16[2,96,1536]{2,1,0:T(8,128)(2,1)}, bf16[2,96,1536]{2,1,0:T(8,128)(2,1)}, u32[]{:S(2)}, u32[]{:S(2)}) collective-permute-start(bf16[2,96,1536]{2,1,0:T(8,128)(2,1)} %bitcast_dynamic-update-slice_fusion.8), channel_id=1, source_target_pairs={{0,8},{4,12},{8,0},{12,4},{16,24},{20,28},{24,16},{28,20},{1,9},{5... | collective-permute-start | bytes 1769480 | tf_op jit(solution)/shard_map/ppermute | solution.py:70
  45.0 19.3 %collective-permute-start.5 = (bf16[2,96,1664]{2,1,0:T(8,128)(2,1)}, bf16[2,96,1664]{2,1,0:T(8,128)(2,1)}, u32[]{:S(2)}, u32[]{:S(2)}) collective-permute-start(bf16[2,96,1664]{2,1,0:T(8,128)(2,1)} %pad_maximum_fusion.5), channel_id=1, source_target_pairs={{0,4},{4,0},{8,12},{12,8},{16,20},{20,16},{24,28},{28,24},{1,5},{5... | collective-permute-start | bytes 1916936 | tf_op jit(solution)/shard_map/ppermute | solution.py:70
  49.8 25.6 %collective-permute-start.6 = (bf16[384,768]{0,1:T(8,128)(2,1)}, bf16[384,768]{0,1:T(8,128)(2,1)}, u32[]{:S(2)}, u32[]{:S(2)}) collective-permute-start(bf16[384,768]{0,1:T(8,128)(2,1)} %slice.261), channel_id=1, source_target_pairs={{0,2},{1,3},{2,0},{3,1},{4,6},{5,7},{6,4},{7,5},{8,10},{9,11},{10,... | collective-permute-start | bytes 1769480 | tf_op jit(solution)/shard_map/ppermute | solution.py:70
  61.3 53.0 %collective-permute-start.12 = (bf16[2,96,1536]{2,1,0:T(8,128)(2,1)}, bf16[2,96,1536]{2,1,0:T(8,128)(2,1)}, u32[]{:S(2)}, u32[]{:S(2)}) collective-permute-start(bf16[2,96,1536]{2,1,0:T(8,128)(2,1)} %get-tuple-element.113), channel_id=1, source_target_pairs={{0,4},{4,0},{8,12},{12,8},{16,20},{20,16},{24,28},{28,24},{1,5},{5... | collective-permute-start | bytes 1769480 | tf_op jit(solution)/shard_map/ppermute | solution.py:70
  62.8 23.5 %collective-permute-start.13 = (bf16[2,96,1536]{2,1,0:T(8,128)(2,1)}, bf16[2,96,1536]{2,1,0:T(8,128)(2,1)}, u32[]{:S(2)}, u32[]{:S(2)}) collective-permute-start(bf16[2,96,1536]{2,1,0:T(8,128)(2,1)} %get-tuple-element.112), channel_id=1, source_target_pairs={{0,2},{1,3},{2,0},{3,1},{4,6},{5,7},{6,4},{7,5},{8,10},{9,11},{10,... | collective-permute-start | bytes 1769480 | tf_op jit(solution)/shard_map/ppermute | solution.py:70
  73.4 15.9 %copy-start.10 = (f32[12,768]{1,0:T(8,128)}, f32[12,768]{1,0:T(8,128)S(1)}, u32[]{:S(2)}) copy-start(f32[12,768]{1,0:T(8,128)S(1)} %convert_bitcast_fusion.1.vec_ref) | copy-start | bytes 110596
  88.8 39.3 %collective-permute-start.14 = (bf16[2,96,3072]{2,1,0:T(8,128)(2,1)}, bf16[2,96,3072]{2,1,0:T(8,128)(2,1)}, u32[]{:S(2)}, u32[]{:S(2)}) collective-permute-start(bf16[2,96,3072]{2,1,0:T(8,128)(2,1)} %pad_maximum_fusion.3), channel_id=1, source_target_pairs={{0,4},{4,0},{8,12},{12,8},{16,20},{20,16},{24,28},{28,24},{1,5},{5... | collective-permute-start | bytes 3538952 | tf_op jit(solution)/shard_map/ppermute | solution.py:70
  95.1 15.3 %copy-start.19 = (bf16[1024,768]{1,0:T(8,128)(2,1)}, bf16[1024,768]{1,0:T(8,128)(2,1)S(1)}, u32[]{:S(2)}) copy-start(bf16[1024,768]{1,0:T(8,128)(2,1)S(1)} %get-tuple-element.51.norm_ref) | copy-start | bytes 4718596
  97.4 13.1 %copy-start.22 = (bf16[384,896]{0,1:T(8,128)(2,1)S(1)}, bf16[384,896]{0,1:T(8,128)(2,1)}, u32[]{:S(2)}) copy-start(bf16[384,896]{0,1:T(8,128)(2,1)} %copy.78) | copy-start | bytes 2064388
  97.4 13.1 %copy-start.24 = (bf16[384,768]{0,1:T(8,128)(2,1)S(1)}, bf16[384,768]{0,1:T(8,128)(2,1)}, u32[]{:S(2)}) copy-start(bf16[384,768]{0,1:T(8,128)(2,1)} %copy.79) | copy-start | bytes 1769476
  110.4 9.8 %collective-permute-start.7 = (bf16[1024,384]{1,0:T(8,128)(2,1)}, bf16[1024,384]{1,0:T(8,128)(2,1)}, u32[]{:S(2)}, u32[]{:S(2)}) collective-permute-start(bf16[1024,384]{1,0:T(8,128)(2,1)} %get-tuple-element.40.heads_ref), channel_id=1, source_target_pairs={{0,1},{1,0},{2,3},{3,2},{4,5},{5,4},{6,7},{7,6},{8,9},{9,8},{10,11... | collective-permute-start | bytes 2359304 | tf_op jit(solution)/shard_map/ppermute | solution.py:70
  112.4 6.5 %collective-permute-start.8 = (bf16[768,384]{0,1:T(8,128)(2,1)}, bf16[768,384]{0,1:T(8,128)(2,1)}, u32[]{:S(2)}, u32[]{:S(2)}) collective-permute-start(bf16[768,384]{0,1:T(8,128)(2,1)} %fusion.14), channel_id=1, source_target_pairs={{0,1},{1,0},{2,3},{3,2},{4,5},{5,4},{6,7},{7,6},{8,9},{9,8},{10,11... | collective-permute-start | bytes 1769480 | tf_op jit(solution)/shard_map/ppermute | solution.py:70
  118.3 28.2 %collective-permute-start.15 = (bf16[384,1536]{1,0:T(8,128)(2,1)}, bf16[384,1536]{1,0:T(8,128)(2,1)}, u32[]{:S(2)}, u32[]{:S(2)}) collective-permute-start(bf16[384,1536]{1,0:T(8,128)(2,1)} %bitcast.29), channel_id=1, source_target_pairs={{0,2},{1,3},{2,0},{3,1},{4,6},{5,7},{6,4},{7,5},{8,10},{9,11},{10,... | collective-permute-start | bytes 3538952 | tf_op jit(solution)/shard_map/ppermute | solution.py:70
  171.5 12.8 %copy-start.13 = (bf16[1024,768]{1,0:T(8,128)(2,1)}, bf16[1024,768]{1,0:T(8,128)(2,1)S(1)}, u32[]{:S(2)}) copy-start(bf16[1024,768]{1,0:T(8,128)(2,1)S(1)} %get-tuple-element.46) | copy-start | bytes 4718596
  187.2 27.4 %collective-permute-start.27 = (bf16[2,2,96,1536]{3,2,1,0:T(8,128)(2,1)}, bf16[2,2,96,1536]{3,2,1,0:T(8,128)(2,1)}, u32[]{:S(2)}, u32[]{:S(2)}) collective-permute-start(bf16[2,2,96,1536]{3,2,1,0:T(8,128)(2,1)} %dynamic-slice_bitcast_fusion), channel_id=1, source_target_pairs={{0,4},{4,0},{8,12},{12,8},{16,20},{20,16},{24,28},{28,24},{1,5},{5... | collective-permute-start | bytes 3538952 | tf_op jit(solution)/shard_map/ppermute | solution.py:70
  191.1 4.3 %collective-permute-start.16 = (bf16[512,768]{1,0:T(8,128)(2,1)}, bf16[512,768]{1,0:T(8,128)(2,1)}, u32[]{:S(2)}, u32[]{:S(2)}) collective-permute-start(bf16[512,768]{1,0:T(8,128)(2,1)} %dynamic-slice_convert_fusion.1), channel_id=1, source_target_pairs={{0,1},{1,0},{2,3},{3,2},{4,5},{5,4},{6,7},{7,6},{8,9},{9,8},{10,11... | collective-permute-start | bytes 2359304 | tf_op jit(solution)/shard_map/ppermute | solution.py:70
  191.4 35.4 %collective-permute-start.17 = (bf16[1024,768]{1,0:T(8,128)(2,1)}, bf16[1024,768]{1,0:T(8,128)(2,1)}, u32[]{:S(2)}, u32[]{:S(2)}) collective-permute-start(bf16[1024,768]{1,0:T(8,128)(2,1)} %copy-done.13), channel_id=1, source_target_pairs={{0,1},{1,0},{2,3},{3,2},{4,5},{5,4},{6,7},{7,6},{8,9},{9,8},{10,11... | collective-permute-start | bytes 4718600 | tf_op jit(solution)/shard_map/ppermute | solution.py:70
  194.3 29.1 %collective-permute-start.25 = (bf16[384,1536]{1,0:T(8,128)(2,1)}, bf16[384,1536]{1,0:T(8,128)(2,1)}, u32[]{:S(2)}, u32[]{:S(2)}) collective-permute-start(bf16[384,1536]{1,0:T(8,128)(2,1)} %slice_bitcast_fusion.1), channel_id=1, source_target_pairs={{0,2},{1,3},{2,0},{3,1},{4,6},{5,7},{6,4},{7,5},{8,10},{9,11},{10,... | collective-permute-start | bytes 3538952 | tf_op jit(solution)/shard_map/ppermute | solution.py:70
  195.5 19.1 %copy-start.26 = (bf16[2,384,1536]{2,1,0:T(8,128)(2,1)S(1)}, bf16[2,384,1536]{2,1,0:T(8,128)(2,1)}, u32[]{:S(2)}) copy-start(bf16[2,384,1536]{2,1,0:T(8,128)(2,1)} %copy-done.25) | copy-start | bytes 7077892
  217.3 69.4 %collective-permute-start.28 = (bf16[2,96,1536]{2,1,0:T(8,128)(2,1)}, bf16[2,96,1536]{2,1,0:T(8,128)(2,1)}, u32[]{:S(2)}, u32[]{:S(2)}) collective-permute-start(bf16[2,96,1536]{2,1,0:T(8,128)(2,1)} %fusion.16), channel_id=1, source_target_pairs={{0,2},{1,3},{2,0},{3,1},{4,6},{5,7},{6,4},{7,5},{8,10},{9,11},{10,... | collective-permute-start | bytes 1769480 | tf_op jit(solution)/shard_map/ppermute | solution.py:70
  235.2 15.9 %copy-start.5 = (bf16[768,1152]{1,0:T(8,128)(2,1)S(1)}, bf16[768,1152]{1,0:T(8,128)(2,1)}, u32[]{:S(2)}) copy-start(bf16[768,1152]{1,0:T(8,128)(2,1)} %copy.61.weight_ref) | copy-start | bytes 5308420
  235.2 15.9 %copy-start.9 = (bf16[2,512,768]{2,1,0:T(8,128)(2,1)S(1)}, bf16[2,512,768]{2,1,0:T(8,128)(2,1)}, u32[]{:S(2)}) copy-start(bf16[2,512,768]{2,1,0:T(8,128)(2,1)} %copy-done.6) | copy-start | bytes 4718596
  256.8 4.1 %collective-permute-start.31 = (f32[12,768]{1,0:T(8,128)S(1)}, f32[12,768]{1,0:T(8,128)S(1)}, u32[]{:S(2)}, u32[]{:S(2)}) collective-permute-start(f32[12,768]{1,0:T(8,128)S(1)} %concatenate.68), channel_id=1, source_target_pairs={{0,2},{1,3},{2,0},{3,1},{4,6},{5,7},{6,4},{7,5},{8,10},{9,11},{10,... | collective-permute-start | bytes 110600 | tf_op jit(solution)/shard_map/ppermute | solution.py:70
  258.7 29.2 %collective-permute-start.26 = (bf16[2,96,1536]{2,1,0:T(8,128)(2,1)S(1)}, bf16[2,96,1536]{2,1,0:T(8,128)(2,1)}, u32[]{:S(2)}, u32[]{:S(2)}) collective-permute-start(bf16[2,96,1536]{2,1,0:T(8,128)(2,1)S(1)} %fusion.12), channel_id=1, source_target_pairs={{0,4},{4,0},{8,12},{12,8},{16,20},{20,16},{24,28},{28,24},{1,5},{5... | collective-permute-start | bytes 1769480 | tf_op jit(solution)/shard_map/ppermute | solution.py:70
  261.0 10.0 %collective-permute-start.32 = (f32[12,768]{1,0:T(8,128)S(1)}, f32[12,768]{1,0:T(8,128)S(1)}, u32[]{:S(2)}, u32[]{:S(2)}) collective-permute-start(f32[12,768]{1,0:T(8,128)S(1)} %add.309), channel_id=1, source_target_pairs={{0,1},{1,0},{2,3},{3,2},{4,5},{5,4},{6,7},{7,6},{8,9},{9,8},{10,11... | collective-permute-start | bytes 110600 | tf_op jit(solution)/shard_map/ppermute | solution.py:70
  262.5 16.0 %copy-start.2 = (f32[1024,768]{1,0:T(8,128)S(1)}, f32[1024,768]{1,0:T(8,128)}, u32[]{:S(2)}) copy-start(f32[1024,768]{1,0:T(8,128)} %get-tuple-element.49.part_ref) | copy-start | bytes 9437188
  271.0 5.6 %collective-permute-start.33 = (f32[12,768]{1,0:T(8,128)S(1)}, f32[12,768]{1,0:T(8,128)S(1)}, u32[]{:S(2)}, u32[]{:S(2)}) collective-permute-start(f32[12,768]{1,0:T(8,128)S(1)} %add.310), channel_id=1, source_target_pairs={{0,16},{4,20},{8,24},{12,28},{16,0},{20,4},{24,8},{28,12},{1,17},{... | collective-permute-start | bytes 110600 | tf_op jit(solution)/shard_map/ppermute | solution.py:70
  276.6 4.1 %collective-permute-start.34 = (f32[12,768]{1,0:T(8,128)S(1)}, f32[12,768]{1,0:T(8,128)S(1)}, u32[]{:S(2)}, u32[]{:S(2)}) collective-permute-start(f32[12,768]{1,0:T(8,128)S(1)} %add.311), channel_id=1, source_target_pairs={{0,8},{4,12},{8,0},{12,4},{16,24},{20,28},{24,16},{28,20},{1,9},{5... | collective-permute-start | bytes 110600 | tf_op jit(solution)/shard_map/ppermute | solution.py:70
  278.6 27.7 %collective-permute-start.18 = (bf16[512,768]{1,0:T(8,128)(2,1)S(1)}, bf16[512,768]{1,0:T(8,128)(2,1)S(1)}, u32[]{:S(2)}, u32[]{:S(2)}) collective-permute-start(bf16[512,768]{1,0:T(8,128)(2,1)S(1)} %dynamic-slice_convert_fusion), channel_id=1, source_target_pairs={{0,1},{1,0},{2,3},{3,2},{4,5},{5,4},{6,7},{7,6},{8,9},{9,8},{10,11... | collective-permute-start | bytes 2359304 | tf_op jit(solution)/shard_map/ppermute | solution.py:70
  280.8 4.7 %collective-permute-start.35 = (f32[12,768]{1,0:T(8,128)S(1)}, f32[12,768]{1,0:T(8,128)S(1)}, u32[]{:S(2)}, u32[]{:S(2)}) collective-permute-start(f32[12,768]{1,0:T(8,128)S(1)} %add.312), channel_id=1, source_target_pairs={{0,4},{4,0},{8,12},{12,8},{16,20},{20,16},{24,28},{28,24},{1,5},{5... | collective-permute-start | bytes 110600 | tf_op jit(solution)/shard_map/ppermute | solution.py:70
  281.4 14.6 %collective-permute-start.21 = (bf16[2,2,96,768]{3,2,1,0:T(8,128)(2,1)S(1)}, bf16[2,2,96,768]{3,2,1,0:T(8,128)(2,1)S(1)}, u32[]{:S(2)}, u32[]{:S(2)}) collective-permute-start(bf16[2,2,96,768]{3,2,1,0:T(8,128)(2,1)S(1)} %dynamic-slice_bitcast_fusion.1), channel_id=1, source_target_pairs={{0,4},{4,0},{8,12},{12,8},{16,20},{20,16},{24,28},{28,24},{1,5},{5... | collective-permute-start | bytes 1769480 | tf_op jit(solution)/shard_map/ppermute | solution.py:70
  285.5 13.4 %collective-permute-start.19 = (bf16[384,768]{1,0:T(8,128)(2,1)S(1)}, bf16[384,768]{1,0:T(8,128)(2,1)S(1)}, u32[]{:S(2)}, u32[]{:S(2)}) collective-permute-start(bf16[384,768]{1,0:T(8,128)(2,1)S(1)} %slice_bitcast_fusion.4), channel_id=1, source_target_pairs={{0,2},{1,3},{2,0},{3,1},{4,6},{5,7},{6,4},{7,5},{8,10},{9,11},{10,... | collective-permute-start | bytes 1769480 | tf_op jit(solution)/shard_map/ppermute | solution.py:70
  289.4 12.2 %collective-permute-start.29 = (bf16[2,96,1536]{2,1,0:T(8,128)(2,1)S(1)}, bf16[2,96,1536]{2,1,0:T(8,128)(2,1)S(1)}, u32[]{:S(2)}, u32[]{:S(2)}) collective-permute-start(bf16[2,96,1536]{2,1,0:T(8,128)(2,1)S(1)} %fusion.11), channel_id=1, source_target_pairs={{0,8},{4,12},{8,0},{12,4},{16,24},{20,28},{24,16},{28,20},{1,9},{5... | collective-permute-start | bytes 1769480 | tf_op jit(solution)/shard_map/ppermute | solution.py:70
  296.2 13.3 %collective-permute-start.22 = (bf16[2,96,768]{2,1,0:T(8,128)(2,1)S(1)}, bf16[2,96,768]{2,1,0:T(8,128)(2,1)S(1)}, u32[]{:S(2)}, u32[]{:S(2)}) collective-permute-start(bf16[2,96,768]{2,1,0:T(8,128)(2,1)S(1)} %fusion.24), channel_id=1, source_target_pairs={{0,2},{1,3},{2,0},{3,1},{4,6},{5,7},{6,4},{7,5},{8,10},{9,11},{10,... | collective-permute-start | bytes 884744 | tf_op jit(solution)/shard_map/ppermute | solution.py:70
  299.1 10.5 %collective-permute-start.20 = (bf16[2,96,768]{2,1,0:T(8,128)(2,1)S(1)}, bf16[2,96,768]{2,1,0:T(8,128)(2,1)S(1)}, u32[]{:S(2)}, u32[]{:S(2)}) collective-permute-start(bf16[2,96,768]{2,1,0:T(8,128)(2,1)S(1)} %fusion.23), channel_id=1, source_target_pairs={{0,4},{4,0},{8,12},{12,8},{16,20},{20,16},{24,28},{28,24},{1,5},{5... | collective-permute-start | bytes 884744 | tf_op jit(solution)/shard_map/ppermute | solution.py:70
  301.8 13.3 %collective-permute-start.30 = (bf16[96,1536]{1,0:T(8,128)(2,1)S(1)}, bf16[96,1536]{1,0:T(8,128)(2,1)S(1)}, u32[]{:S(2)}, u32[]{:S(2)}) collective-permute-start(bf16[96,1536]{1,0:T(8,128)(2,1)S(1)} %fusion.22), channel_id=1, source_target_pairs={{0,16},{4,20},{8,24},{12,28},{16,0},{20,4},{24,8},{28,12},{1,17},{... | collective-permute-start | bytes 884744 | tf_op jit(solution)/shard_map/ppermute | solution.py:70
  309.8 8.0 %collective-permute-start.23 = (bf16[2,96,768]{2,1,0:T(8,128)(2,1)S(1)}, bf16[2,96,768]{2,1,0:T(8,128)(2,1)S(1)}, u32[]{:S(2)}, u32[]{:S(2)}) collective-permute-start(bf16[2,96,768]{2,1,0:T(8,128)(2,1)S(1)} %fusion.21), channel_id=1, source_target_pairs={{0,8},{4,12},{8,0},{12,4},{16,24},{20,28},{24,16},{28,20},{1,9},{5... | collective-permute-start | bytes 884744 | tf_op jit(solution)/shard_map/ppermute | solution.py:70
  317.9 8.3 %collective-permute-start.24 = (bf16[96,768]{1,0:T(8,128)(2,1)S(1)}, bf16[96,768]{1,0:T(8,128)(2,1)S(1)}, u32[]{:S(2)}, u32[]{:S(2)}) collective-permute-start(bf16[96,768]{1,0:T(8,128)(2,1)S(1)} %fusion.31), channel_id=1, source_target_pairs={{0,16},{4,20},{8,24},{12,28},{16,0},{20,4},{24,8},{28,12},{1,17},{... | collective-permute-start | bytes 442376 | tf_op jit(solution)/shard_map/ppermute | solution.py:70
  (39 other events, 217.0 us)

commit v3 on v2

--- a/solution.py
+++ b/solution.py
@@ -1,3 +1,4 @@
+import functools
 import math
 
 import jax
@@ -51,99 +52,134 @@
     return (updated, first, second)
 
 
-def bit_strides(high, low):
-    strides = []
-    while high > low:
-        high //= 2
-        strides.append(high)
-    return strides
-
-
-def place_on(line):
-    name, stride = line
-    return lax.axis_index(name) // stride % 2
-
-
 def swap_over(value, line):
-    name, stride = line
-    pairs = [(index, index ^ stride) for index in range(lax.axis_size(name))]
+    name, offset = line
+    pairs = [(index, index ^ offset) for index in range(lax.axis_size(name))]
     return lax.ppermute(value, name, pairs)
 
 
-def gather_bit(block, line, dim):
-    other = jnp.expand_dims(swap_over(block, line), dim)
-    shape = block.shape[:dim] + (2,) + block.shape[dim:]
-    both = jnp.broadcast_to(jnp.expand_dims(block, dim), shape)
-    return lax.dynamic_update_slice_in_dim(both, other, 1 - place_on(line), dim)
-
-
-def gather_bits(block, lines, dim):
-    for line in lines:
-        block = gather_bit(block, line, dim)
-        dim += 1
-    return block
-
-
-def reduce_bit(parts, line, dim):
-    place = place_on(line)
-
-    def part(index):
-        return lax.dynamic_index_in_dim(parts, index, dim, keepdims=False)
-
-    sent = swap_over(part(1 - place).astype(BF16), line)
-    return part(place).astype(F32) + sent.astype(F32)
-
-
-def reduce_bits(parts, lines, dim):
-    for line in reversed(lines):
-        parts = reduce_bit(parts, line, dim + len(lines) - 1)
-        lines = lines[:-1]
-    return parts
+def bit_offsets(low, high):
+    offsets = []
+    while low < high:
+        offsets.append(low)
+        low *= 2
+    return offsets
+
+
+def flip_order(blocks):
+    count = blocks.shape[0]
+    row = lax.axis_index("row")
+    for offset in bit_offsets(1, count):
+        cut = blocks.reshape((-1, 2, offset) + blocks.shape[1:])
+        turned = jnp.where((row // offset) % 2 == 1, cut[:, ::-1], cut)
+        blocks = turned.reshape(blocks.shape)
+    return blocks
+
+
+def gather_small(block):
+    blocks = block[None]
+    for offset in bit_offsets(1, lax.axis_size("row")):
+        blocks = jnp.concatenate([blocks, swap_over(blocks, ("row", offset))], axis=0)
+    return flip_order(blocks)
+
+
+class Gathered:
+    def __init__(self, arrays, table):
+        self.arrays = arrays
+        self.table = table
+        self.rows = arrays[0].shape[1]
+        self.cols = arrays[0].shape[2]
+        if self.rows % 16:
+            total = []
+            for x in range(2):
+                found = sorted((offset, array, at) for x_at, array, at, offset in table if x_at == x)
+                blocks = jnp.stack([arrays[array][at] for _, array, at in found])
+                total.append(flip_order(blocks).reshape(-1, self.cols))
+            self.arrays = [jnp.stack(total)]
+            self.table = [(0, 0, 0, 0), (1, 0, 1, 0)]
+            self.rows = self.arrays[0].shape[1]
 
 
 class Grid:
     def __init__(self, row_count):
-        near_size = {8: 2, 64: 4}.get(row_count, 1)
+        self.near_size = {8: 2, 64: 4}.get(row_count, 1)
         self.row_count = row_count
-        self.far = [("row", stride) for stride in bit_strides(row_count, near_size)]
-        self.near = [("row", stride) for stride in bit_strides(near_size, 1)]
+        self.far_count = row_count // self.near_size
+        self.near = bit_offsets(1, self.near_size)
         self.x_line = ("col", 2)
 
     def gather_far(self, block):
-        rows, cols = block.shape
-        return gather_bits(block, self.far, 0).reshape(-1, rows, cols)
-
-    def gather_near(self, stacked, keep_cols):
-        far, _, cols = stacked.shape
-        front, back = stacked[: far // 2], stacked[far // 2 :]
-        front_own = gather_bits(front, self.near, 1).reshape(-1, cols)
-        front_other = swap_over(front_own[:, :keep_cols], self.x_line)
-        back_other = swap_over(back[:, :, :keep_cols], self.x_line)
-        back_pair = gather_bits(jnp.concatenate([back, back_other], axis=2), self.near, 1)
-        back_pair = back_pair.reshape(-1, cols + keep_cols)
-        own = jnp.concatenate([front_own, back_pair[:, :cols]], axis=0)
-        other = jnp.concatenate([front_other, back_pair[:, cols:]], axis=0)
-        return own, other
-
-    def reduce_all(self, pair):
+        blocks = [block]
+        for index in range(1, self.far_count):
+            blocks.append(swap_over(block, ("row", index * self.near_size)))
+        return blocks
+
+    def gather_near(self, blocks):
+        half = self.far_count // 2
+        front, back = jnp.stack(blocks[:half]), jnp.stack(blocks[half:])
+        front_at = [index * self.near_size for index in range(half)]
+        back_at = [(index + half) * self.near_size for index in range(half)]
+        back_x = swap_over(back, self.x_line)
+        for offset in self.near:
+            front = jnp.concatenate([front, swap_over(front, ("row", offset))], axis=0)
+            front_at = front_at + [at ^ offset for at in front_at]
+        back = jnp.concatenate([back, back_x], axis=0)
+        back_at = [(x, at) for x in range(2) for at in back_at]
+        arrays = [front, swap_over(front, self.x_line), back]
+        table = [(x, x, index, at) for x in range(2) for index, at in enumerate(front_at)]
+        table += [(x, 2, index, at) for index, (x, at) in enumerate(back_at)]
+        for offset in self.near:
+            sent = back if len(arrays) == 3 else jnp.concatenate(arrays[2:], axis=0)
+            arrays.append(swap_over(sent, ("row", offset)))
+            moved = [(x, at ^ offset) for x, at in back_at]
+            table += [(x, len(arrays) - 1, index, at) for index, (x, at) in enumerate(moved)]
+            back_at = back_at + moved
+        return Gathered(arrays, table)
+
+    def reduce_near(self, pair, hold=None):
         _, all_rows, cols = pair.shape
         rows = all_rows // self.row_count
-        middle = all_rows // 2
-        bits = (2,) * len(self.near)
-        front = pair[0, :middle].astype(F32) + swap_over(pair[1, :middle], self.x_line).astype(F32)
-        front = reduce_bits(front.reshape((-1,) + bits + (rows, cols)), self.near, 1)
-        back = pair[:, middle:].reshape((2, -1) + bits + (rows, cols))
-        back = reduce_bits(back, self.near, 2)
-        back = back[0].astype(F32) + swap_over(back[1].astype(BF16), self.x_line).astype(F32)
-        total = jnp.concatenate([front, back], axis=0)
-        total = total.reshape((2,) * len(self.far) + (rows, cols))
-        return reduce_bits(total, self.far, 0)
+        half = self.far_count // 2
+        pair = pair.reshape((2, 2, half, self.near_size, rows, cols))
+        front_x = swap_over(pair[1, 0], self.x_line)
+        back = pair[:, 1]
+        step = self.near_size // 2
+        sent = swap_over(back[:, :, step:], ("row", step)) if step else None
+        if hold is not None:
+            front_x, sent, _ = lax.optimization_barrier((front_x, sent, hold))
+        back = back.astype(F32)
+        if step:
+            back = back[:, :, :step] + sent.astype(F32)
+        front = pair[0, 0].astype(F32) + front_x.astype(F32)
+        back = self.reduce_bits(back, 2)
+        back = back[0] + swap_over(back[1].astype(BF16), self.x_line).astype(F32)
+        front = self.reduce_bits(front, 1)
+        return jnp.concatenate([front, back], axis=0).reshape(self.far_count, rows, cols)
+
+    def reduce_bits(self, parts, dim):
+        while parts.shape[dim] > 1:
+            step = parts.shape[dim] // 2
+            kept = lax.slice_in_dim(parts, 0, step, axis=dim)
+            sent = lax.slice_in_dim(parts, step, 2 * step, axis=dim).astype(BF16)
+            parts = kept + swap_over(sent, ("row", step)).astype(F32)
+        return parts
+
+    def reduce_far(self, parts):
+        low = parts.astype(BF16)
+        arrived = [
+            swap_over(low[index], ("row", index * self.near_size))
+            for index in range(1, self.far_count)
+        ]
+        total = parts[0]
+        for part in arrived:
+            total = total + part.astype(F32)
+        return total
 
 
 def sum_everywhere(value):
     for name in ("col", "row"):
-        for stride in bit_strides(lax.axis_size(name), 1):
-            value = value + swap_over(value, (name, stride))
+        for offset in bit_offsets(1, lax.axis_size(name)):
+            value = value + swap_over(value, (name, offset))
     return value
 
 
@@ -166,7 +202,7 @@
     return key_at <= query_at
 
 
-def attend_kernel(q_ref, k_ref, v_ref, out_ref, lse_ref):
+def attend_kernel(q_ref, k_ref, v_ref, out_ref, turned_ref, lse_ref):
     length = q_ref.shape[0]
     block = min(QUERY_BLOCK, length)
     allowed = causal_block(block)
@@ -196,7 +232,9 @@
                 result = result + dot_nn(values_t[rows, 0:first], (rest * inverse).astype(BF16))
             outs.append(result)
             lse_ref[0, half : half + 1, first:last] = top + jnp.log(total)
-        out_ref[first:last, :] = jnp.concatenate(outs, axis=0).T.astype(BF16)
+        turned = jnp.concatenate(outs, axis=0)
+        out_ref[first:last, :] = turned.T.astype(BF16)
+        turned_ref[:, first:last] = turned.astype(BF16)
 
 
 def attend_forward(qkv):
@@ -210,9 +248,14 @@
         attend_kernel,
         grid=(pairs,),
         in_specs=[lanes(0), lanes(1), lanes(2)],
-        out_specs=[lanes(0), pl.BlockSpec((1, 8, length), lambda pair: (pair, 0, 0))],
+        out_specs=[
+            lanes(0),
+            pl.BlockSpec((PAIR, length), lambda pair: (pair, 0)),
+            pl.BlockSpec((1, 8, length), lambda pair: (pair, 0, 0)),
+        ],
         out_shape=[
             jax.ShapeDtypeStruct((length, pairs * PAIR), BF16),
+            jax.ShapeDtypeStruct((pairs * PAIR, length), BF16),
             jax.ShapeDtypeStruct((pairs, 8, length), F32),
         ],
         compiler_params=pltpu.CompilerParams(vmem_limit_bytes=40 * 2**20),
@@ -325,46 +368,138 @@
 PARAMS = pltpu.CompilerParams(vmem_limit_bytes=48 * 2**20)
 
 
-def first_norm_kernel(tokens_ref, vec_ref, weight_ref, bias_ref, norm_ref, qkv_ref):
+ANYWHERE = pl.BlockSpec(memory_space=pl.ANY)
+
+
+def weight_copies(gathered, refs, held, sems):
+    row = lax.axis_index("row")
+    copies = ([], [])
+    for number, (x, array, at, offset) in enumerate(gathered.table):
+        if len(gathered.table) > 2:
+            start = pl.multiple_of((row ^ offset) * gathered.rows, 16)
+        else:
+            start = 0
+        target = held.at[x, pl.ds(start, gathered.rows), :]
+        copies[x].append(
+            pltpu.make_async_copy(refs[array].at[at], target, sems.at[number])
+        )
+    return copies
+
+
+def weight_scratch(gathered):
+    all_rows = len(gathered.table) // 2 * gathered.rows
+    return [
+        pltpu.VMEM((2, all_rows, gathered.cols), BF16),
+        pltpu.SemaphoreType.DMA((len(gathered.table),)),
+    ]
+
+
+def start_all(copies):
+    for copy in copies:
+        copy.start()
+
+
+def wait_all(copies):
+    for copy in copies:
+        copy.wait()
+
+
+def store_rows(value, out_ref, x, lanes, count):
+    rows = value.shape[0] // count
+    if rows % 16:
+        out_ref[x, :, lanes] = value
+        return
+    row = lax.axis_index("row")
+    for index in range(count):
+        start = pl.multiple_of((row ^ index) * rows, 16)
+        out_ref[x, pl.ds(start, rows), lanes] = value[index * rows : (index + 1) * rows]
+
+
+def relative_rows(pair, count):
+    _, all_rows, cols = pair.shape
+    if all_rows // count % 16 == 0:
+        return pair
+    blocks = jnp.moveaxis(pair.reshape(2, count, -1, cols), 1, 0)
+    return jnp.moveaxis(flip_order(blocks), 0, 1).reshape(pair.shape)
+
+
+def turn(value):
+    return value.T
+
+
+def first_norm_kernel(gathered, cols, tokens_ref, vec_ref, bias_ref, *refs):
+    count = len(gathered.arrays)
+    norm_ref, qkv_ref, out_w_ref, held, sems = refs[count:]
+    copies = weight_copies(gathered, refs[:count], held, sems)
+    third = cols // 3
+
+    @pl.when(pl.program_id(0) == 0)
+    def _():
+        start_all(copies[0] + copies[1])
+
     normed, _ = normalize_rows(tokens_ref[...].astype(F32))
     first_in = (normed * vec_ref[0:1, :] + vec_ref[1:2, :]).astype(BF16)
     norm_ref[...] = first_in
-    qkv_ref[...] = (dot_nn(first_in, weight_ref[...]) + bias_ref[...]).astype(BF16)
-
-
-def first_norm(tokens, vec_all, weight, bias):
+
+    @pl.when(pl.program_id(0) == 0)
+    def _():
+        wait_all(copies[0] + copies[1])
+        for x in range(2):
+            out_w_ref[:, x * third : (x + 1) * third] = held[x, :, held.shape[2] - third :]
+
+    for x in range(2):
+        result = dot_nn(first_in, held[x, :, :cols])
+        for part in range(3):
+            lanes = slice((2 * part + x) * third, (2 * part + x + 1) * third)
+            value = result[:, part * third : (part + 1) * third] + bias_ref[0:1, lanes]
+            qkv_ref[:, lanes] = value.astype(BF16)
+
+
+def first_norm(tokens, vec_all, bias, gathered, width_loc):
     length, width = tokens.shape
-    cols = weight.shape[1]
+    cols = 3 * width_loc
     return pl.pallas_call(
-        first_norm_kernel,
+        functools.partial(first_norm_kernel, gathered, cols),
         grid=(length // ROW_BLOCK,),
-        in_specs=[
+        in_specs=[rows_of(ROW_BLOCK, width), whole(vec_all.shape), whole(bias.shape)]
+        + [ANYWHERE] * len(gathered.arrays),
+        out_specs=[
             rows_of(ROW_BLOCK, width),
-            whole(vec_all.shape),
-            whole(weight.shape),
-            whole(bias.shape),
-        ],
-        out_specs=[rows_of(ROW_BLOCK, width), rows_of(ROW_BLOCK, cols)],
-        out_shape=[shaped((length, width), BF16), shaped((length, cols), BF16)],
+            rows_of(ROW_BLOCK, 2 * cols),
+            whole((width, 2 * width_loc)),
+        ],
+        out_shape=[
+            shaped((length, width), BF16),
+            shaped((length, 2 * cols), BF16),
+            shaped((width, 2 * width_loc), BF16),
+        ],
+        scratch_shapes=weight_scratch(gathered),
         compiler_params=PARAMS,
-        cost_estimate=cost(2 * length * width * cols, 2 * length * (2 * width + cols)),
+        cost_estimate=cost(4 * length * width * cols, 2 * length * (2 * width + cols)),
         name="first_norm",
-    )(tokens, vec_all, weight, bias)
+    )(tokens, vec_all, bias, *gathered.arrays)
 
 
 def attended_kernel(
-    heads_ref, partner_ref, own_ref, other_ref, tokens_ref, vec_ref, hidden_ref, norm_ref
+    heads_ref, partner_ref, own_ref, other_ref, tokens_ref, vec_ref, first_ref, cot_ref,
+    hidden_ref, norm_ref, norm_turned_ref, first_turned_ref, cot_turned_ref,
 ):
     attended = dot_nt(heads_ref[...], own_ref[...]) + dot_nt(partner_ref[...], other_ref[...])
     hidden = tokens_ref[...].astype(F32) + attended + vec_ref[4:5, :]
     hidden_ref[...] = hidden
     normed, _ = normalize_rows(hidden)
-    norm_ref[...] = (normed * vec_ref[5:6, :] + vec_ref[6:7, :]).astype(BF16)
-
-
-def attended_norm(heads, partner_heads, own_out, partner_out, tokens, vec_all):
+    second_in = (normed * vec_ref[5:6, :] + vec_ref[6:7, :]).astype(BF16)
+    norm_ref[...] = second_in
+    norm_turned_ref[...] = turn(second_in)
+    first_turned_ref[...] = turn(first_ref[...])
+    cot_turned_ref[...] = turn(cot_ref[...])
+
+
+def attended_norm(heads, partner_heads, own_out, partner_out, tokens, vec_all, first_in, cot):
     length, width = tokens.shape
     cols = heads.shape[1]
+    full = rows_of(ROW_BLOCK, width)
+    turned = pl.BlockSpec((width, ROW_BLOCK), lambda step: (0, step))
     return pl.pallas_call(
         attended_kernel,
         grid=(length // ROW_BLOCK,),
@@ -373,34 +508,49 @@
             rows_of(ROW_BLOCK, cols),
             whole(own_out.shape),
             whole(partner_out.shape),
-            rows_of(ROW_BLOCK, width),
+            full,
             whole(vec_all.shape),
-        ],
-        out_specs=[rows_of(ROW_BLOCK, width), rows_of(ROW_BLOCK, width)],
-        out_shape=[shaped((length, width), F32), shaped((length, width), BF16)],
+            full,
+            full,
+        ],
+        out_specs=[full, full, turned, turned, turned],
+        out_shape=[shaped((length, width), F32), shaped((length, width), BF16)]
+        + [shaped((width, length), BF16)] * 3,
         compiler_params=PARAMS,
-        cost_estimate=cost(4 * length * width * cols, length * width * 10),
+        cost_estimate=cost(4 * length * width * cols, length * width * 20),
         name="attended_norm",
-    )(heads, partner_heads, own_out, partner_out, tokens, vec_all)
-
-
-def feed_kernel(
-    norm_ref, cot_ref, up_ref, down_ref, bias_ref, act_ref, gup_ref, bias_sum_ref, out_ref, back_ref,
-    back_low_ref,
-):
+    )(heads, partner_heads, own_out, partner_out, tokens, vec_all, first_in, cot)
+
+
+def feed_kernel(gathered, norm_ref, cot_ref, bias_ref, *refs):
+    count = len(gathered.arrays)
+    act_ref, gup_ref, bias_sum_ref, out_ref, back_ref, back_low_ref, held, sems = refs[count:]
+    copies = weight_copies(gathered, refs[:count], held, sems)
     step = pl.program_id(0)
     length = norm_ref.shape[0]
     curve, cubic = math.sqrt(2 / math.pi), 0.044715
+    cols = held.shape[2] // 2
+    block = act_ref.shape[1]
+    per_x = cols // block
+    x = step // per_x
+    up_lanes = pl.ds(pl.multiple_of(step % per_x * block, 128), block)
+    down_lanes = pl.ds(pl.multiple_of(cols + step % per_x * block, 128), block)
 
     @pl.when(step == 0)
     def _():
+        start_all(copies[0] + copies[1])
         out_ref[...] = jnp.zeros_like(out_ref)
         back_ref[...] = jnp.zeros_like(back_ref)
+        wait_all(copies[0])
+
+    @pl.when(step == per_x)
+    def _():
+        wait_all(copies[1])
 
     bias_sum = jnp.zeros(bias_ref.shape, F32)
     for first in range(0, length, ROW_BLOCK):
         rows = slice(first, first + ROW_BLOCK)
-        up = dot_nn(norm_ref[rows, :], up_ref[...]) + bias_ref[...]
+        up = dot_nn(norm_ref[rows, :], held[x, :, up_lanes]) + bias_ref[...]
         square = up * up
         tanh = jnp.tanh(curve * up * (1.0 + cubic * square))
         act = (0.5 * up * (1.0 + tanh)).astype(BF16)
@@ -408,11 +558,11 @@
         slope = 0.5 * (1.0 + tanh) + 0.5 * up * (1.0 - tanh * tanh) * (
             curve * (1.0 + 3.0 * cubic * square)
         )
-        grad_up = (dot_nn(cot_ref[rows, :], down_ref[...]) * slope).astype(BF16)
+        grad_up = (dot_nn(cot_ref[rows, :], held[x, :, down_lanes]) * slope).astype(BF16)
         gup_ref[rows, :] = grad_up
         bias_sum = bias_sum + jnp.sum(grad_up.astype(F32), axis=0, keepdims=True)
-        out_ref[rows, :] += dot_nt(act, down_ref[...])
-        back_ref[rows, :] += dot_nt(grad_up, up_ref[...])
+        out_ref[rows, :] += dot_nt(act, held[x, :, down_lanes])
+        back_ref[rows, :] += dot_nt(grad_up, held[x, :, up_lanes])
     bias_sum_ref[...] = bias_sum
 
     @pl.when(step == pl.num_programs(0) - 1)
@@ -420,18 +570,17 @@
         back_low_ref[...] = back_ref[...].astype(BF16)
 
 
-def feed(norm, cot, up, down, bias):
+def feed(norm, cot, bias, gathered):
     length, width = norm.shape
-    hidden = up.shape[1]
-    block = 512
-    cols = pl.BlockSpec((width, block), lambda step: (0, step))
+    hidden = bias.shape[1]
+    block = hidden // 4
     tall = pl.BlockSpec((length, block), lambda step: (0, step))
     flat = pl.BlockSpec((1, block), lambda step: (0, step))
     full = whole((length, width))
     return pl.pallas_call(
-        feed_kernel,
+        functools.partial(feed_kernel, gathered),
         grid=(hidden // block,),
-        in_specs=[full, full, cols, cols, flat],
+        in_specs=[full, full, flat] + [ANYWHERE] * len(gathered.arrays),
         out_specs=[tall, tall, flat, full, full, full],
         out_shape=[
             shaped((length, hidden), BF16),
@@ -441,58 +590,53 @@
             shaped((length, width), F32),
             shaped((length, width), BF16),
         ],
+        scratch_shapes=weight_scratch(gathered),
         compiler_params=PARAMS,
         cost_estimate=cost(8 * length * width * hidden, 4 * length * (width + hidden)),
         name="feed",
-    )(norm, cot, up, down, bias)
-
-
-def feed_grads_kernel(cot_ref, norm_ref, act_ref, gup_ref, out_ref, turned):
+    )(norm, cot, bias, *gathered.arrays)
+
+
+def feed_grads_kernel(row_count, cot_ref, norm_ref, act_ref, gup_ref, out_ref):
     kind = pl.program_id(0)
-    first = (pl.program_id(1) == 0) & (pl.program_id(2) == 0)
-
-    @pl.when(first & (kind == 0))
-    def _():
-        turned[...] = cot_ref[...].T
-
-    @pl.when(first & (kind == 1))
-    def _():
-        turned[...] = norm_ref[...].T
 
     @pl.when(kind == 0)
     def _():
-        out_ref[0] = dot_nn(turned[...], act_ref[...]).astype(BF16)
+        value = dot_nn(cot_ref[...], act_ref[...]).astype(BF16)
+        store_rows(value, out_ref, 0, slice(None), row_count)
 
     @pl.when(kind == 1)
     def _():
-        out_ref[0] = dot_nn(turned[...], gup_ref[...]).astype(BF16)
-
-
-def feed_grads(cot, norm, act, grad_up):
-    length, width = norm.shape
+        value = dot_nn(norm_ref[...], gup_ref[...]).astype(BF16)
+        store_rows(value, out_ref, 0, slice(None), row_count)
+
+
+def feed_grads(cot_turned, norm_turned, act, grad_up, row_count):
+    width, length = cot_turned.shape
     hidden = act.shape[1]
-    block = hidden // 4
+    block = hidden // 2
     return pl.pallas_call(
-        feed_grads_kernel,
-        grid=(2, 2, 2),
+        functools.partial(feed_grads_kernel, row_count),
+        grid=(2, 2),
         in_specs=[
-            whole((length, width)),
-            whole((length, width)),
-            pl.BlockSpec((length, block), lambda kind, x, n: (0, jnp.where(kind == 0, 2 * x + n, 3))),
-            pl.BlockSpec((length, block), lambda kind, x, n: (0, jnp.where(kind == 1, 2 * x + n, 0))),
-        ],
-        out_specs=pl.BlockSpec((1, width, block), lambda kind, x, n: (x, 0, 2 * kind + n)),
+            whole((width, length)),
+            whole((width, length)),
+            pl.BlockSpec((length, block), lambda kind, x: (0, jnp.where(kind == 0, x, 1))),
+            pl.BlockSpec((length, block), lambda kind, x: (0, jnp.where(kind == 1, x, 0))),
+        ],
+        out_specs=pl.BlockSpec((1, width, block), lambda kind, x: (x, 0, 1 - kind)),
         out_shape=shaped((2, width, hidden), BF16),
-        scratch_shapes=[pltpu.VMEM((width, length), BF16)],
         compiler_params=PARAMS,
         cost_estimate=cost(4 * length * width * hidden, 4 * length * (width + hidden)),
         name="feed_grads",
-    )(cot, norm, act, grad_up)
+    )(cot_turned, norm_turned, act, grad_up)
 
 
 def second_back_kernel(
-    part_ref, other_ref, hidden_ref, cot_ref, vec_ref, out_w_ref, grad_ref, low_ref, heads_ref, sum_ref
+    part_ref, other_ref, hidden_ref, cot_ref, vec_ref, out_w_ref, turned_ref,
+    grad_ref, heads_ref, sum_ref, out_grad_ref, total,
 ):
+    step = pl.program_id(0)
     normed, inv_std = normalize_rows(hidden_ref[...])
     part = part_ref[...]
     cot = cot_ref[...].astype(F32)
@@ -500,114 +644,126 @@
     grad = cot + norm_back(grad_second * vec_ref[5:6, :], normed, inv_std)
     grad_ref[...] = grad
     low = grad.astype(BF16)
-    low_ref[...] = low
     heads_ref[...] = dot_nn(low, out_w_ref[...]).astype(BF16)
 
-    @pl.when(pl.program_id(0) == 0)
+    @pl.when(step == 0)
     def _():
         sum_ref[...] = jnp.zeros_like(sum_ref)
-
+        total[...] = jnp.zeros_like(total)
+
+    total[...] += dot_nn(turned_ref[...], low)
     for row, value in enumerate((grad, part * normed, part, cot)):
         sum_ref[row : row + 1, :] += jnp.sum(value, axis=0, keepdims=True)
 
-
-def second_back(part, other, hidden, cot, vec_all, out_w):
+    @pl.when(step == pl.num_programs(0) - 1)
+    def _():
+        out_grad_ref[...] = total[...].T.astype(BF16)
+
+
+def second_back(part, other, hidden, cot, vec_all, out_w, heads_turned):
     length, width = part.shape
     cols = out_w.shape[1]
     full = rows_of(ROW_BLOCK, width)
     return pl.pallas_call(
         second_back_kernel,
         grid=(length // ROW_BLOCK,),
-        in_specs=[full, full, full, full, whole(vec_all.shape), whole(out_w.shape)],
-        out_specs=[full, full, rows_of(ROW_BLOCK, cols), whole((8, width))],
+        in_specs=[full, full, full, full, whole(vec_all.shape), whole(out_w.shape)]
+        + [pl.BlockSpec((cols, ROW_BLOCK), lambda step: (0, step))],
+        out_specs=[full, rows_of(ROW_BLOCK, cols), whole((8, width)), whole((width, cols))],
         out_shape=[
             shaped((length, width), F32),
-            shaped((length, width), BF16),
             shaped((length, cols), BF16),
             shaped((8, width), F32),
-        ],
+            shaped((width, cols), BF16),
+        ],
+        scratch_shapes=[pltpu.VMEM((cols, width), F32)],
         compiler_params=PARAMS,
-        cost_estimate=cost(2 * length * width * cols, length * width * 20),
+        cost_estimate=cost(4 * length * width * cols, length * width * 20),
         name="second_back",
-    )(part, other, hidden, cot, vec_all, out_w)
-
-
-def qkv_grads_kernel(norm_ref, low_ref, grad_ref, heads_ref, out_ref, turned):
+    )(part, other, hidden, cot, vec_all, out_w, heads_turned)
+
+
+def qkv_grads_kernel(row_count, norm_ref, grad_ref, out_grad_ref, out_ref):
     part = pl.program_id(0)
-    cols = heads_ref.shape[1]
-    half = cols // 2
-
-    @pl.when(part == 0)
-    def _():
-        turned[...] = norm_ref[...].T
-
-    @pl.when(part == 3)
-    def _():
-        turned[...] = low_ref[...].T
-
+    half = grad_ref.shape[1] // 2
     for index in range(4):
 
         @pl.when(part == index)
         def _():
-            right = heads_ref if index == 3 else grad_ref
-            grads = dot_nn(turned[...], right[...]).astype(BF16)
+            if index == 3:
+                grads = out_grad_ref[...]
+            else:
+                grads = dot_nn(norm_ref[...], grad_ref[...]).astype(BF16)
+            lanes = slice(index * half, (index + 1) * half)
             for x in range(2):
-                out_ref[x, :, index * half : (index + 1) * half] = grads[:, x * half : (x + 1) * half]
-
-
-def qkv_grads(norm, low, grad_qkv, heads):
-    length, width = norm.shape
-    cols = heads.shape[1]
+                store_rows(grads[:, x * half : (x + 1) * half], out_ref, x, lanes, row_count)
+
+
+def qkv_grads(norm_turned, grad_qkv, out_grad, row_count):
+    width, length = norm_turned.shape
+    cols = out_grad.shape[1]
     return pl.pallas_call(
-        qkv_grads_kernel,
+        functools.partial(qkv_grads_kernel, row_count),
         grid=(4,),
         in_specs=[
-            whole((length, width)),
-            whole((length, width)),
+            whole((width, length)),
             pl.BlockSpec((length, cols), lambda part: (0, jnp.minimum(part, 2))),
-            whole((length, cols)),
+            whole((width, cols)),
         ],
         out_specs=whole((2, width, 2 * cols)),
         out_shape=shaped((2, width, 2 * cols), BF16),
-        scratch_shapes=[pltpu.VMEM((width, length), BF16)],
         compiler_params=PARAMS,
-        cost_estimate=cost(8 * length * width * cols, 4 * length * (2 * width + 2 * cols)),
+        cost_estimate=cost(6 * length * width * cols, 4 * length * (2 * width + 2 * cols)),
         name="qkv_grads",
-    )(norm, low, grad_qkv, heads)
-
-
-def first_back_kernel(grad_ref, weight_ref, tokens_ref, part_ref, sum_ref, bias_ref):
-    part = dot_nt(grad_ref[...], weight_ref[...])
+    )(norm_turned, grad_qkv, out_grad)
+
+
+def first_back_kernel(gathered, cols, grad_ref, tokens_ref, after_ref, *refs):
+    count = len(gathered.arrays)
+    part_ref, sum_ref, bias_ref, held, sems = refs[count:]
+    copies = weight_copies(gathered, refs[:count], held, sems)
+    third = cols // 3
+
+    @pl.when(pl.program_id(0) == 0)
+    def _():
+        start_all(copies[0] + copies[1])
+        sum_ref[...] = jnp.zeros_like(sum_ref)
+        bias_ref[...] = jnp.zeros_like(bias_ref)
+        wait_all(copies[0] + copies[1])
+
+    part = None
+    for x in range(2):
+        grads = jnp.concatenate(
+            [grad_ref[:, (2 * at + x) * third : (2 * at + x + 1) * third] for at in range(3)], axis=1
+        )
+        product = dot_nt(grads, held[x, :, :cols])
+        part = product if part is None else part + product
     part_ref[...] = part
     normed, _ = normalize_rows(tokens_ref[...].astype(F32))
-
-    @pl.when(pl.program_id(0) == 0)
-    def _():
-        sum_ref[...] = jnp.zeros_like(sum_ref)
-        bias_ref[...] = jnp.zeros_like(bias_ref)
-
     for row, value in enumerate((part * normed, part)):
         sum_ref[row : row + 1, :] += jnp.sum(value, axis=0, keepdims=True)
     bias_ref[0:1, :] += jnp.sum(grad_ref[...].astype(F32), axis=0, keepdims=True)
 
 
-def first_back(grad_qkv, weight, tokens):
+def first_back(grad_qkv, tokens, gathered, width_loc, after):
     length, width = tokens.shape
     cols = grad_qkv.shape[1]
     return pl.pallas_call(
-        first_back_kernel,
+        functools.partial(first_back_kernel, gathered, 3 * width_loc),
         grid=(length // ROW_BLOCK,),
-        in_specs=[rows_of(ROW_BLOCK, cols), whole(weight.shape), rows_of(ROW_BLOCK, width)],
+        in_specs=[rows_of(ROW_BLOCK, cols), rows_of(ROW_BLOCK, width), ANYWHERE]
+        + [ANYWHERE] * len(gathered.arrays),
         out_specs=[rows_of(ROW_BLOCK, width), whole((8, width)), whole((8, cols))],
         out_shape=[
             shaped((length, width), F32),
             shaped((8, width), F32),
             shaped((8, cols), F32),
         ],
+        scratch_shapes=weight_scratch(gathered),
         compiler_params=PARAMS,
         cost_estimate=cost(2 * length * width * cols, length * (6 * width + 2 * cols)),
         name="first_back",
-    )(grad_qkv, weight, tokens)
+    )(grad_qkv, tokens, after, *gathered.arrays)
 
 
 def token_back_kernel(core_ref, part_ref, other_ref, tokens_ref, grad_ref, vec_ref, out_ref):
@@ -668,16 +824,21 @@
     hidden_loc = w_up.shape[1]
     shard_rows = w_up.shape[0]
 
-    pad = -VEC_ROWS % 128
+    pad = -3 * width_loc % 128
     pack_qkv = jnp.concatenate(
         [w_qkv[:, part].astype(BF16) for part in range(3)]
-        + [w_out.T.astype(BF16), vectors.T.astype(BF16), jnp.zeros((shard_rows, pad), BF16)],
+        + [jnp.zeros((shard_rows, pad), BF16), w_out.T.astype(BF16)],
         axis=1,
     )
     pack_feed = jnp.concatenate([w_up.astype(BF16), w_down.T.astype(BF16)], axis=1)
 
     def both_halves(mine):
-        return gather_bit(mine, core_line, 0).reshape(-1, width)
+        other = swap_over(mine, core_line)
+        return jnp.where(
+            core == 0,
+            jnp.concatenate([mine, other], axis=0),
+            jnp.concatenate([other, mine], axis=0),
+        )
 
     def own_rows(value):
         return lax.dynamic_slice_in_dim(value, core * rows_loc, rows_loc, 0)
@@ -686,15 +847,16 @@
         return lax.dynamic_slice_in_dim(value, (1 - core) * rows_loc, rows_loc, 0)
 
     far_qkv = grid.gather_far(pack_qkv)
-    pack_feed, far_qkv = lax.optimization_barrier((pack_feed, far_qkv))
-    own_qkv, other_qkv = grid.gather_near(far_qkv, 4 * width_loc)
+    vec_blocks = gather_small(vectors.astype(BF16))
+    pack_feed, *far_qkv = lax.optimization_barrier((pack_feed, *far_qkv))
+    near_qkv = grid.gather_near(far_qkv)
     far_feed = grid.gather_far(pack_feed)
-    own_feed, other_feed = grid.gather_near(far_feed, 2 * hidden_loc)
+    *far_feed, _ = lax.optimization_barrier((*far_feed, near_qkv.arrays[-1]))
+    near_feed = grid.gather_near(far_feed)
 
     all_tokens = both_halves(tokens)
     all_cot = both_halves(cotangent)
-
-    vec_all = own_qkv[:, 4 * width_loc : 4 * width_loc + VEC_ROWS].T.astype(F32)
+    vec_all = jnp.swapaxes(vec_blocks, 0, 1).reshape(VEC_ROWS, width).astype(F32)
 
     def cat_blocks(vec_row, size):
         return jnp.concatenate(
@@ -704,22 +866,6 @@
             ]
         )
 
-    def joined(own, other, size, parts):
-        return jnp.concatenate(
-            [
-                block[:, part * size : (part + 1) * size]
-                for part in parts
-                for block in (own, other)
-            ],
-            axis=1,
-        )
-
-    full_qkv = joined(own_qkv, other_qkv, width_loc, range(3))
-    full_out = joined(own_qkv, other_qkv, width_loc, (3,))
-    full_up = joined(own_feed, other_feed, hidden_loc, (0,))
-    full_down = joined(own_feed, other_feed, hidden_loc, (1,))
-    partner_out = swap_over(full_out, core_line)
-
     bias_qkv = jnp.concatenate(
         [
             cat_blocks(vec_all[2], width_loc),
@@ -727,33 +873,40 @@
             cat_blocks(vec_all[3], width_loc),
         ]
     )
-    first_in, qkv = first_norm(all_tokens, vec_all, full_qkv, bias_qkv[None])
-    heads_low, lse = attend_forward(qkv)
+    bias_up = cat_blocks(vec_all[8:].reshape(-1), hidden_loc)
+    first_in, qkv, full_out = first_norm(
+        all_tokens, vec_all, bias_qkv[None], near_qkv, width_loc
+    )
+    partner_out = swap_over(full_out, core_line)
+    heads_low, heads_turned, lse = attend_forward(qkv)
     partner_heads = swap_over(heads_low, core_line)
-    hidden_state, second_in = attended_norm(
-        heads_low, partner_heads, full_out, partner_out, all_tokens, vec_all
-    )
-    bias_up = cat_blocks(vec_all[8:].reshape(-1), hidden_loc)
+    hidden_state, second_in, second_turned, first_turned, cot_turned = attended_norm(
+        heads_low, partner_heads, full_out, partner_out, all_tokens, vec_all, first_in, all_cot
+    )
     activated, grad_upper, grad_bias_up, down_part, second_part, second_low = feed(
-        second_in, all_cot, full_up, full_down, bias_up[None]
+        second_in, all_cot, bias_up[None], near_feed
     )
 
     second_other = swap_over(second_low, core_line)
-    pair_feed = feed_grads(all_cot, second_in, activated, grad_upper)
-    grad_hidden, grad_hidden_low, grad_heads, second_sums = second_back(
-        second_part, second_other, hidden_state, all_cot, vec_all, full_out
+    pair_feed = feed_grads(cot_turned, second_turned, activated, grad_upper, grid.row_count)
+    pair_feed = relative_rows(pair_feed, grid.row_count)
+    grad_hidden, grad_heads, second_sums, out_grad = second_back(
+        second_part, second_other, hidden_state, all_cot, vec_all, full_out, heads_turned
     )
     down_other = swap_over(partner_rows(down_part).astype(BF16), core_line).astype(F32)
     mixed_out = own_rows(hidden_state) + own_rows(down_part) + down_other + vec_all[7]
     grad_qkv_low = attend_backward(qkv, grad_heads, lse)
-    pair_qkv = qkv_grads(first_in, grad_hidden_low, grad_qkv_low, heads_low)
-    first_part, first_sums, bias_sums = first_back(grad_qkv_low, full_qkv, all_tokens)
+    pair_qkv = qkv_grads(first_turned, grad_qkv_low, out_grad, grid.row_count)
+    first_part, first_sums, bias_sums = first_back(
+        grad_qkv_low, all_tokens, near_qkv, width_loc, pair_qkv
+    )
+    pair_qkv = relative_rows(pair_qkv, grid.row_count)
     first_other = swap_over(partner_rows(first_part).astype(BF16), core_line)
     token_grad = token_back(core, first_part, first_other, tokens, grad_hidden, vec_all)
 
-    owned_feed = grid.reduce_all(pair_feed)
-    owned_down, owned_up = owned_feed[:, :hidden_loc], owned_feed[:, hidden_loc:]
-    owned_pack = grid.reduce_all(pair_qkv)
+    owned_feed = grid.reduce_far(grid.reduce_near(pair_feed, grad_qkv_low))
+    owned_up, owned_down = owned_feed[:, :hidden_loc], owned_feed[:, hidden_loc:]
+    owned_pack = grid.reduce_far(grid.reduce_near(pair_qkv))
     owned_qkv = jnp.stack(
         [owned_pack[:, part * width_loc : (part + 1) * width_loc] for part in range(3)], axis=1
     )

time: 336 us -> 313 us (0.932); the launches traced: 330 us -> 311 us
  local copies, waits for them, and re-layouts: 58.4 us -> 25.4 us
  Pallas kernels: 93.3 us -> 108 us
  starting transfers between devices: 42.2 us -> 50.4 us
  other arithmetic: 40 us -> 33.9 us
    pallas_call x5, Pallas kernels: 48.5 us -> 59.2 us  [the longest x1 24.1 us: feed(): pl.pallas_call(functools.partial(feed_kernel, gathered), grid=(hidden //...]
    concatenate x9 -> x7, other arithmetic: 15.3 us -> 5.71 us  [the longest x2 3.37 us: gather_near(): front = jnp.concatenate([front, swap_over(front, ('row', offset))], axis=0)]
    ppermute x36 -> x43, starting transfers between devices: 42.2 us -> 50.4 us  [swap_over(): return lax.ppermute(value, name, pairs)]
    dynamic_update_slice x10 -> x0, local copies, waits for them, and re-layouts: 7.77 us -> none  [gather_bit(): return lax.dynamic_update_slice_in_dim(both, other, 1 - place_on(line), dim)]
    broadcast_in_dim x11 -> x1, local copies, waits for them, and re-layouts: 7.24 us -> 0.01 us  [shards(): bias_qkv[None]]
    select_n x0 -> x5, other arithmetic: none -> 6.61 us  [the longest x2 6.57 us: both_halves(): jnp.where(core == 0, jnp.concatenate([mine, other], axis=0), jnp.concaten...]
    unnamed x5 -> x0, other arithmetic: 6.5 us -> none
    concatenate x3 -> x1, local copies, waits for them, and re-layouts: 5.93 us -> 0.12 us  [shards(): jnp.concatenate([w_qkv[:, part].astype(BF16) for part in range(3)] + [jnp...]
  transfers between devices with their start and end apart: 36 -> 43, of which waited for: 17 -> 17; matrix products, arithmetic and copies ran while one was open for 22% -> 13% of each run, Pallas kernels for 19% -> 22%
where the time goes in v3:
time: 313 us; the launch traced here: 311 us
  Pallas kernels  108 us (35%)
  waiting for transfers between devices  91.7 us (29%)
  starting transfers between devices  50.4 us (16%)
  other arithmetic  33.9 us (11%)
  local copies, waits for them, and re-layouts  25.4 us (8%)
    ppermute x43, waiting for transfers between devices, swap_over(): return lax.ppermute(value, name, pairs)  91.7 us
    ppermute x43, starting transfers between devices, swap_over(): return lax.ppermute(value, name, pairs)  50.4 us
    pallas_call x1, Pallas kernels, feed(): pl.pallas_call(functools.partial(feed_kernel, gathered), grid=(hidden //...  24.1 us
    pallas_call x1, Pallas kernels, attend_backward(): pl.pallas_call(attend_back_kernel, grid=(pairs,), in_specs=[lanes(0), lan...  15.7 us
    unnamed x100, local copies, waits for them, and re-layouts  13.7 us
    pallas_call x1, Pallas kernels, attend_forward(): pl.pallas_call(attend_kernel, grid=(pairs,), in_specs=[lanes(0), lanes(1)...  13 us
    pallas_call x1, Pallas kernels, first_norm(): pl.pallas_call(functools.partial(first_norm_kernel, gathered, cols), grid...  10.8 us
    pallas_call x1, Pallas kernels, first_back(): pl.pallas_call(functools.partial(first_back_kernel, gathered, 3 * width_l...  9.71 us
  transfers between devices with their start and end apart: 43, of which 17 were waited for; matrix products, arithmetic and copies ran while one was open for 13% of the time, Pallas kernels for 22%

profile of v3, /device:TPU:0, one launch (start us, length us, event | category | flops | bytes accessed | tf_op | source)
XLA Modules:
  0.0 310.9 jit_solution(1442221487906862941)
XLA Ops:
  1.4 3.0 collective-permute-start.1
  6.6 1.6 collective-permute-start.4
  8.2 2.6 collective-permute-start.5
  11.8 7.3 %collective-permute-done.2 = bf16[2,12,96]{2,1,0:T(8,128)(2,1)S(1)} collective-permute-done((bf16[2,12,96]{2,1,0:T(8,128)(2,1)S(1)}, bf16[2,12,96]{2,1,0:T(8,128)(2,1)S(1)}, u32[]{:S(2)}, u32[]{:S(2)}) %collective-permute-start.2) | collective-permute-done | bytes 4640 | tf_op jit(solution)/shard_map/ppermute | solution.py:58
  19.1 3.6 %collective-permute-start.3 = (bf16[4,12,96]{2,1,0:T(8,128)(2,1)S(1)}, bf16[4,12,96]{2,1,0:T(8,128)(2,1)S(1)}, u32[]{:S(2)}, u32[]{:S(2)}) collective-permute-start(bf16[4,12,96]{2,1,0:T(8,128)(2,1)S(1)} %pad_maximum_fusion.11), channel_id=1, source_target_pairs={{0,16},{4,20},{8,24},{12,28},{16,0},{20,4},{24,8},{28,12},{1,17},{... | collective-permute-start | bytes 27656 | tf_op jit(solution)/shard_map/ppermute | solution.py:58
  22.8 3.6 %collective-permute-done.3 = bf16[4,12,96]{2,1,0:T(8,128)(2,1)S(1)} collective-permute-done((bf16[4,12,96]{2,1,0:T(8,128)(2,1)S(1)}, bf16[4,12,96]{2,1,0:T(8,128)(2,1)S(1)}, u32[]{:S(2)}, u32[]{:S(2)}) %collective-permute-start.3) | collective-permute-done | bytes 9248 | tf_op jit(solution)/shard_map/ppermute | solution.py:58
  28.2 6.3 %collective-permute-done.9 = bf16[2,96,832]{2,1,0:T(8,128)(2,1)S(1)} collective-permute-done((bf16[2,96,832]{2,1,0:T(8,128)(2,1)S(1)}, bf16[2,96,832]{2,1,0:T(8,128)(2,1)S(1)}, u32[]{:S(2)}, u32[]{:S(2)}) %collective-permute-start.9) | collective-permute-done | bytes 319520 | tf_op jit(solution)/shard_map/ppermute | solution.py:58
  35.8 2.9 collective-permute-start.15
  40.6 4.9 %collective-permute-done.14 = bf16[96,1536]{1,0:T(8,128)(2,1)S(1)} collective-permute-done((bf16[96,1536]{1,0:T(8,128)(2,1)S(1)}, bf16[96,1536]{1,0:T(8,128)(2,1)S(1)}, u32[]{:S(2)}, u32[]{:S(2)}) %collective-permute-start.14) | collective-permute-done | bytes 294944 | tf_op jit(solution)/shard_map/ppermute | solution.py:58
  45.6 12.9 %collective-permute-done.15 = bf16[96,1536]{1,0:T(8,128)(2,1)S(1)} collective-permute-done((bf16[96,1536]{1,0:T(8,128)(2,1)S(1)}, bf16[96,1536]{1,0:T(8,128)(2,1)S(1)}, u32[]{:S(2)}, u32[]{:S(2)}) %collective-permute-start.15) | collective-permute-done | bytes 294944 | tf_op jit(solution)/shard_map/ppermute | solution.py:58
  64.8 3.9 %collective-permute-done.7 = bf16[2,96,832]{2,1,0:T(8,128)(2,1)} collective-permute-done((bf16[2,96,832]{2,1,0:T(8,128)(2,1)}, bf16[2,96,832]{2,1,0:T(8,128)(2,1)}, u32[]{:S(2)}, u32[]{:S(2)}) %collective-permute-start.7) | collective-permute-done | bytes 319520 | tf_op jit(solution)/shard_map/ppermute | solution.py:58
  69.8 3.1 %maximum_select_fusion.tokens_ref = bf16[1024,768]{1,0:T(8,128)(2,1)} fusion(bf16[512,768]{1,0:T(8,128)(2,1)} %collective-permute-done, bf16[512,768]{1,0:T(8,128)(2,1)S(1)} %copy-done.8, pred[]{:T(512)S(6)} %eq.18), kind=kLoop, calls=%fused_computation.3 | loop fusion | flops 7077888 | bytes 3145729 | tf_op jit(solution)/shard_map/jit(_where)/select_n | solution.py:837
  73.0 5.2 %collective-permute-done.19 = bf16[2,96,1536]{2,1,0:T(8,128)(2,1)} collective-permute-done((bf16[2,96,1536]{2,1,0:T(8,128)(2,1)}, bf16[2,96,1536]{2,1,0:T(8,128)(2,1)}, u32[]{:S(2)}, u32[]{:S(2)}) %collective-permute-start.19) | collective-permute-done | bytes 589856 | tf_op jit(solution)/shard_map/ppermute | solution.py:58
  78.2 2.2 pad_maximum_fusion.1.refs_2_
  81.3 2.3 pad_maximum_fusion.refs_0_
  84.7 8.1 %collective-permute-done.8.refs_1_ = bf16[4,96,832]{2,1,0:T(8,128)(2,1)S(1)} collective-permute-done((bf16[4,96,832]{2,1,0:T(8,128)(2,1)S(1)}, bf16[4,96,832]{2,1,0:T(8,128)(2,1)S(1)}, u32[]{:S(2)}, u32[]{:S(2)}) %collective-permute-start.8) | collective-permute-done | bytes 639008 | tf_op jit(solution)/shard_map/ppermute | solution.py:58
  92.9 10.8 %first_norm.1 = (bf16[1024,768]{1,0:T(8,128)(2,1)S(1)}, bf16[1024,1152]{1,0:T(8,128)(2,1)}, bf16[768,384]{1,0:T(8,128)(2,1)S(1)}) custom-call(bf16[1024,768]{1,0:T(8,128)(2,1)} %maximum_select_fusion.tokens_ref, f32[12,768]{1,0:T(8,128)S(1)} %convert_element_type.138.vec_ref, f32[1,1152]{1,0:T(1,128)S(1)} %broadcast_in_dim.20.bias_ref, ...), custom_call_target="tpu_custom_call" | custom-call | flops 1811939328 | bytes 4325376 | tf_op jit(solution)/shard_map/first_norm/pallas_call | solution.py:461
  103.7 2.2 copy-done
  105.9 13.0 %attend_forward.1 = (bf16[1024,384]{1,0:T(8,128)(2,1)}, bf16[384,1024]{1,0:T(8,128)(2,1)S(1)}, f32[3,8,1024]{2,1,0:T(8,128)S(1)}) custom-call(bf16[1024,1152]{1,0:T(8,128)(2,1)S(1)} %copy-done, bf16[1024,1152]{1,0:T(8,128)(2,1)S(1)} %copy-done, bf16[1024,1152]{1,0:T(8,128)(2,1)S(1)} %copy-done), custom_call_target="tpu_custom_call" | custom-call | flops 1610612736 | bytes 3145728 | tf_op jit(solution)/shard_map/attend_forward/pallas_call | solution.py:247
  121.2 3.4 %maximum_select_fusion.1.cot_ref = bf16[1024,768]{1,0:T(8,128)(2,1)} fusion(bf16[512,768]{1,0:T(8,128)(2,1)} %collective-permute-done.13, bf16[512,768]{1,0:T(8,128)(2,1)} %param.18, pred[]{:T(512)S(6)} %eq.18), kind=kLoop, calls=%fused_computation.4 | loop fusion | flops 7077888 | bytes 3145729 | tf_op jit(solution)/shard_map/jit(_where)/select_n | solution.py:837
  124.6 7.9 %attended_norm.1 = (f32[1024,768]{1,0:T(8,128)}, bf16[1024,768]{1,0:T(8,128)(2,1)S(1)}, bf16[768,1024]{1,0:T(8,128)(2,1)S(1)}, bf16[768,1024]{1,0:T(8,128)(2,1)}, bf16[768,1024]{1,0:T(8,128)(2,1)}) custom-call(bf16[1024,384]{1,0:T(8,128)(2,1)} %get-tuple-element.57.heads_ref, bf16[1024,384]{1,0:T(8,128)(2,1)} %collective-permute-done.11.partner_ref, ...), custom_call_target="tpu_custom_call" | custom-call | flops 1207959552 | bytes 15728640 | tf_op jit(solution)/shard_map/attended_norm/pallas_call | solution.py:503
  133.6 24.1 %feed.1 = (bf16[1024,1536]{1,0:T(8,128)(2,1)}, bf16[1024,1536]{1,0:T(8,128)(2,1)}, f32[1,1536]{1,0:T(1,128)S(1)}, f32[1024,768]{1,0:T(8,128)}, f32[1024,768]{1,0:T(8,128)}, /*index=5*/bf16[1024,768]{1,0:T(8,128)(2,1)}) custom-call(bf16[1024,768]{1,0:T(8,128)(2,1)} %copy-done.16, bf16[1024,768]{1,0:T(8,128)(2,1)} %maximum_select_fusion.1.cot_ref, ...), custom_call_target="tpu_custom_call" | custom-call | flops 9663676416 | bytes 9437184 | tf_op jit(solution)/shard_map/feed/pallas_call | solution.py:580
  157.8 2.5 dynamic-slice_convert_fusion.1
  160.7 9.1 %feed_grads.1 = bf16[2,768,1536]{2,1,0:T(8,128)(2,1)} custom-call(bf16[768,1024]{1,0:T(8,128)(2,1)S(1)} %copy-done.15, bf16[768,1024]{1,0:T(8,128)(2,1)S(1)} %get-tuple-element.78.norm_ref, bf16[1024,1536]{1,0:T(8,128)(2,1)} %get-tuple-element.79.act_ref, bf16[1024,1536]{1,0:T(8,128)(2,1)} %get-tuple-element.80.gup_ref), custom_call_target="tpu_custom_call" | custom-call | flops 4831838208 | bytes 9437184 | tf_op jit(solution)/shard_map/feed_grads/pallas_call | solution.py:618
  169.7 1.8 slice_bitcast_fusion
  172.8 2.4 slice_bitcast_fusion.2
  181.2 3.7 %add_add_fusion = f32[512,768]{1,0:T(8,128)} fusion(bf16[512,768]{1,0:T(8,128)(2,1)} %collective-permute-done.21, f32[1024,768]{1,0:T(8,128)} %get-tuple-element.67, s32[]{:T(128)S(6)} %select_n.111, f32[1024,768]{1,0:T(8,128)} %get-tuple-element.60.hidden_ref, f32[768]{0:T(1024)S(1)} %add.207), kind=kLoop, calls=%fused_computation.6 | loop fusion | flops 1572864 | bytes 5508100 | tf_op jit(solution)/shard_map/add | solution.py:897
  184.8 8.9 %second_back.1 = (f32[1024,768]{1,0:T(8,128)}, bf16[1024,384]{1,0:T(8,128)(2,1)S(1)}, f32[8,768]{1,0:T(8,128)S(1)}, bf16[768,384]{1,0:T(8,128)(2,1)S(1)}) custom-call(f32[1024,768]{1,0:T(8,128)} %get-tuple-element.68.part_ref, bf16[1024,768]{1,0:T(8,128)(2,1)} %collective-permute-done.22.other_ref, f32[1024,768]{1,0:T(8,128)} %get-tuple-element.60.hidden_ref, ...), custom_call_target="tpu_custom_call" | custom-call | flops 1207959552 | bytes 15728640 | tf_op jit(solution)/shard_map/second_back/pallas_call | solution.py:667
  193.8 15.7 %attend_backward.1.grad_ref = bf16[1024,1152]{1,0:T(8,128)(2,1)S(1)} custom-call(bf16[1024,1152]{1,0:T(8,128)(2,1)S(1)} %copy-done.1, bf16[1024,1152]{1,0:T(8,128)(2,1)S(1)} %copy-done.1, bf16[1024,1152]{1,0:T(8,128)(2,1)S(1)} %copy-done.1, bf16[1024,384]{1,0:T(8,128)(2,1)S(1)} %get-tuple-element.71.go_ref, f32[3,8,1024]{2,1,0:T(8,128)S(1)} %copy-done.18), custom_call_target="tpu_custom_call" | custom-call | flops 4026531840 | bytes 5505024 | tf_op jit(solution)/shard_map/attend_backward/pallas_call | solution.py:329
  209.6 3.4 %convert_add_fusion.1 = bf16[2,2,1,96,1536]{4,3,2,1,0:T(8,128)(2,1)} fusion(bf16[2,2,1,96,1536]{4,3,2,1,0:T(8,128)(2,1)} %collective-permute-done.32, bf16[2,2,2,96,1536]{4,3,2,1,0:T(8,128)(2,1)S(1)} %copy-done.20), kind=kLoop, calls=%fused_computation.2 | loop fusion | flops 2359296 | bytes 3538944 | tf_op jit(solution)/shard_map/add | solution.py:152
  213.0 3.1 %fusion.21 = f32[2,2,1,96,1536]{4,3,1,2,0:T(8,128)} fusion(bf16[2,2,1,96,1536]{4,3,2,1,0:T(8,128)(2,1)} %collective-permute-done.32, bf16[2,2,2,96,1536]{4,3,2,1,0:T(8,128)(2,1)S(1)} %copy-done.20), kind=kLoop, calls=%fused_computation.105 | loop fusion | flops 1769472 | bytes 4718592 | tf_op jit(solution)/shard_map/add | solution.py:152
  216.1 5.5 %qkv_grads.1.after_ref = bf16[2,768,768]{2,1,0:T(8,128)(2,1)S(1)} custom-call(bf16[768,1024]{1,0:T(8,128)(2,1)S(1)} %copy-done.10, bf16[1024,1152]{1,0:T(8,128)(2,1)} %copy-done.6, bf16[768,384]{1,0:T(8,128)(2,1)S(1)} %get-tuple-element.74.out_grad_ref), custom_call_target="tpu_custom_call" | custom-call | flops 1811939328 | bytes 9437184 | tf_op jit(solution)/shard_map/qkv_grads/pallas_call | solution.py:705
  223.1 9.7 %first_back.1 = (f32[1024,768]{1,0:T(8,128)}, f32[8,768]{1,0:T(8,128)S(1)}, f32[8,1152]{1,0:T(8,128)S(1)}) custom-call(bf16[1024,1152]{1,0:T(8,128)(2,1)} %copy-done.6, bf16[1024,768]{1,0:T(8,128)(2,1)S(1)} %copy-done.4, bf16[2,768,768]{2,1,0:T(8,128)(2,1)} %copy-done.2, bf16[4,96,832]{2,1,0:T(8,128)(2,1)S(1)} %pad_maximum_fusion.2.refs_0_, ...), custom_call_target="tpu_custom_call" | custom-call | flops 1811939328 | bytes 7077888 | tf_op jit(solution)/shard_map/first_back/pallas_call | solution.py:751
  237.0 2.0 convert_add_fusion
  239.0 12.7 %collective-permute-done.39 = f32[12,768]{1,0:T(8,128)S(1)} collective-permute-done((f32[12,768]{1,0:T(8,128)S(1)}, f32[12,768]{1,0:T(8,128)S(1)}, u32[]{:S(2)}, u32[]{:S(2)}) %collective-permute-start.39) | collective-permute-done | bytes 36896 | tf_op jit(solution)/shard_map/ppermute | solution.py:58
  253.3 2.5 collective-permute-done.40
  255.8 3.3 %collective-permute-start.41 = (f32[12,768]{1,0:T(8,128)S(1)}, f32[12,768]{1,0:T(8,128)S(1)}, u32[]{:S(2)}, u32[]{:S(2)}) collective-permute-start(f32[12,768]{1,0:T(8,128)S(1)} %add.246), channel_id=1, source_target_pairs={{0,8},{4,12},{8,0},{12,4},{16,24},{20,28},{24,16},{28,20},{1,9},{5... | collective-permute-start | bytes 110600 | tf_op jit(solution)/shard_map/ppermute | solution.py:58
  262.0 2.8 collective-permute-start.42
  264.9 2.2 collective-permute-done.42
  268.0 2.8 collective-permute-start.36
  270.7 4.9 %collective-permute-done.33 = bf16[2,1,96,1536]{3,2,1,0:T(8,128)(2,1)S(1)} collective-permute-done((bf16[2,1,96,1536]{3,2,1,0:T(8,128)(2,1)S(1)}, bf16[2,1,96,1536]{3,2,1,0:T(8,128)(2,1)S(1)}, u32[]{:S(2)}, u32[]{:S(2)}) %collective-permute-start.33) | collective-permute-done | bytes 589856 | tf_op jit(solution)/shard_map/ppermute | solution.py:58
  275.6 2.7 collective-permute-start.37
  278.5 7.0 %collective-permute-done.27 = bf16[2,2,1,96,768]{4,3,2,1,0:T(8,128)(2,1)S(1)} collective-permute-done((bf16[2,2,1,96,768]{4,3,2,1,0:T(8,128)(2,1)S(1)}, bf16[2,2,1,96,768]{4,3,2,1,0:T(8,128)(2,1)S(1)}, u32[]{:S(2)}, u32[]{:S(2)}) %collective-permute-start.27) | collective-permute-done | bytes 589856 | tf_op jit(solution)/shard_map/ppermute | solution.py:58
  287.5 3.1 token_back.1
  290.6 2.2 collective-permute-done.28
  292.8 3.0 collective-permute-start.29
  297.4 1.6 collective-permute-done.34
  301.3 5.9 %collective-permute-done.29 = bf16[96,768]{1,0:T(8,128)(2,1)S(1)} collective-permute-done((bf16[96,768]{1,0:T(8,128)(2,1)S(1)}, bf16[96,768]{1,0:T(8,128)(2,1)S(1)}, u32[]{:S(2)}, u32[]{:S(2)}) %collective-permute-start.29) | collective-permute-done | bytes 147488 | tf_op jit(solution)/shard_map/ppermute | solution.py:58
  (246 shorter events, 49.7 us)
Async XLA Ops:
  1.4 9.6 %collective-permute-start.1 = (bf16[1,12,96]{2,1,0:T(8,128)(2,1)S(1)}, bf16[1,12,96]{2,1,0:T(8,128)(2,1)S(1)}, u32[]{:S(2)}, u32[]{:S(2)}) collective-permute-start(bf16[1,12,96]{2,1,0:T(8,128)(2,1)S(1)} %convert_bitcast_fusion.3), channel_id=1, source_target_pairs={{0,4},{4,0},{8,12},{12,8},{16,20},{20,16},{24,28},{28,24},{1,5},{5... | collective-permute-start | bytes 6920 | tf_op jit(solution)/shard_map/ppermute | solution.py:58
  6.4 21.8 %copy-start.33 = (f32[192,96]{0,1:T(8,128)}, f32[192,96]{0,1:T(8,128)S(1)}, u32[]{:S(2)}) copy-start(f32[192,96]{0,1:T(8,128)S(1)} %copy.50) | copy-start | bytes 221188
  6.6 19.9 %collective-permute-start.4 = (bf16[96,832]{1,0:T(8,128)(2,1)S(1)}, bf16[96,832]{1,0:T(8,128)(2,1)S(1)}, u32[]{:S(2)}, u32[]{:S(2)}) collective-permute-start(bf16[96,832]{1,0:T(8,128)(2,1)S(1)} %concatenate.66), channel_id=1, source_target_pairs={{0,8},{4,12},{8,0},{12,4},{16,24},{20,28},{24,16},{28,20},{1,9},{5... | collective-permute-start | bytes 479240 | tf_op jit(solution)/shard_map/ppermute | solution.py:58
  8.2 18.3 %collective-permute-start.5 = (bf16[96,832]{1,0:T(8,128)(2,1)S(1)}, bf16[96,832]{1,0:T(8,128)(2,1)S(1)}, u32[]{:S(2)}, u32[]{:S(2)}) collective-permute-start(bf16[96,832]{1,0:T(8,128)(2,1)S(1)} %concatenate.66), channel_id=1, source_target_pairs={{0,16},{4,20},{8,24},{12,28},{16,0},{20,4},{24,8},{28,12},{1,17},{... | collective-permute-start | bytes 479240 | tf_op jit(solution)/shard_map/ppermute | solution.py:58
  10.8 15.7 %collective-permute-start.6 = (bf16[96,832]{1,0:T(8,128)(2,1)S(1)}, bf16[96,832]{1,0:T(8,128)(2,1)S(1)}, u32[]{:S(2)}, u32[]{:S(2)}) collective-permute-start(bf16[96,832]{1,0:T(8,128)(2,1)S(1)} %concatenate.66), channel_id=1, source_target_pairs={{0,24},{4,28},{8,16},{12,20},{16,8},{20,12},{24,0},{28,4},{1,25},{... | collective-permute-start | bytes 479240 | tf_op jit(solution)/shard_map/ppermute | solution.py:58
  11.0 58.8 %collective-permute-start = (bf16[512,768]{1,0:T(8,128)(2,1)}, bf16[512,768]{1,0:T(8,128)(2,1)}, u32[]{:S(2)}, u32[]{:S(2)}) collective-permute-start(bf16[512,768]{1,0:T(8,128)(2,1)} %tokens_ref.1), channel_id=1, source_target_pairs={{0,1},{1,0},{2,3},{3,2},{4,5},{5,4},{6,7},{7,6},{8,9},{9,8},{10,11... | collective-permute-start | bytes 2359304 | tf_op jit(solution)/shard_map/ppermute | solution.py:58
  11.0 8.1 %collective-permute-start.2 = (bf16[2,12,96]{2,1,0:T(8,128)(2,1)S(1)}, bf16[2,12,96]{2,1,0:T(8,128)(2,1)S(1)}, u32[]{:S(2)}, u32[]{:S(2)}) collective-permute-start(bf16[2,12,96]{2,1,0:T(8,128)(2,1)S(1)} %pad_maximum_fusion.12), channel_id=1, source_target_pairs={{0,8},{4,12},{8,0},{12,4},{16,24},{20,28},{24,16},{28,20},{1,9},{5... | collective-permute-start | bytes 13832 | tf_op jit(solution)/shard_map/ppermute | solution.py:58
  19.1 7.4 %collective-permute-start.3 = (bf16[4,12,96]{2,1,0:T(8,128)(2,1)S(1)}, bf16[4,12,96]{2,1,0:T(8,128)(2,1)S(1)}, u32[]{:S(2)}, u32[]{:S(2)}) collective-permute-start(bf16[4,12,96]{2,1,0:T(8,128)(2,1)S(1)} %pad_maximum_fusion.11), channel_id=1, source_target_pairs={{0,16},{4,20},{8,24},{12,28},{16,0},{20,4},{24,8},{28,12},{1,17},{... | collective-permute-start | bytes 27656 | tf_op jit(solution)/shard_map/ppermute | solution.py:58
  26.6 8.0 %collective-permute-start.9 = (bf16[2,96,832]{2,1,0:T(8,128)(2,1)S(1)}, bf16[2,96,832]{2,1,0:T(8,128)(2,1)S(1)}, u32[]{:S(2)}, u32[]{:S(2)}) collective-permute-start(bf16[2,96,832]{2,1,0:T(8,128)(2,1)S(1)} %pad_maximum_fusion.7), channel_id=1, source_target_pairs={{0,2},{1,3},{2,0},{3,1},{4,6},{5,7},{6,4},{7,5},{8,10},{9,11},{10,... | collective-permute-start | bytes 958472 | tf_op jit(solution)/shard_map/ppermute | solution.py:58
  34.6 25.4 %collective-permute-start.10 = (bf16[4,96,832]{2,1,0:T(8,128)(2,1)S(1)}, bf16[4,96,832]{2,1,0:T(8,128)(2,1)S(1)}, u32[]{:S(2)}, u32[]{:S(2)}) collective-permute-start(bf16[4,96,832]{2,1,0:T(8,128)(2,1)S(1)} %pad_maximum_fusion.3.refs_2_), channel_id=1, source_target_pairs={{0,4},{4,0},{8,12},{12,8},{16,20},{20,16},{24,28},{28,24},{1,5},{5... | collective-permute-start | bytes 1916936 | tf_op jit(solution)/shard_map/ppermute | solution.py:58
  35.2 29.4 %copy-start.37 = (f32[12,8,96]{2,1,0:T(8,128)}, f32[12,8,96]{2,1,0:T(8,128)S(1)}, u32[]{:S(2)}) copy-start(f32[12,8,96]{2,1,0:T(8,128)S(1)} %convert_bitcast_fusion.1) | copy-start | bytes 110596
  35.2 10.3 %collective-permute-start.14 = (bf16[96,1536]{1,0:T(8,128)(2,1)S(1)}, bf16[96,1536]{1,0:T(8,128)(2,1)S(1)}, u32[]{:S(2)}, u32[]{:S(2)}) collective-permute-start(bf16[96,1536]{1,0:T(8,128)(2,1)S(1)} %pad_maximum_fusion.8), channel_id=1, source_target_pairs={{0,8},{4,12},{8,0},{12,4},{16,24},{20,28},{24,16},{28,20},{1,9},{5... | collective-permute-start | bytes 884744 | tf_op jit(solution)/shard_map/ppermute | solution.py:58
  35.8 22.7 %collective-permute-start.15 = (bf16[96,1536]{1,0:T(8,128)(2,1)S(1)}, bf16[96,1536]{1,0:T(8,128)(2,1)S(1)}, u32[]{:S(2)}, u32[]{:S(2)}) collective-permute-start(bf16[96,1536]{1,0:T(8,128)(2,1)S(1)} %pad_maximum_fusion.8), channel_id=1, source_target_pairs={{0,16},{4,20},{8,24},{12,28},{16,0},{20,4},{24,8},{28,12},{1,17},{... | collective-permute-start | bytes 884744 | tf_op jit(solution)/shard_map/ppermute | solution.py:58
  38.7 21.3 %collective-permute-start.16 = (bf16[96,1536]{1,0:T(8,128)(2,1)S(1)}, bf16[96,1536]{1,0:T(8,128)(2,1)S(1)}, u32[]{:S(2)}, u32[]{:S(2)}) collective-permute-start(bf16[96,1536]{1,0:T(8,128)(2,1)S(1)} %pad_maximum_fusion.8), channel_id=1, source_target_pairs={{0,24},{4,28},{8,16},{12,20},{16,8},{20,12},{24,0},{28,4},{1,25},{... | collective-permute-start | bytes 884744 | tf_op jit(solution)/shard_map/ppermute | solution.py:58
  45.6 19.2 %copy-start.22 = (bf16[96,1536]{1,0:T(8,128)(2,1)}, bf16[96,1536]{1,0:T(8,128)(2,1)S(1)}, u32[]{:S(2)}) copy-start(bf16[96,1536]{1,0:T(8,128)(2,1)S(1)} %collective-permute-done.14) | copy-start | bytes 884740
  45.6 75.6 %collective-permute-start.13 = (bf16[512,768]{1,0:T(8,128)(2,1)}, bf16[512,768]{1,0:T(8,128)(2,1)}, u32[]{:S(2)}, u32[]{:S(2)}) collective-permute-start(bf16[512,768]{1,0:T(8,128)(2,1)} %param.18), channel_id=1, source_target_pairs={{0,1},{1,0},{2,3},{3,2},{4,5},{5,4},{6,7},{7,6},{8,9},{9,8},{10,11... | collective-permute-start | bytes 2359304 | tf_op jit(solution)/shard_map/ppermute | solution.py:58
  58.5 10.1 %collective-permute-start.7 = (bf16[2,96,832]{2,1,0:T(8,128)(2,1)}, bf16[2,96,832]{2,1,0:T(8,128)(2,1)}, u32[]{:S(2)}, u32[]{:S(2)}) collective-permute-start(bf16[2,96,832]{2,1,0:T(8,128)(2,1)} %pad_maximum_fusion.6), channel_id=1, source_target_pairs={{0,4},{4,0},{8,12},{12,8},{16,20},{20,16},{24,28},{28,24},{1,5},{5... | collective-permute-start | bytes 958472 | tf_op jit(solution)/shard_map/ppermute | solution.py:58
  61.6 16.6 %collective-permute-start.19 = (bf16[2,96,1536]{2,1,0:T(8,128)(2,1)}, bf16[2,96,1536]{2,1,0:T(8,128)(2,1)}, u32[]{:S(2)}, u32[]{:S(2)}) collective-permute-start(bf16[2,96,1536]{2,1,0:T(8,128)(2,1)} %pad_maximum_fusion.5), channel_id=1, source_target_pairs={{0,2},{1,3},{2,0},{3,1},{4,6},{5,7},{6,4},{7,5},{8,10},{9,11},{10,... | collective-permute-start | bytes 1769480 | tf_op jit(solution)/shard_map/ppermute | solution.py:58
  64.0 17.3 %collective-permute-start.17 = (bf16[2,96,1536]{2,1,0:T(8,128)(2,1)}, bf16[2,96,1536]{2,1,0:T(8,128)(2,1)}, u32[]{:S(2)}, u32[]{:S(2)}) collective-permute-start(bf16[2,96,1536]{2,1,0:T(8,128)(2,1)} %pad_maximum_fusion.4), channel_id=1, source_target_pairs={{0,4},{4,0},{8,12},{12,8},{16,20},{20,16},{24,28},{28,24},{1,5},{5... | collective-permute-start | bytes 1769480 | tf_op jit(solution)/shard_map/ppermute | solution.py:58
  69.7 23.1 %collective-permute-start.8 = (bf16[4,96,832]{2,1,0:T(8,128)(2,1)S(1)}, bf16[4,96,832]{2,1,0:T(8,128)(2,1)S(1)}, u32[]{:S(2)}, u32[]{:S(2)}) collective-permute-start(bf16[4,96,832]{2,1,0:T(8,128)(2,1)S(1)} %pad_maximum_fusion.2.refs_0_), channel_id=1, source_target_pairs={{0,2},{1,3},{2,0},{3,1},{4,6},{5,7},{6,4},{7,5},{8,10},{9,11},{10,... | collective-permute-start | bytes 1916936 | tf_op jit(solution)/shard_map/ppermute | solution.py:58
  80.4 53.2 %collective-permute-start.20 = (bf16[4,96,1536]{2,1,0:T(8,128)(2,1)}, bf16[4,96,1536]{2,1,0:T(8,128)(2,1)}, u32[]{:S(2)}, u32[]{:S(2)}) collective-permute-start(bf16[4,96,1536]{2,1,0:T(8,128)(2,1)} %pad_maximum_fusion.1.refs_2_), channel_id=1, source_target_pairs={{0,4},{4,0},{8,12},{12,8},{16,20},{20,16},{24,28},{28,24},{1,5},{5... | collective-permute-start | bytes 3538952 | tf_op jit(solution)/shard_map/ppermute | solution.py:58
  83.6 50.1 %collective-permute-start.18 = (bf16[4,96,1536]{2,1,0:T(8,128)(2,1)}, bf16[4,96,1536]{2,1,0:T(8,128)(2,1)}, u32[]{:S(2)}, u32[]{:S(2)}) collective-permute-start(bf16[4,96,1536]{2,1,0:T(8,128)(2,1)} %pad_maximum_fusion.refs_0_), channel_id=1, source_target_pairs={{0,2},{1,3},{2,0},{3,1},{4,6},{5,7},{6,4},{7,5},{8,10},{9,11},{10,... | collective-permute-start | bytes 3538952 | tf_op jit(solution)/shard_map/ppermute | solution.py:58
  120.5 4.1 %collective-permute-start.11 = (bf16[1024,384]{1,0:T(8,128)(2,1)}, bf16[1024,384]{1,0:T(8,128)(2,1)}, u32[]{:S(2)}, u32[]{:S(2)}) collective-permute-start(bf16[1024,384]{1,0:T(8,128)(2,1)} %get-tuple-element.57.heads_ref), channel_id=1, source_target_pairs={{0,1},{1,0},{2,3},{3,2},{4,5},{5,4},{6,7},{7,6},{8,9},{9,8},{10,11... | collective-permute-start | bytes 2359304 | tf_op jit(solution)/shard_map/ppermute | solution.py:58
  120.5 4.1 %collective-permute-start.12 = (bf16[768,384]{1,0:T(8,128)(2,1)S(1)}, bf16[768,384]{1,0:T(8,128)(2,1)}, u32[]{:S(2)}, u32[]{:S(2)}) collective-permute-start(bf16[768,384]{1,0:T(8,128)(2,1)S(1)} %get-tuple-element.58.own_ref.out_w_ref), channel_id=1, source_target_pairs={{0,1},{1,0},{2,3},{3,2},{4,5},{5,4},{6,7},{7,6},{8,9},{9,8},{10,11... | collective-permute-start | bytes 1769480 | tf_op jit(solution)/shard_map/ppermute | solution.py:58
  157.7 27.1 %collective-permute-start.22 = (bf16[1024,768]{1,0:T(8,128)(2,1)}, bf16[1024,768]{1,0:T(8,128)(2,1)}, u32[]{:S(2)}, u32[]{:S(2)}) collective-permute-start(bf16[1024,768]{1,0:T(8,128)(2,1)} %get-tuple-element.69), channel_id=1, source_target_pairs={{0,1},{1,0},{2,3},{3,2},{4,5},{5,4},{6,7},{7,6},{8,9},{9,8},{10,11... | collective-permute-start | bytes 4718600 | tf_op jit(solution)/shard_map/ppermute | solution.py:58
  160.3 20.8 %collective-permute-start.21 = (bf16[512,768]{1,0:T(8,128)(2,1)}, bf16[512,768]{1,0:T(8,128)(2,1)}, u32[]{:S(2)}, u32[]{:S(2)}) collective-permute-start(bf16[512,768]{1,0:T(8,128)(2,1)} %dynamic-slice_convert_fusion.1), channel_id=1, source_target_pairs={{0,1},{1,0},{2,3},{3,2},{4,5},{5,4},{6,7},{7,6},{8,9},{9,8},{10,11... | collective-permute-start | bytes 2359304 | tf_op jit(solution)/shard_map/ppermute | solution.py:58
  175.2 34.4 %collective-permute-start.32 = (bf16[2,2,1,96,1536]{4,3,2,1,0:T(8,128)(2,1)}, bf16[2,2,1,96,1536]{4,3,2,1,0:T(8,128)(2,1)}, u32[]{:S(2)}, u32[]{:S(2)}) collective-permute-start(bf16[2,2,1,96,1536]{4,3,2,1,0:T(8,128)(2,1)} %slice.286), channel_id=1, source_target_pairs={{0,4},{4,0},{8,12},{12,8},{16,20},{20,16},{24,28},{28,24},{1,5},{5... | collective-permute-start | bytes 3538952 | tf_op jit(solution)/shard_map/ppermute | solution.py:58
  175.7 33.9 %collective-permute-start.31 = (bf16[2,2,96,1536]{3,2,1,0:T(8,128)(2,1)}, bf16[2,2,96,1536]{3,2,1,0:T(8,128)(2,1)}, u32[]{:S(2)}, u32[]{:S(2)}) collective-permute-start(bf16[2,2,96,1536]{3,2,1,0:T(8,128)(2,1)} %slice_bitcast_fusion.2), channel_id=1, source_target_pairs={{0,2},{1,3},{2,0},{3,1},{4,6},{5,7},{6,4},{7,5},{8,10},{9,11},{10,... | collective-permute-start | bytes 3538952 | tf_op jit(solution)/shard_map/ppermute | solution.py:58
  193.8 15.7 %copy-start.20 = (bf16[2,2,2,96,1536]{4,3,2,1,0:T(8,128)(2,1)S(1)}, bf16[2,2,2,96,1536]{4,3,2,1,0:T(8,128)(2,1)}, u32[]{:S(2)}) copy-start(bf16[2,2,2,96,1536]{4,3,2,1,0:T(8,128)(2,1)} %copy-done.19) | copy-start | bytes 7077892
  233.6 1.8 collective-permute-start.38
  234.8 33.0 %collective-permute-start.35 = (bf16[2,1,96,1536]{3,2,0,1:T(8,128)(2,1)S(1)}, bf16[2,1,96,1536]{3,2,0,1:T(8,128)(2,1)S(1)}, u32[]{:S(2)}, u32[]{:S(2)}) collective-permute-start(bf16[2,1,96,1536]{3,2,0,1:T(8,128)(2,1)S(1)} %fusion.3), channel_id=1, source_target_pairs={{0,2},{1,3},{2,0},{3,1},{4,6},{5,7},{6,4},{7,5},{8,10},{9,11},{10,... | collective-permute-start | bytes 1769480 | tf_op jit(solution)/shard_map/ppermute | solution.py:58
  235.4 17.8 %copy-start.3 = (bf16[2,768,768]{2,1,0:T(8,128)(2,1)S(1)}, bf16[2,768,768]{2,1,0:T(8,128)(2,1)}, u32[]{:S(2)}) copy-start(bf16[2,768,768]{2,1,0:T(8,128)(2,1)} %copy-done.2) | copy-start | bytes 7077892
  235.5 16.2 %collective-permute-start.39 = (f32[12,768]{1,0:T(8,128)S(1)}, f32[12,768]{1,0:T(8,128)S(1)}, u32[]{:S(2)}, u32[]{:S(2)}) collective-permute-start(f32[12,768]{1,0:T(8,128)S(1)} %add.244), channel_id=1, source_target_pairs={{0,2},{1,3},{2,0},{3,1},{4,6},{5,7},{6,4},{7,5},{8,10},{9,11},{10,... | collective-permute-start | bytes 110600 | tf_op jit(solution)/shard_map/ppermute | solution.py:58
  251.7 4.2 %collective-permute-start.40 = (f32[12,768]{1,0:T(8,128)S(1)}, f32[12,768]{1,0:T(8,128)S(1)}, u32[]{:S(2)}, u32[]{:S(2)}) collective-permute-start(f32[12,768]{1,0:T(8,128)S(1)} %add.245), channel_id=1, source_target_pairs={{0,4},{4,0},{8,12},{12,8},{16,20},{20,16},{24,28},{28,24},{1,5},{5... | collective-permute-start | bytes 110600 | tf_op jit(solution)/shard_map/ppermute | solution.py:58
  255.8 6.2 %collective-permute-start.41 = (f32[12,768]{1,0:T(8,128)S(1)}, f32[12,768]{1,0:T(8,128)S(1)}, u32[]{:S(2)}, u32[]{:S(2)}) collective-permute-start(f32[12,768]{1,0:T(8,128)S(1)} %add.246), channel_id=1, source_target_pairs={{0,8},{4,12},{8,0},{12,4},{16,24},{20,28},{24,16},{28,20},{1,9},{5... | collective-permute-start | bytes 110600 | tf_op jit(solution)/shard_map/ppermute | solution.py:58
  259.3 16.3 %collective-permute-start.33 = (bf16[2,1,96,1536]{3,2,1,0:T(8,128)(2,1)S(1)}, bf16[2,1,96,1536]{3,2,1,0:T(8,128)(2,1)S(1)}, u32[]{:S(2)}, u32[]{:S(2)}) collective-permute-start(bf16[2,1,96,1536]{3,2,1,0:T(8,128)(2,1)S(1)} %slice.388), channel_id=1, source_target_pairs={{0,4},{4,0},{8,12},{12,8},{16,20},{20,16},{24,28},{28,24},{1,5},{5... | collective-permute-start | bytes 1769480 | tf_op jit(solution)/shard_map/ppermute | solution.py:58
  259.9 25.6 %collective-permute-start.27 = (bf16[2,2,1,96,768]{4,3,2,1,0:T(8,128)(2,1)S(1)}, bf16[2,2,1,96,768]{4,3,2,1,0:T(8,128)(2,1)S(1)}, u32[]{:S(2)}, u32[]{:S(2)}) collective-permute-start(bf16[2,2,1,96,768]{4,3,2,1,0:T(8,128)(2,1)S(1)} %slice.274), channel_id=1, source_target_pairs={{0,4},{4,0},{8,12},{12,8},{16,20},{20,16},{24,28},{28,24},{1,5},{5... | collective-permute-start | bytes 1769480 | tf_op jit(solution)/shard_map/ppermute | solution.py:58
  261.5 24.5 %collective-permute-start.24 = (bf16[2,2,96,768]{3,2,1,0:T(8,128)(2,1)S(1)}, bf16[2,2,96,768]{3,2,1,0:T(8,128)(2,1)S(1)}, u32[]{:S(2)}, u32[]{:S(2)}) collective-permute-start(bf16[2,2,96,768]{3,2,1,0:T(8,128)(2,1)S(1)} %slice_bitcast_fusion.7), channel_id=1, source_target_pairs={{0,2},{1,3},{2,0},{3,1},{4,6},{5,7},{6,4},{7,5},{8,10},{9,11},{10,... | collective-permute-start | bytes 1769480 | tf_op jit(solution)/shard_map/ppermute | solution.py:58
  262.0 5.1 %collective-permute-start.42 = (f32[12,768]{1,0:T(8,128)S(1)}, f32[12,768]{1,0:T(8,128)S(1)}, u32[]{:S(2)}, u32[]{:S(2)}) collective-permute-start(f32[12,768]{1,0:T(8,128)S(1)} %add.247), channel_id=1, source_target_pairs={{0,16},{4,20},{8,24},{12,28},{16,0},{20,4},{24,8},{28,12},{1,17},{... | collective-permute-start | bytes 110600 | tf_op jit(solution)/shard_map/ppermute | solution.py:58
  267.1 19.8 %collective-permute-start.23 = (bf16[512,768]{1,0:T(8,128)(2,1)S(1)}, bf16[512,768]{1,0:T(8,128)(2,1)S(1)}, u32[]{:S(2)}, u32[]{:S(2)}) collective-permute-start(bf16[512,768]{1,0:T(8,128)(2,1)S(1)} %dynamic-slice_convert_fusion), channel_id=1, source_target_pairs={{0,1},{1,0},{2,3},{3,2},{4,5},{5,4},{6,7},{7,6},{8,9},{9,8},{10,11... | collective-permute-start | bytes 2359304 | tf_op jit(solution)/shard_map/ppermute | solution.py:58
  268.0 29.3 %collective-permute-start.36 = (bf16[96,1536]{1,0:T(8,128)(2,1)S(1)}, bf16[96,1536]{1,0:T(8,128)(2,1)S(1)}, u32[]{:S(2)}, u32[]{:S(2)}) collective-permute-start(bf16[96,1536]{1,0:T(8,128)(2,1)S(1)} %get-tuple-element.138), channel_id=1, source_target_pairs={{0,16},{4,20},{8,24},{12,28},{16,0},{20,4},{24,8},{28,12},{1,17},{... | collective-permute-start | bytes 884744 | tf_op jit(solution)/shard_map/ppermute | solution.py:58
  275.6 21.8 %collective-permute-start.37 = (bf16[96,1536]{1,0:T(8,128)(2,1)S(1)}, bf16[96,1536]{1,0:T(8,128)(2,1)S(1)}, u32[]{:S(2)}, u32[]{:S(2)}) collective-permute-start(bf16[96,1536]{1,0:T(8,128)(2,1)S(1)} %get-tuple-element.139), channel_id=1, source_target_pairs={{0,24},{4,28},{8,16},{12,20},{16,8},{20,12},{24,0},{28,4},{1,25},{... | collective-permute-start | bytes 884744 | tf_op jit(solution)/shard_map/ppermute | solution.py:58
  285.5 13.5 %collective-permute-start.34 = (bf16[96,1536]{1,0:T(8,128)(2,1)S(1)}, bf16[96,1536]{1,0:T(8,128)(2,1)S(1)}, u32[]{:S(2)}, u32[]{:S(2)}) collective-permute-start(bf16[96,1536]{1,0:T(8,128)(2,1)S(1)} %fusion.13), channel_id=1, source_target_pairs={{0,8},{4,12},{8,0},{12,4},{16,24},{20,28},{24,16},{28,20},{1,9},{5... | collective-permute-start | bytes 884744 | tf_op jit(solution)/shard_map/ppermute | solution.py:58
  286.0 6.8 %collective-permute-start.28 = (bf16[2,1,96,768]{3,2,0,1:T(8,128)(2,1)S(1)}, bf16[2,1,96,768]{3,2,0,1:T(8,128)(2,1)S(1)}, u32[]{:S(2)}, u32[]{:S(2)}) collective-permute-start(bf16[2,1,96,768]{3,2,0,1:T(8,128)(2,1)S(1)} %fusion.12), channel_id=1, source_target_pairs={{0,2},{1,3},{2,0},{3,1},{4,6},{5,7},{6,4},{7,5},{8,10},{9,11},{10,... | collective-permute-start | bytes 884744 | tf_op jit(solution)/shard_map/ppermute | solution.py:58
  286.9 9.0 %collective-permute-start.25 = (bf16[2,1,96,768]{3,2,1,0:T(8,128)(2,1)S(1)}, bf16[2,1,96,768]{3,2,1,0:T(8,128)(2,1)S(1)}, u32[]{:S(2)}, u32[]{:S(2)}) collective-permute-start(bf16[2,1,96,768]{3,2,1,0:T(8,128)(2,1)S(1)} %slice.389), channel_id=1, source_target_pairs={{0,4},{4,0},{8,12},{12,8},{16,20},{20,16},{24,28},{28,24},{1,5},{5... | collective-permute-start | bytes 884744 | tf_op jit(solution)/shard_map/ppermute | solution.py:58
  292.8 14.4 %collective-permute-start.29 = (bf16[96,768]{1,0:T(8,128)(2,1)S(1)}, bf16[96,768]{1,0:T(8,128)(2,1)S(1)}, u32[]{:S(2)}, u32[]{:S(2)}) collective-permute-start(bf16[96,768]{1,0:T(8,128)(2,1)S(1)} %slice_bitcast_fusion.14), channel_id=1, source_target_pairs={{0,16},{4,20},{8,24},{12,28},{16,0},{20,4},{24,8},{28,12},{1,17},{... | collective-permute-start | bytes 442376 | tf_op jit(solution)/shard_map/ppermute | solution.py:58
  295.9 11.3 %collective-permute-start.30 = (bf16[96,768]{1,0:T(8,128)(2,1)S(1)}, bf16[96,768]{1,0:T(8,128)(2,1)S(1)}, u32[]{:S(2)}, u32[]{:S(2)}) collective-permute-start(bf16[96,768]{1,0:T(8,128)(2,1)S(1)} %slice_bitcast_fusion.13), channel_id=1, source_target_pairs={{0,24},{4,28},{8,16},{12,20},{16,8},{20,12},{24,0},{28,4},{1,25},{... | collective-permute-start | bytes 442376 | tf_op jit(solution)/shard_map/ppermute | solution.py:58
  297.2 10.0 %collective-permute-start.26 = (bf16[96,768]{1,0:T(8,128)(2,1)S(1)}, bf16[96,768]{1,0:T(8,128)(2,1)S(1)}, u32[]{:S(2)}, u32[]{:S(2)}) collective-permute-start(bf16[96,768]{1,0:T(8,128)(2,1)S(1)} %fusion.17), channel_id=1, source_target_pairs={{0,8},{4,12},{8,0},{12,4},{16,24},{20,28},{24,16},{28,20},{1,9},{5... | collective-permute-start | bytes 442376 | tf_op jit(solution)/shard_map/ppermute | solution.py:58
  (43 other events, 275.4 us)

commit v4 on v3

--- a/solution.py
+++ b/solution.py
@@ -74,13 +74,6 @@
         turned = jnp.where((row // offset) % 2 == 1, cut[:, ::-1], cut)
         blocks = turned.reshape(blocks.shape)
     return blocks
-
-
-def gather_small(block):
-    blocks = block[None]
-    for offset in bit_offsets(1, lax.axis_size("row")):
-        blocks = jnp.concatenate([blocks, swap_over(blocks, ("row", offset))], axis=0)
-    return flip_order(blocks)
 
 
 class Gathered:
@@ -136,25 +129,49 @@
             back_at = back_at + moved
         return Gathered(arrays, table)
 
-    def reduce_near(self, pair, hold=None):
+    def split(self, pair):
         _, all_rows, cols = pair.shape
-        rows = all_rows // self.row_count
+        blocks = jnp.moveaxis(pair.reshape(2, self.row_count, -1, cols), 1, 0)
+        blocks = jnp.moveaxis(flip_order(blocks), 0, 1)
+        rows = blocks.shape[2]
+        half = self.row_count // 2
+        back = blocks[:, half:].reshape(2, self.far_count // 2, 2, -1, rows, cols)
+        return (
+            blocks[0, :half],
+            blocks[1, :half],
+            back[:, :, 0].reshape(2, -1, rows, cols),
+            back[:, :, 1].reshape(2, -1, rows, cols),
+        )
+
+    def part_of(self, x, index):
+        far, near = index // self.near_size, index % self.near_size
+        half, step = self.far_count // 2, self.near_size // 2
+        if far < half:
+            return x, (index,)
+        if near < step:
+            return 2, (x, (far - half) * step + near)
+        return 3, (x, (far - half) * step + near - step)
+
+    def part_shapes(self, rows, cols):
+        count = self.row_count
+        return [(count // 2, rows, cols)] * 2 + [(2, count // 4, rows, cols)] * 2
+
+    def reduce_near(self, parts, hold=None):
+        front, other, back, sent = parts
+        step = self.near_size // 2
+        front_x = swap_over(other, self.x_line)
+        back_y = swap_over(sent, ("row", step))
+        if hold is not None:
+            front_x, back_y, _ = lax.optimization_barrier((front_x, back_y, hold))
+        rows, cols = front.shape[1:]
         half = self.far_count // 2
-        pair = pair.reshape((2, 2, half, self.near_size, rows, cols))
-        front_x = swap_over(pair[1, 0], self.x_line)
-        back = pair[:, 1]
-        step = self.near_size // 2
-        sent = swap_over(back[:, :, step:], ("row", step)) if step else None
-        if hold is not None:
-            front_x, sent, _ = lax.optimization_barrier((front_x, sent, hold))
-        back = back.astype(F32)
-        if step:
-            back = back[:, :, :step] + sent.astype(F32)
-        front = pair[0, 0].astype(F32) + front_x.astype(F32)
-        back = self.reduce_bits(back, 2)
+        back = back.astype(F32) + back_y.astype(F32)
+        back = self.reduce_bits(back.reshape(2, half, step, rows, cols), 2)
         back = back[0] + swap_over(back[1].astype(BF16), self.x_line).astype(F32)
-        front = self.reduce_bits(front, 1)
-        return jnp.concatenate([front, back], axis=0).reshape(self.far_count, rows, cols)
+        front = front.astype(F32) + front_x.astype(F32)
+        front = self.reduce_bits(front.reshape(half, self.near_size, rows, cols), 1)
+        total = jnp.concatenate([front, back], axis=0).reshape(self.far_count, rows, cols)
+        return total, front_x
 
     def reduce_bits(self, parts, dim):
         while parts.shape[dim] > 1:
@@ -404,85 +421,119 @@
         copy.wait()
 
 
-def store_rows(value, out_ref, x, lanes, count):
-    rows = value.shape[0] // count
-    if rows % 16:
-        out_ref[x, :, lanes] = value
+def store_parts(held, grid, refs, x, lanes):
+    if len(refs) == 1:
+        refs[0][x, :, lanes] = held[...]
         return
     row = lax.axis_index("row")
-    for index in range(count):
+    rows = held.shape[0] // grid.row_count
+    for index in range(grid.row_count):
         start = pl.multiple_of((row ^ index) * rows, 16)
-        out_ref[x, pl.ds(start, rows), lanes] = value[index * rows : (index + 1) * rows]
-
-
-def relative_rows(pair, count):
-    _, all_rows, cols = pair.shape
-    if all_rows // count % 16 == 0:
-        return pair
-    blocks = jnp.moveaxis(pair.reshape(2, count, -1, cols), 1, 0)
-    return jnp.moveaxis(flip_order(blocks), 0, 1).reshape(pair.shape)
+        array, place = grid.part_of(x, index)
+        refs[array][place + (slice(None), lanes)] = held[pl.ds(start, rows), :]
+
+
+def parts_out(grid, width, cols):
+    rows = width // grid.row_count
+    if rows % 16:
+        return [(2, width, cols)]
+    return grid.part_shapes(rows, cols)
 
 
 def turn(value):
     return value.T
 
 
-def first_norm_kernel(gathered, cols, tokens_ref, vec_ref, bias_ref, *refs):
+def pick_half(here, mine_ref, other_ref):
+    mine, other = mine_ref[...].astype(F32), other_ref[...].astype(F32)
+    return jnp.where(here, mine, other)
+
+
+def first_norm_kernel(gathered, cols, place_ref, mine_ref, other_ref, *refs):
     count = len(gathered.arrays)
-    norm_ref, qkv_ref, out_w_ref, held, sems = refs[count:]
+    norm_ref, qkv_ref, tokens_ref, full_ref, out_w_ref, vec_ref, held, bias, sems = refs[count:]
     copies = weight_copies(gathered, refs[:count], held, sems)
     third = cols // 3
-
-    @pl.when(pl.program_id(0) == 0)
+    step = pl.program_id(0)
+    per_half = pl.num_programs(0) // 2
+
+    @pl.when(step == 0)
     def _():
         start_all(copies[0] + copies[1])
-
-    normed, _ = normalize_rows(tokens_ref[...].astype(F32))
-    first_in = (normed * vec_ref[0:1, :] + vec_ref[1:2, :]).astype(BF16)
-    norm_ref[...] = first_in
-
-    @pl.when(pl.program_id(0) == 0)
-    def _():
         wait_all(copies[0] + copies[1])
         for x in range(2):
             out_w_ref[:, x * third : (x + 1) * third] = held[x, :, held.shape[2] - third :]
-
-    for x in range(2):
-        result = dot_nn(first_in, held[x, :, :cols])
-        for part in range(3):
-            lanes = slice((2 * part + x) * third, (2 * part + x + 1) * third)
-            value = result[:, part * third : (part + 1) * third] + bias_ref[0:1, lanes]
-            qkv_ref[:, lanes] = value.astype(BF16)
-
-
-def first_norm(tokens, vec_all, bias, gathered, width_loc):
-    length, width = tokens.shape
+            for part in range(3):
+                lanes = slice((2 * part + x) * third, (2 * part + x + 1) * third)
+                full_ref[:, lanes] = held[x, :, part * third : (part + 1) * third]
+        first = cols // 128 * 128
+        rows = turn(held[0, :, first : first + 128].astype(F32))[cols - first :]
+        vec_ref[...] = rows[: vec_ref.shape[0]]
+        row_at = lax.broadcasted_iota(jnp.int32, (rows.shape[1], 2 * third), 0)
+        lane_at = lax.broadcasted_iota(jnp.int32, (rows.shape[1], 2 * third), 1)
+        wanted = jnp.where(
+            lane_at < third, place_ref[1] + lane_at, place_ref[2] + lane_at - third
+        )
+        chosen = jnp.where(row_at == wanted, 1.0, 0.0).astype(BF16)
+        picked = dot_nn(vec_ref[...].astype(BF16), chosen)
+        bias[...] = jnp.zeros_like(bias)
+        bias[0:1, : 2 * third] = picked[2:3]
+        bias[0:1, 4 * third :] = picked[3:4]
+
+    tokens = pick_half(step // per_half == place_ref[0], mine_ref, other_ref)
+    tokens_ref[...] = tokens.astype(BF16)
+    normed, _ = normalize_rows(tokens)
+    first_in = (normed * vec_ref[0:1, :] + vec_ref[1:2, :]).astype(BF16)
+    norm_ref[...] = first_in
+    qkv_ref[...] = (dot_nn(first_in, full_ref[...]) + bias[0:1, :]).astype(BF16)
+
+
+def first_norm(place, mine, other, gathered, width_loc):
+    rows, width = mine.shape
+    length = 2 * rows
     cols = 3 * width_loc
+    steps = rows // ROW_BLOCK
+    half = pl.BlockSpec((ROW_BLOCK, width), lambda step, place_ref: (step % steps, 0))
+
+    def by_row(size):
+        return pl.BlockSpec((ROW_BLOCK, size), lambda step, place_ref: (step, 0))
+
     return pl.pallas_call(
         functools.partial(first_norm_kernel, gathered, cols),
-        grid=(length // ROW_BLOCK,),
-        in_specs=[rows_of(ROW_BLOCK, width), whole(vec_all.shape), whole(bias.shape)]
-        + [ANYWHERE] * len(gathered.arrays),
-        out_specs=[
-            rows_of(ROW_BLOCK, width),
-            rows_of(ROW_BLOCK, 2 * cols),
-            whole((width, 2 * width_loc)),
-        ],
+        grid_spec=pltpu.PrefetchScalarGridSpec(
+            num_scalar_prefetch=1,
+            grid=(2 * steps,),
+            in_specs=[half, half] + [ANYWHERE] * len(gathered.arrays),
+            out_specs=[
+                by_row(width),
+                by_row(2 * cols),
+                by_row(width),
+                whole((width, 2 * cols)),
+                whole((width, 2 * width_loc)),
+                whole((16, width)),
+            ],
+            scratch_shapes=weight_scratch(gathered)[:1]
+            + [pltpu.VMEM((8, 2 * cols), F32)]
+            + weight_scratch(gathered)[1:],
+        ),
         out_shape=[
             shaped((length, width), BF16),
             shaped((length, 2 * cols), BF16),
+            shaped((length, width), BF16),
+            shaped((width, 2 * cols), BF16),
             shaped((width, 2 * width_loc), BF16),
+            shaped((16, width), F32),
         ],
-        scratch_shapes=weight_scratch(gathered),
         compiler_params=PARAMS,
         cost_estimate=cost(4 * length * width * cols, 2 * length * (2 * width + cols)),
         name="first_norm",
-    )(tokens, vec_all, bias, *gathered.arrays)
+    )(place, mine, other, *gathered.arrays)
 
 
 def attended_kernel(
-    heads_ref, partner_ref, own_ref, other_ref, tokens_ref, vec_ref, first_ref, cot_ref,
-    hidden_ref, norm_ref, norm_turned_ref, first_turned_ref, cot_turned_ref,
+    place_ref, heads_ref, partner_ref, own_ref, other_ref, tokens_ref, vec_ref, first_ref,
+    mine_ref, other_cot_ref, hidden_ref, norm_ref, norm_turned_ref, first_turned_ref,
+    cot_turned_ref, cot_ref,
 ):
     attended = dot_nt(heads_ref[...], own_ref[...]) + dot_nt(partner_ref[...], other_ref[...])
     hidden = tokens_ref[...].astype(F32) + attended + vec_ref[4:5, :]
@@ -492,34 +543,48 @@
     norm_ref[...] = second_in
     norm_turned_ref[...] = turn(second_in)
     first_turned_ref[...] = turn(first_ref[...])
-    cot_turned_ref[...] = turn(cot_ref[...])
-
-
-def attended_norm(heads, partner_heads, own_out, partner_out, tokens, vec_all, first_in, cot):
+    here = pl.program_id(0) // (pl.num_programs(0) // 2) == place_ref[0]
+    cot = pick_half(here, mine_ref, other_cot_ref).astype(BF16)
+    cot_ref[...] = cot
+    cot_turned_ref[...] = turn(cot)
+
+
+def attended_norm(place, heads, partner_heads, own_out, partner_out, tokens, vec_all, first_in, cots):
     length, width = tokens.shape
     cols = heads.shape[1]
-    full = rows_of(ROW_BLOCK, width)
-    turned = pl.BlockSpec((width, ROW_BLOCK), lambda step: (0, step))
+    steps = length // ROW_BLOCK
+    half = pl.BlockSpec((ROW_BLOCK, width), lambda step, place_ref: (step % (steps // 2), 0))
+    turned = pl.BlockSpec((width, ROW_BLOCK), lambda step, place_ref: (0, step))
+
+    def by_row(size):
+        return pl.BlockSpec((ROW_BLOCK, size), lambda step, place_ref: (step, 0))
+
+    full = by_row(width)
     return pl.pallas_call(
         attended_kernel,
-        grid=(length // ROW_BLOCK,),
-        in_specs=[
-            rows_of(ROW_BLOCK, cols),
-            rows_of(ROW_BLOCK, cols),
-            whole(own_out.shape),
-            whole(partner_out.shape),
-            full,
-            whole(vec_all.shape),
-            full,
-            full,
-        ],
-        out_specs=[full, full, turned, turned, turned],
+        grid_spec=pltpu.PrefetchScalarGridSpec(
+            num_scalar_prefetch=1,
+            grid=(steps,),
+            in_specs=[
+                by_row(cols),
+                by_row(cols),
+                whole(own_out.shape),
+                whole(partner_out.shape),
+                full,
+                whole(vec_all.shape),
+                full,
+                half,
+                half,
+            ],
+            out_specs=[full, full, turned, turned, turned, full],
+        ),
         out_shape=[shaped((length, width), F32), shaped((length, width), BF16)]
-        + [shaped((width, length), BF16)] * 3,
+        + [shaped((width, length), BF16)] * 3
+        + [shaped((length, width), BF16)],
         compiler_params=PARAMS,
         cost_estimate=cost(4 * length * width * cols, length * width * 20),
         name="attended_norm",
-    )(heads, partner_heads, own_out, partner_out, tokens, vec_all, first_in, cot)
+    )(place, heads, partner_heads, own_out, partner_out, tokens, vec_all, first_in, *cots)
 
 
 def feed_kernel(gathered, norm_ref, cot_ref, bias_ref, *refs):
@@ -530,11 +595,8 @@
     length = norm_ref.shape[0]
     curve, cubic = math.sqrt(2 / math.pi), 0.044715
     cols = held.shape[2] // 2
-    block = act_ref.shape[1]
-    per_x = cols // block
-    x = step // per_x
-    up_lanes = pl.ds(pl.multiple_of(step % per_x * block, 128), block)
-    down_lanes = pl.ds(pl.multiple_of(cols + step % per_x * block, 128), block)
+    x = step
+    up_lanes, down_lanes = slice(0, cols), slice(cols, 2 * cols)
 
     @pl.when(step == 0)
     def _():
@@ -543,7 +605,7 @@
         back_ref[...] = jnp.zeros_like(back_ref)
         wait_all(copies[0])
 
-    @pl.when(step == per_x)
+    @pl.when(step == 1)
     def _():
         wait_all(copies[1])
 
@@ -573,7 +635,7 @@
 def feed(norm, cot, bias, gathered):
     length, width = norm.shape
     hidden = bias.shape[1]
-    block = hidden // 4
+    block = hidden // 2
     tall = pl.BlockSpec((length, block), lambda step: (0, step))
     flat = pl.BlockSpec((1, block), lambda step: (0, step))
     full = whole((length, width))
@@ -597,26 +659,34 @@
     )(norm, cot, bias, *gathered.arrays)
 
 
-def feed_grads_kernel(row_count, cot_ref, norm_ref, act_ref, gup_ref, out_ref):
-    kind = pl.program_id(0)
+def feed_grads_kernel(grid, cot_ref, norm_ref, act_ref, gup_ref, *refs):
+    kind, x_at = pl.program_id(0), pl.program_id(1)
+    outs, held = refs[:-1], refs[-1]
+    size = held.shape[1]
 
     @pl.when(kind == 0)
     def _():
-        value = dot_nn(cot_ref[...], act_ref[...]).astype(BF16)
-        store_rows(value, out_ref, 0, slice(None), row_count)
+        held[...] = dot_nn(cot_ref[...], act_ref[...]).astype(BF16)
 
     @pl.when(kind == 1)
     def _():
-        value = dot_nn(norm_ref[...], gup_ref[...]).astype(BF16)
-        store_rows(value, out_ref, 0, slice(None), row_count)
-
-
-def feed_grads(cot_turned, norm_turned, act, grad_up, row_count):
+        held[...] = dot_nn(norm_ref[...], gup_ref[...]).astype(BF16)
+
+    for index in range(2):
+        for x in range(2):
+
+            @pl.when((kind == index) & (x_at == x))
+            def _():
+                store_parts(held, grid, outs, x, slice((1 - index) * size, (2 - index) * size))
+
+
+def feed_grads(cot_turned, norm_turned, act, grad_up, grid):
     width, length = cot_turned.shape
     hidden = act.shape[1]
     block = hidden // 2
-    return pl.pallas_call(
-        functools.partial(feed_grads_kernel, row_count),
+    shapes = parts_out(grid, width, hidden)
+    parts = pl.pallas_call(
+        functools.partial(feed_grads_kernel, grid),
         grid=(2, 2),
         in_specs=[
             whole((width, length)),
@@ -624,12 +694,14 @@
             pl.BlockSpec((length, block), lambda kind, x: (0, jnp.where(kind == 0, x, 1))),
             pl.BlockSpec((length, block), lambda kind, x: (0, jnp.where(kind == 1, x, 0))),
         ],
-        out_specs=pl.BlockSpec((1, width, block), lambda kind, x: (x, 0, 1 - kind)),
-        out_shape=shaped((2, width, hidden), BF16),
+        out_specs=[whole(shape) for shape in shapes],
+        out_shape=[shaped(shape, BF16) for shape in shapes],
+        scratch_shapes=[pltpu.VMEM((width, block), BF16)],
         compiler_params=PARAMS,
         cost_estimate=cost(4 * length * width * hidden, 4 * length * (width + hidden)),
         name="feed_grads",
     )(cot_turned, norm_turned, act, grad_up)
+    return parts if len(parts) == 4 else grid.split(parts[0])
 
 
 def second_back_kernel(
@@ -683,9 +755,10 @@
     )(part, other, hidden, cot, vec_all, out_w, heads_turned)
 
 
-def qkv_grads_kernel(row_count, norm_ref, grad_ref, out_grad_ref, out_ref):
+def qkv_grads_kernel(grid, norm_ref, grad_ref, out_grad_ref, *refs):
     part = pl.program_id(0)
-    half = grad_ref.shape[1] // 2
+    outs, held = refs[:-1], refs[-1]
+    half = held.shape[1]
     for index in range(4):
 
         @pl.when(part == index)
@@ -694,76 +767,70 @@
                 grads = out_grad_ref[...]
             else:
                 grads = dot_nn(norm_ref[...], grad_ref[...]).astype(BF16)
-            lanes = slice(index * half, (index + 1) * half)
             for x in range(2):
-                store_rows(grads[:, x * half : (x + 1) * half], out_ref, x, lanes, row_count)
-
-
-def qkv_grads(norm_turned, grad_qkv, out_grad, row_count):
+                held[...] = grads[:, x * half : (x + 1) * half]
+                store_parts(held, grid, outs, x, slice(index * half, (index + 1) * half))
+
+
+def qkv_grads(norm_turned, grad_qkv, out_grad, grid):
     width, length = norm_turned.shape
     cols = out_grad.shape[1]
-    return pl.pallas_call(
-        functools.partial(qkv_grads_kernel, row_count),
+    shapes = parts_out(grid, width, 2 * cols)
+    parts = pl.pallas_call(
+        functools.partial(qkv_grads_kernel, grid),
         grid=(4,),
         in_specs=[
             whole((width, length)),
             pl.BlockSpec((length, cols), lambda part: (0, jnp.minimum(part, 2))),
             whole((width, cols)),
         ],
-        out_specs=whole((2, width, 2 * cols)),
-        out_shape=shaped((2, width, 2 * cols), BF16),
+        out_specs=[whole(shape) for shape in shapes],
+        out_shape=[shaped(shape, BF16) for shape in shapes],
+        scratch_shapes=[pltpu.VMEM((width, cols // 2), BF16)],
         compiler_params=PARAMS,
         cost_estimate=cost(6 * length * width * cols, 4 * length * (2 * width + 2 * cols)),
         name="qkv_grads",
     )(norm_turned, grad_qkv, out_grad)
-
-
-def first_back_kernel(gathered, cols, grad_ref, tokens_ref, after_ref, *refs):
-    count = len(gathered.arrays)
-    part_ref, sum_ref, bias_ref, held, sems = refs[count:]
-    copies = weight_copies(gathered, refs[:count], held, sems)
-    third = cols // 3
+    return parts if len(parts) == 4 else grid.split(parts[0])
+
+
+def first_back_kernel(grad_ref, weight_ref, tokens_ref, after_ref, part_ref, sum_ref, bias_ref):
+    part = dot_nt(grad_ref[...], weight_ref[...])
+    part_ref[...] = part
+    normed, _ = normalize_rows(tokens_ref[...].astype(F32))
 
     @pl.when(pl.program_id(0) == 0)
     def _():
-        start_all(copies[0] + copies[1])
         sum_ref[...] = jnp.zeros_like(sum_ref)
         bias_ref[...] = jnp.zeros_like(bias_ref)
-        wait_all(copies[0] + copies[1])
-
-    part = None
-    for x in range(2):
-        grads = jnp.concatenate(
-            [grad_ref[:, (2 * at + x) * third : (2 * at + x + 1) * third] for at in range(3)], axis=1
-        )
-        product = dot_nt(grads, held[x, :, :cols])
-        part = product if part is None else part + product
-    part_ref[...] = part
-    normed, _ = normalize_rows(tokens_ref[...].astype(F32))
+
     for row, value in enumerate((part * normed, part)):
         sum_ref[row : row + 1, :] += jnp.sum(value, axis=0, keepdims=True)
     bias_ref[0:1, :] += jnp.sum(grad_ref[...].astype(F32), axis=0, keepdims=True)
 
 
-def first_back(grad_qkv, tokens, gathered, width_loc, after):
+def first_back(grad_qkv, weight, tokens, after):
     length, width = tokens.shape
     cols = grad_qkv.shape[1]
     return pl.pallas_call(
-        functools.partial(first_back_kernel, gathered, 3 * width_loc),
+        first_back_kernel,
         grid=(length // ROW_BLOCK,),
-        in_specs=[rows_of(ROW_BLOCK, cols), rows_of(ROW_BLOCK, width), ANYWHERE]
-        + [ANYWHERE] * len(gathered.arrays),
+        in_specs=[
+            rows_of(ROW_BLOCK, cols),
+            whole(weight.shape),
+            rows_of(ROW_BLOCK, width),
+            ANYWHERE,
+        ],
         out_specs=[rows_of(ROW_BLOCK, width), whole((8, width)), whole((8, cols))],
         out_shape=[
             shaped((length, width), F32),
             shaped((8, width), F32),
             shaped((8, cols), F32),
         ],
-        scratch_shapes=weight_scratch(gathered),
         compiler_params=PARAMS,
         cost_estimate=cost(2 * length * width * cols, length * (6 * width + 2 * cols)),
         name="first_back",
-    )(grad_qkv, tokens, after, *gathered.arrays)
+    )(grad_qkv, weight, tokens, after)
 
 
 def token_back_kernel(core_ref, part_ref, other_ref, tokens_ref, grad_ref, vec_ref, out_ref):
@@ -824,21 +891,13 @@
     hidden_loc = w_up.shape[1]
     shard_rows = w_up.shape[0]
 
-    pad = -3 * width_loc % 128
+    pad = -(3 * width_loc + VEC_ROWS) % 128
     pack_qkv = jnp.concatenate(
         [w_qkv[:, part].astype(BF16) for part in range(3)]
-        + [jnp.zeros((shard_rows, pad), BF16), w_out.T.astype(BF16)],
+        + [vectors.T.astype(BF16), jnp.zeros((shard_rows, pad), BF16), w_out.T.astype(BF16)],
         axis=1,
     )
     pack_feed = jnp.concatenate([w_up.astype(BF16), w_down.T.astype(BF16)], axis=1)
-
-    def both_halves(mine):
-        other = swap_over(mine, core_line)
-        return jnp.where(
-            core == 0,
-            jnp.concatenate([mine, other], axis=0),
-            jnp.concatenate([other, mine], axis=0),
-        )
 
     def own_rows(value):
         return lax.dynamic_slice_in_dim(value, core * rows_loc, rows_loc, 0)
@@ -846,17 +905,16 @@
     def partner_rows(value):
         return lax.dynamic_slice_in_dim(value, (1 - core) * rows_loc, rows_loc, 0)
 
-    far_qkv = grid.gather_far(pack_qkv)
-    vec_blocks = gather_small(vectors.astype(BF16))
-    pack_feed, *far_qkv = lax.optimization_barrier((pack_feed, *far_qkv))
-    near_qkv = grid.gather_near(far_qkv)
-    far_feed = grid.gather_far(pack_feed)
-    *far_feed, _ = lax.optimization_barrier((*far_feed, near_qkv.arrays[-1]))
-    near_feed = grid.gather_near(far_feed)
-
-    all_tokens = both_halves(tokens)
-    all_cot = both_halves(cotangent)
-    vec_all = jnp.swapaxes(vec_blocks, 0, 1).reshape(VEC_ROWS, width).astype(F32)
+    def rows_gathered(block):
+        return lax.all_gather(block, "row", axis=0, tiled=True)[None]
+
+    near_qkv = grid.gather_near(grid.gather_far(pack_qkv))
+    near_feed = Gathered(
+        [rows_gathered(pack_feed), rows_gathered(swap_over(pack_feed, grid.x_line))],
+        [(0, 0, 0, 0), (1, 1, 0, 0)],
+    )
+    partner = swap_over(jnp.stack([tokens, cotangent]), core_line)
+    place = jnp.stack([core, col_index * width_loc, other_col * width_loc]).astype(jnp.int32)
 
     def cat_blocks(vec_row, size):
         return jnp.concatenate(
@@ -866,47 +924,41 @@
             ]
         )
 
-    bias_qkv = jnp.concatenate(
-        [
-            cat_blocks(vec_all[2], width_loc),
-            jnp.zeros((width_core,), F32),
-            cat_blocks(vec_all[3], width_loc),
-        ]
-    )
-    bias_up = cat_blocks(vec_all[8:].reshape(-1), hidden_loc)
-    first_in, qkv, full_out = first_norm(
-        all_tokens, vec_all, bias_qkv[None], near_qkv, width_loc
-    )
+    first_in, qkv, all_tokens, full_qkv, full_out, vec_all = first_norm(
+        place, tokens, partner[0], near_qkv, width_loc
+    )
+    bias_up = cat_blocks(vec_all[8:VEC_ROWS].reshape(-1), hidden_loc)
     partner_out = swap_over(full_out, core_line)
     heads_low, heads_turned, lse = attend_forward(qkv)
     partner_heads = swap_over(heads_low, core_line)
-    hidden_state, second_in, second_turned, first_turned, cot_turned = attended_norm(
-        heads_low, partner_heads, full_out, partner_out, all_tokens, vec_all, first_in, all_cot
+    hidden_state, second_in, second_turned, first_turned, cot_turned, all_cot = attended_norm(
+        place, heads_low, partner_heads, full_out, partner_out, all_tokens, vec_all, first_in,
+        (cotangent, partner[1]),
     )
     activated, grad_upper, grad_bias_up, down_part, second_part, second_low = feed(
         second_in, all_cot, bias_up[None], near_feed
     )
 
     second_other = swap_over(second_low, core_line)
-    pair_feed = feed_grads(cot_turned, second_turned, activated, grad_upper, grid.row_count)
-    pair_feed = relative_rows(pair_feed, grid.row_count)
+    parts_feed = feed_grads(cot_turned, second_turned, activated, grad_upper, grid)
     grad_hidden, grad_heads, second_sums, out_grad = second_back(
         second_part, second_other, hidden_state, all_cot, vec_all, full_out, heads_turned
     )
     down_other = swap_over(partner_rows(down_part).astype(BF16), core_line).astype(F32)
     mixed_out = own_rows(hidden_state) + own_rows(down_part) + down_other + vec_all[7]
     grad_qkv_low = attend_backward(qkv, grad_heads, lse)
-    pair_qkv = qkv_grads(first_turned, grad_qkv_low, out_grad, grid.row_count)
+    parts_qkv = qkv_grads(first_turned, grad_qkv_low, out_grad, grid)
     first_part, first_sums, bias_sums = first_back(
-        grad_qkv_low, all_tokens, near_qkv, width_loc, pair_qkv
-    )
-    pair_qkv = relative_rows(pair_qkv, grid.row_count)
+        grad_qkv_low, full_qkv, all_tokens, parts_qkv[1]
+    )
+
+    near_pack, arrived = grid.reduce_near(parts_qkv)
+    owned_pack = grid.reduce_far(near_pack)
+    owned_feed = grid.reduce_far(grid.reduce_near(parts_feed, parts_qkv[1])[0])
+    owned_up, owned_down = owned_feed[:, :hidden_loc], owned_feed[:, hidden_loc:]
+    first_part, first_sums, _ = lax.optimization_barrier((first_part, first_sums, arrived))
     first_other = swap_over(partner_rows(first_part).astype(BF16), core_line)
     token_grad = token_back(core, first_part, first_other, tokens, grad_hidden, vec_all)
-
-    owned_feed = grid.reduce_far(grid.reduce_near(pair_feed, grad_qkv_low))
-    owned_up, owned_down = owned_feed[:, :hidden_loc], owned_feed[:, hidden_loc:]
-    owned_pack = grid.reduce_far(grid.reduce_near(pair_qkv))
     owned_qkv = jnp.stack(
         [owned_pack[:, part * width_loc : (part + 1) * width_loc] for part in range(3)], axis=1
     )

time: 313 us -> 312 us (level)
  waiting for transfers between devices: 91.7 us -> 112 us
  starting transfers between devices: 50.4 us -> 33.8 us
  between operations: 1.65 us -> 14.9 us
  Pallas kernels: 108 us -> 95.3 us
  other arithmetic: 33.9 us -> 23.5 us
  local copies, waits for them, and re-layouts: 25.4 us -> 31.4 us
    all_gather x0 -> x2, waiting for transfers between devices: none -> 17.7 us  [rows_gathered(): return lax.all_gather(block, 'row', axis=0, tiled=True)[None]]
    ppermute x43 -> x33, starting transfers between devices: 50.4 us -> 33.7 us  [swap_over(): return lax.ppermute(value, name, pairs)]
    unnamed x100 -> x108, local copies, waits for them, and re-layouts: 13.7 us -> 21 us
    pallas_call x1, Pallas kernels: 24.1 us -> 17.5 us  [feed(): pl.pallas_call(functools.partial(feed_kernel, gathered), grid=(hidden //...]
    select_n x5 -> x0, other arithmetic: 6.61 us -> none  [the longest x2 6.57 us: both_halves(): jnp.where(core == 0, jnp.concatenate([mine, other], axis=0), jnp.concaten...]
    add x6 -> x4, other arithmetic: 8.92 us -> 5.77 us  [the longest x2 2.91 us: reduce_near(): front = front.astype(F32) + front_x.astype(F32)]
    ppermute x43 -> x33, waiting for transfers between devices: 91.7 us -> 94.1 us  [swap_over(): return lax.ppermute(value, name, pairs)]
  transfers between devices with their start and end apart: 43 -> 35, of which waited for: 17 -> 14; matrix products, arithmetic and copies ran while one was open for 13% -> 12% of each run, Pallas kernels for 22% -> 24%
where the time goes in v4:
time: 312 us; the launch traced here: 311 us
  waiting for transfers between devices  112 us (36%)
  Pallas kernels  95.3 us (31%)
  starting transfers between devices  33.8 us (11%)
  local copies, waits for them, and re-layouts  31.4 us (10%)
  other arithmetic  23.5 us (8%)
  between operations  14.9 us (5%)
    ppermute x33, waiting for transfers between devices, swap_over(): return lax.ppermute(value, name, pairs)  94.1 us
    ppermute x33, starting transfers between devices, swap_over(): return lax.ppermute(value, name, pairs)  33.7 us
    unnamed x108, local copies, waits for them, and re-layouts  21 us
    all_gather x2, waiting for transfers between devices, rows_gathered(): return lax.all_gather(block, 'row', axis=0, tiled=True)[None]  17.7 us
    pallas_call x1, Pallas kernels, feed(): pl.pallas_call(functools.partial(feed_kernel, gathered), grid=(hidden //...  17.5 us
    pallas_call x1, Pallas kernels, attend_backward(): pl.pallas_call(attend_back_kernel, grid=(pairs,), in_specs=[lanes(0), lan...  15.7 us
    pallas_call x1, Pallas kernels, attend_forward(): pl.pallas_call(attend_kernel, grid=(pairs,), in_specs=[lanes(0), lanes(1)...  12.4 us
    pallas_call x1, Pallas kernels, feed_grads(): pl.pallas_call(functools.partial(feed_grads_kernel, grid), grid=(2, 2), i...  10.4 us
  transfers between devices with their start and end apart: 35, of which 14 were waited for; matrix products, arithmetic and copies ran while one was open for 12% of the time, Pallas kernels for 24%

profile of v4, /device:TPU:0, one launch (start us, length us, event | category | flops | bytes accessed | tf_op | source)
XLA Modules:
  0.0 310.6 jit_solution(17842407417625163353)
XLA Ops:
  10.1 3.0 collective-permute-start.10
  13.1 7.2 %collective-permute-done.10 = bf16[96,1536]{1,0:T(8,128)(2,1)S(1)} collective-permute-done((bf16[96,1536]{1,0:T(8,128)(2,1)}, bf16[96,1536]{1,0:T(8,128)(2,1)S(1)}, u32[]{:S(2)}, u32[]{:S(2)}) %collective-permute-start.10) | collective-permute-done | bytes 294944 | tf_op jit(solution)/shard_map/ppermute | solution.py:58
  23.4 2.9 collective-permute-start.4
  27.8 18.1 %collective-permute-done.4 = bf16[96,832]{1,0:T(8,128)(2,1)S(1)} collective-permute-done((bf16[96,832]{1,0:T(8,128)(2,1)S(1)}, bf16[96,832]{1,0:T(8,128)(2,1)S(1)}, u32[]{:S(2)}, u32[]{:S(2)}) %collective-permute-start.4) | collective-permute-done | bytes 159776 | tf_op jit(solution)/shard_map/ppermute | solution.py:58
  46.0 1.6 collective-permute-start.6
  47.7 1.5 collective-permute-start.2
  49.3 6.9 %collective-permute-done.6 = bf16[2,96,832]{2,1,0:T(8,128)(2,1)S(1)} collective-permute-done((bf16[2,96,832]{2,1,0:T(8,128)(2,1)S(1)}, bf16[2,96,832]{2,1,0:T(8,128)(2,1)S(1)}, u32[]{:S(2)}, u32[]{:S(2)}) %collective-permute-start.6) | collective-permute-done | bytes 319520 | tf_op jit(solution)/shard_map/ppermute | solution.py:58
  57.7 7.3 %collective-permute-done.2 = bf16[2,96,832]{2,1,0:T(8,128)(2,1)S(1)} collective-permute-done((bf16[2,96,832]{2,1,0:T(8,128)(2,1)S(1)}, bf16[2,96,832]{2,1,0:T(8,128)(2,1)S(1)}, u32[]{:S(2)}, u32[]{:S(2)}) %collective-permute-start.2) | collective-permute-done | bytes 319520 | tf_op jit(solution)/shard_map/ppermute | solution.py:58
  66.0 1.5 slice_bitcast_fusion.1
  67.5 17.3 %collective-permute-done.7.refs_3_ = bf16[4,96,832]{2,1,0:T(8,128)(2,1)} collective-permute-done((bf16[4,96,832]{2,1,0:T(8,128)(2,1)S(1)}, bf16[4,96,832]{2,1,0:T(8,128)(2,1)}, u32[]{:S(2)}, u32[]{:S(2)}) %collective-permute-start.7) | collective-permute-done | bytes 639008 | tf_op jit(solution)/shard_map/ppermute | solution.py:58
  86.0 8.1 %first_norm.1 = (bf16[1024,768]{1,0:T(8,128)(2,1)}, bf16[1024,1152]{1,0:T(8,128)(2,1)}, bf16[1024,768]{1,0:T(8,128)(2,1)}, bf16[768,1152]{1,0:T(8,128)(2,1)}, bf...) custom-call(s32[3]{0:T(128)S(1)} %pad_add_fusion.place_ref, bf16[512,768]{1,0:T(8,128)(2,1)S(1)} %copy-done.3, ...), custom_call_target="tpu_custom_call" | custom-call | flops 1811939328 | bytes 4325376 | tf_op jit(solution)/shard_map/first_norm/pallas_call | solution.py:501
  94.1 1.7 copy-done
  95.8 12.4 %attend_forward.1 = (bf16[1024,384]{1,0:T(8,128)(2,1)S(1)}, bf16[384,1024]{1,0:T(8,128)(2,1)S(1)}, f32[3,8,1024]{2,1,0:T(8,128)S(1)}) custom-call(bf16[1024,1152]{1,0:T(8,128)(2,1)S(1)} %copy-done, bf16[1024,1152]{1,0:T(8,128)(2,1)S(1)} %copy-done, bf16[1024,1152]{1,0:T(8,128)(2,1)S(1)} %copy-done), custom_call_target="tpu_custom_call" | custom-call | flops 1610612736 | bytes 3145728 | tf_op jit(solution)/shard_map/attend_forward/pallas_call | solution.py:264
  114.6 8.1 %attended_norm.1 = (f32[1024,768]{1,0:T(8,128)}, bf16[1024,768]{1,0:T(8,128)(2,1)S(1)}, bf16[768,1024]{1,0:T(8,128)(2,1)}, bf16[768,1024]{1,0:T(8,128)(2,1)}, bf...) custom-call(s32[3]{0:T(128)S(1)} %pad_add_fusion.place_ref, bf16[1024,384]{1,0:T(8,128)(2,1)S(1)} %get-tuple-element.58.heads_ref, ...), custom_call_target="tpu_custom_call" | custom-call | flops 1207959552 | bytes 15728640 | tf_op jit(solution)/shard_map/attended_norm/pallas_call | solution.py:563
  123.9 17.7 %all-gather.5.cloned.1.call-done = bf16[768,1536]{1,0:T(8,128)(2,1)} async-done(((bf16[96,1536]{1,0:T(8,128)(2,1)}), bf16[768,1536]{1,0:T(8,128)(2,1)}) %all-gather.5.cloned.1.call-update) | async-done | bytes 2359312 | tf_op jit(solution)/shard_map/all_gather | solution.py:909
  144.3 17.5 %feed.1 = (bf16[1024,1536]{1,0:T(8,128)(2,1)}, bf16[1024,1536]{1,0:T(8,128)(2,1)}, f32[1,1536]{1,0:T(1,128)S(1)}, f32[1024,768]{1,0:T(8,128)}, f32[1024,768]{1,0:T(8,128)}, /*index=5*/bf16[1024,768]{1,0:T(8,128)(2,1)}) custom-call(bf16[1024,768]{1,0:T(8,128)(2,1)S(1)} %copy-done.24, bf16[1024,768]{1,0:T(8,128)(2,1)S(1)} %copy-done.7, ...), custom_call_target="tpu_custom_call" | custom-call | flops 9663676416 | bytes 9437184 | tf_op jit(solution)/shard_map/feed/pallas_call | solution.py:642
  161.9 2.4 dynamic-slice_convert_fusion.1
  164.8 10.4 %feed_grads.1 = (bf16[4,96,1536]{2,1,0:T(8,128)(2,1)S(1)}, bf16[4,96,1536]{2,1,0:T(8,128)(2,1)}, bf16[2,2,96,1536]{3,2,1,0:T(8,128)(2,1)S(1)}, bf16[2,2,96,1536]{3,2,1,0:T(8,128)(2,1)}) custom-call(bf16[768,1024]{1,0:T(8,128)(2,1)} %get-tuple-element.83.cot_ref, bf16[768,1024]{1,0:T(8,128)(2,1)} %get-tuple-element.84.norm_ref, ...), custom_call_target="tpu_custom_call" | custom-call | flops 4831838208 | bytes 9437184 | tf_op jit(solution)/shard_map/feed_grads/pallas_call | solution.py:688
  181.5 3.4 %add_add_fusion = f32[512,768]{1,0:T(8,128)} fusion(bf16[512,768]{1,0:T(8,128)(2,1)S(1)} %collective-permute-done.11, f32[1024,768]{1,0:T(8,128)} %get-tuple-element.66, s32[]{:T(128)S(6)} %select_n.35, f32[1024,768]{1,0:T(8,128)} %get-tuple-element.63.hidden_ref, f32[768]{0:T(1024)S(1)} %slice_reduce_fusion.2), kind=kLoop, calls=%fused_computation.4 | loop fusion | flops 1572864 | bytes 5508100 | tf_op jit(solution)/shard_map/add | solution.py:948
  185.0 8.7 %second_back.1 = (f32[1024,768]{1,0:T(8,128)}, bf16[1024,384]{1,0:T(8,128)(2,1)S(1)}, f32[8,768]{1,0:T(8,128)S(1)}, bf16[768,384]{1,0:T(8,128)(2,1)S(1)}) custom-call(f32[1024,768]{1,0:T(8,128)} %get-tuple-element.67.part_ref, bf16[1024,768]{1,0:T(8,128)(2,1)S(1)} %collective-permute-done.12.other_ref, f32[1024,768]{1,0:T(8,128)} %get-tuple-element.63.hidden_ref, ...), custom_call_target="tpu_custom_call" | custom-call | flops 1207959552 | bytes 15728640 | tf_op jit(solution)/shard_map/second_back/pallas_call | solution.py:739
  193.7 15.7 %attend_backward.1.grad_ref = bf16[1024,1152]{1,0:T(8,128)(2,1)S(1)} custom-call(bf16[1024,1152]{1,0:T(8,128)(2,1)S(1)} %copy-done.1, bf16[1024,1152]{1,0:T(8,128)(2,1)S(1)} %copy-done.1, bf16[1024,1152]{1,0:T(8,128)(2,1)S(1)} %copy-done.1, bf16[1024,384]{1,0:T(8,128)(2,1)S(1)} %get-tuple-element.70.go_ref, f32[3,8,1024]{2,1,0:T(8,128)S(1)} %copy-done.26), custom_call_target="tpu_custom_call" | custom-call | flops 4026531840 | bytes 5505024 | tf_op jit(solution)/shard_map/attend_backward/pallas_call | solution.py:346
  210.8 5.4 %qkv_grads.1 = (bf16[4,96,768]{2,1,0:T(8,128)(2,1)S(1)}, bf16[4,96,768]{2,1,0:T(8,128)(2,1)S(1)}, bf16[2,2,96,768]{3,2,1,0:T(8,128)(2,1)S(1)}, bf16[2,2,96,768]{3,2,1,0:T(8,128)(2,1)S(1)}) custom-call(bf16[768,1024]{1,0:T(8,128)(2,1)S(1)} %copy-done.22, bf16[1024,1152]{1,0:T(8,128)(2,1)} %copy-done.27, bf16[768,384]{1,0:T(8,128)(2,1)S(1)} %get-tuple-element.74.out_grad_ref), custom_call_target="tpu_custom_call" | custom-call | flops 1811939328 | bytes 9437184 | tf_op jit(solution)/shard_map/qkv_grads/pallas_call | solution.py:779
  216.9 1.6 convert_add_fusion
  218.6 1.5 collective-permute-start.25
  220.7 1.7 convert_add_fusion.1
  222.5 1.5 collective-permute-start.23
  224.6 5.8 %first_back.1 = (f32[1024,768]{1,0:T(8,128)}, f32[8,768]{1,0:T(8,128)S(1)}, f32[8,1152]{1,0:T(8,128)S(1)}) custom-call(bf16[1024,1152]{1,0:T(8,128)(2,1)} %copy-done.27, bf16[768,1152]{1,0:T(8,128)(2,1)S(1)} %copy-done.28, bf16[1024,768]{1,0:T(8,128)(2,1)S(1)} %copy-done.6, bf16[4,96,768]{2,1,0:T(8,128)(2,1)S(1)} %get-tuple-element.75.after_ref), custom_call_target="tpu_custom_call" | custom-call | flops 1811939328 | bytes 7077888 | tf_op jit(solution)/shard_map/first_back/pallas_call | solution.py:815
  231.1 1.6 collective-permute-done.13
  232.8 10.9 %collective-permute-done.25 = bf16[2,1,96,1536]{3,2,0,1:T(8,128)(2,1)} collective-permute-done((bf16[2,1,96,1536]{3,2,0,1:T(8,128)(2,1)S(1)}, bf16[2,1,96,1536]{3,2,0,1:T(8,128)(2,1)}, u32[]{:S(2)}, u32[]{:S(2)}) %collective-permute-start.25) | collective-permute-done | bytes 589856 | tf_op jit(solution)/shard_map/ppermute | solution.py:58
  243.7 1.5 fusion.1
  245.3 1.9 collective-permute-start.26
  247.2 2.1 collective-permute-start.27
  252.5 2.3 collective-permute-done.29
  254.8 1.8 collective-permute-start.30
  257.2 1.7 collective-permute-done.30
  259.0 2.1 collective-permute-start.31
  262.2 7.9 %collective-permute-done.31 = f32[12,768]{1,0:T(8,128)S(1)} collective-permute-done((f32[12,768]{1,0:T(8,128)S(1)}, f32[12,768]{1,0:T(8,128)S(1)}, u32[]{:S(2)}, u32[]{:S(2)}) %collective-permute-start.31) | collective-permute-done | bytes 36896 | tf_op jit(solution)/shard_map/ppermute | solution.py:58
  271.2 4.0 %collective-permute-done.32 = f32[12,768]{1,0:T(8,128)S(1)} collective-permute-done((f32[12,768]{1,0:T(8,128)S(1)}, f32[12,768]{1,0:T(8,128)S(1)}, u32[]{:S(2)}, u32[]{:S(2)}) %collective-permute-start.32) | collective-permute-done | bytes 36896 | tf_op jit(solution)/shard_map/ppermute | solution.py:58
  275.2 1.5 collective-permute-start.15
  277.5 4.4 %collective-permute-done.15 = bf16[2,1,96,768]{3,2,1,0:T(8,128)(2,1)S(1)} collective-permute-done((bf16[2,1,96,768]{3,2,1,0:T(8,128)(2,1)S(1)}, bf16[2,1,96,768]{3,2,1,0:T(8,128)(2,1)S(1)}, u32[]{:S(2)}, u32[]{:S(2)}) %collective-permute-start.15) | collective-permute-done | bytes 294944 | tf_op jit(solution)/shard_map/ppermute | solution.py:58
  282.1 2.0 collective-permute-start.20
  284.1 1.5 collective-permute-start.16
  287.9 4.5 %collective-permute-done.19 = bf16[96,768]{1,0:T(8,128)(2,1)S(1)} collective-permute-done((bf16[96,768]{1,0:T(8,128)(2,1)S(1)}, bf16[96,768]{1,0:T(8,128)(2,1)S(1)}, u32[]{:S(2)}, u32[]{:S(2)}) %collective-permute-start.19) | collective-permute-done | bytes 147488 | tf_op jit(solution)/shard_map/ppermute | solution.py:58
  293.3 1.6 copy.42
  294.9 1.6 copy.43
  296.6 1.6 copy.44
  298.3 2.2 multiply_subtract_fusion.2
  300.5 3.2 %token_back.1 = f32[512,768]{1,0:T(8,128)} custom-call(s32[1]{0:T(128)} %bitcast.core_ref, f32[1024,768]{1,0:T(8,128)S(1)} %copy-done.2, bf16[512,768]{1,0:T(8,128)(2,1)} %collective-permute-done.14.other_ref, bf16[512,768]{1,0:T(8,128)(2,1)S(1)} %copy-done.4, f32[1024,768]{1,0:T(8,128)} %get-tuple-element.79.grad_ref, f32[16,768]{1,0:T(8,128)S(1)} %copy-done.21), custom_call_target="tpu_custom_call" | custom-call | flops 7864320 | bytes 6291456 | tf_op jit(solution)/shard_map/token_back/pallas_call | solution.py:847
  (214 shorter events, 42.8 us)
Async XLA Ops:
  7.2 13.9 %copy-start.3 = (bf16[512,768]{1,0:T(8,128)(2,1)S(1)}, bf16[512,768]{1,0:T(8,128)(2,1)}, u32[]{:S(2)}) copy-start(bf16[512,768]{1,0:T(8,128)(2,1)} %tokens_ref.1) | copy-start | bytes 2359300
  7.2 13.9 %copy-start.5 = (bf16[512,768]{1,0:T(8,128)(2,1)S(1)}, bf16[512,768]{1,0:T(8,128)(2,1)}, u32[]{:S(2)}) copy-start(bf16[512,768]{1,0:T(8,128)(2,1)} %mine_ref.3) | copy-start | bytes 2359300
  7.2 116.7 %all-gather.3.cloned.1.call-start = ((), (), s32[]{:S(2)}) async-start(), calls=%async_computation | async-start | bytes 2654208 | tf_op jit(solution)/shard_map/all_gather | solution.py:909
  10.1 131.4 %all-gather.5.cloned.1.call-start = ((), (), s32[]{:S(2)}) async-start(), calls=%async_computation.1 | async-start | bytes 2654208 | tf_op jit(solution)/shard_map/all_gather | solution.py:909
  10.1 10.2 %collective-permute-start.10 = (bf16[96,1536]{1,0:T(8,128)(2,1)}, bf16[96,1536]{1,0:T(8,128)(2,1)S(1)}, u32[]{:S(2)}, u32[]{:S(2)}) collective-permute-start(bf16[96,1536]{1,0:T(8,128)(2,1)} %pad_maximum_fusion.5), channel_id=1, source_target_pairs={{0,2},{1,3},{2,0},{3,1},{4,6},{5,7},{6,4},{7,5},{8,10},{9,11},{10,... | collective-permute-start | bytes 884744 | tf_op jit(solution)/shard_map/ppermute | solution.py:58
  22.4 43.6 %collective-permute-start = (bf16[2,512,768]{2,1,0:T(8,128)(2,1)}, bf16[2,512,768]{2,1,0:T(8,128)(2,1)}, u32[]{:S(2)}, u32[]{:S(2)}) collective-permute-start(bf16[2,512,768]{2,1,0:T(8,128)(2,1)} %pad_maximum_fusion), channel_id=1, source_target_pairs={{0,1},{1,0},{2,3},{3,2},{4,5},{5,4},{6,7},{7,6},{8,9},{9,8},{10,11... | collective-permute-start | bytes 4718600 | tf_op jit(solution)/shard_map/ppermute | solution.py:58
  23.4 22.6 %collective-permute-start.4 = (bf16[96,832]{1,0:T(8,128)(2,1)S(1)}, bf16[96,832]{1,0:T(8,128)(2,1)S(1)}, u32[]{:S(2)}, u32[]{:S(2)}) collective-permute-start(bf16[96,832]{1,0:T(8,128)(2,1)S(1)} %concatenate.25), channel_id=1, source_target_pairs={{0,16},{4,20},{8,24},{12,28},{16,0},{20,4},{24,8},{28,12},{1,17},{... | collective-permute-start | bytes 479240 | tf_op jit(solution)/shard_map/ppermute | solution.py:58
  26.3 19.7 %collective-permute-start.5 = (bf16[96,832]{1,0:T(8,128)(2,1)S(1)}, bf16[96,832]{1,0:T(8,128)(2,1)S(1)}, u32[]{:S(2)}, u32[]{:S(2)}) collective-permute-start(bf16[96,832]{1,0:T(8,128)(2,1)S(1)} %concatenate.25), channel_id=1, source_target_pairs={{0,24},{4,28},{8,16},{12,20},{16,8},{20,12},{24,0},{28,4},{1,25},{... | collective-permute-start | bytes 479240 | tf_op jit(solution)/shard_map/ppermute | solution.py:58
  27.6 20.1 %collective-permute-start.1 = (bf16[96,832]{1,0:T(8,128)(2,1)S(1)}, bf16[96,832]{1,0:T(8,128)(2,1)S(1)}, u32[]{:S(2)}, u32[]{:S(2)}) collective-permute-start(bf16[96,832]{1,0:T(8,128)(2,1)S(1)} %concatenate.25), channel_id=1, source_target_pairs={{0,8},{4,12},{8,0},{12,4},{16,24},{20,28},{24,16},{28,20},{1,9},{5... | collective-permute-start | bytes 479240 | tf_op jit(solution)/shard_map/ppermute | solution.py:58
  46.0 10.1 %collective-permute-start.6 = (bf16[2,96,832]{2,1,0:T(8,128)(2,1)S(1)}, bf16[2,96,832]{2,1,0:T(8,128)(2,1)S(1)}, u32[]{:S(2)}, u32[]{:S(2)}) collective-permute-start(bf16[2,96,832]{2,1,0:T(8,128)(2,1)S(1)} %pad_maximum_fusion.4), channel_id=1, source_target_pairs={{0,2},{1,3},{2,0},{3,1},{4,6},{5,7},{6,4},{7,5},{8,10},{9,11},{10,... | collective-permute-start | bytes 958472 | tf_op jit(solution)/shard_map/ppermute | solution.py:58
  47.7 17.3 %collective-permute-start.2 = (bf16[2,96,832]{2,1,0:T(8,128)(2,1)S(1)}, bf16[2,96,832]{2,1,0:T(8,128)(2,1)S(1)}, u32[]{:S(2)}, u32[]{:S(2)}) collective-permute-start(bf16[2,96,832]{2,1,0:T(8,128)(2,1)S(1)} %pad_maximum_fusion.3), channel_id=1, source_target_pairs={{0,4},{4,0},{8,12},{12,8},{16,20},{20,16},{24,28},{28,24},{1,5},{5... | collective-permute-start | bytes 958472 | tf_op jit(solution)/shard_map/ppermute | solution.py:58
  56.3 28.6 %collective-permute-start.7 = (bf16[4,96,832]{2,1,0:T(8,128)(2,1)S(1)}, bf16[4,96,832]{2,1,0:T(8,128)(2,1)}, u32[]{:S(2)}, u32[]{:S(2)}) collective-permute-start(bf16[4,96,832]{2,1,0:T(8,128)(2,1)S(1)} %pad_maximum_fusion.2.refs_2_), channel_id=1, source_target_pairs={{0,4},{4,0},{8,12},{12,8},{16,20},{20,16},{24,28},{28,24},{1,5},{5... | collective-permute-start | bytes 1916936 | tf_op jit(solution)/shard_map/ppermute | solution.py:58
  66.0 18.9 %collective-permute-start.3 = (bf16[4,96,832]{2,1,0:T(8,128)(2,1)}, bf16[4,96,832]{2,1,0:T(8,128)(2,1)}, u32[]{:S(2)}, u32[]{:S(2)}) collective-permute-start(bf16[4,96,832]{2,1,0:T(8,128)(2,1)} %pad_maximum_fusion.1.refs_0_), channel_id=1, source_target_pairs={{0,2},{1,3},{2,0},{3,1},{4,6},{5,7},{6,4},{7,5},{8,10},{9,11},{10,... | collective-permute-start | bytes 1916936 | tf_op jit(solution)/shard_map/ppermute | solution.py:58
  94.1 15.6 %copy-start.19 = (f32[16,768]{1,0:T(8,128)}, f32[16,768]{1,0:T(8,128)S(1)}, u32[]{:S(2)}) copy-start(f32[16,768]{1,0:T(8,128)S(1)} %get-tuple-element.61.vec_ref) | copy-start | bytes 147460
  109.7 4.0 %collective-permute-start.8 = (bf16[1024,384]{1,0:T(8,128)(2,1)S(1)}, bf16[1024,384]{1,0:T(8,128)(2,1)}, u32[]{:S(2)}, u32[]{:S(2)}) collective-permute-start(bf16[1024,384]{1,0:T(8,128)(2,1)S(1)} %get-tuple-element.58.heads_ref), channel_id=1, source_target_pairs={{0,1},{1,0},{2,3},{3,2},{4,5},{5,4},{6,7},{7,6},{8,9},{9,8},{10,11... | collective-permute-start | bytes 2359304 | tf_op jit(solution)/shard_map/ppermute | solution.py:58
  109.7 4.0 %collective-permute-start.9 = (bf16[768,384]{1,0:T(8,128)(2,1)S(1)}, bf16[768,384]{1,0:T(8,128)(2,1)S(1)}, u32[]{:S(2)}, u32[]{:S(2)}) collective-permute-start(bf16[768,384]{1,0:T(8,128)(2,1)S(1)} %get-tuple-element.59.own_ref.out_w_ref), channel_id=1, source_target_pairs={{0,1},{1,0},{2,3},{3,2},{4,5},{5,4},{6,7},{7,6},{8,9},{9,8},{10,11... | collective-permute-start | bytes 1769480 | tf_op jit(solution)/shard_map/ppermute | solution.py:58
  161.8 23.1 %collective-permute-start.12 = (bf16[1024,768]{1,0:T(8,128)(2,1)}, bf16[1024,768]{1,0:T(8,128)(2,1)S(1)}, u32[]{:S(2)}, u32[]{:S(2)}) collective-permute-start(bf16[1024,768]{1,0:T(8,128)(2,1)} %get-tuple-element.68), channel_id=1, source_target_pairs={{0,1},{1,0},{2,3},{3,2},{4,5},{5,4},{6,7},{7,6},{8,9},{9,8},{10,11... | collective-permute-start | bytes 4718600 | tf_op jit(solution)/shard_map/ppermute | solution.py:58
  164.3 17.2 %collective-permute-start.11 = (bf16[512,768]{1,0:T(8,128)(2,1)}, bf16[512,768]{1,0:T(8,128)(2,1)S(1)}, u32[]{:S(2)}, u32[]{:S(2)}) collective-permute-start(bf16[512,768]{1,0:T(8,128)(2,1)} %dynamic-slice_convert_fusion.1), channel_id=1, source_target_pairs={{0,1},{1,0},{2,3},{3,2},{4,5},{5,4},{6,7},{7,6},{8,9},{9,8},{10,11... | collective-permute-start | bytes 2359304 | tf_op jit(solution)/shard_map/ppermute | solution.py:58
  164.8 14.6 %copy-start.45 = (f32[192,96]{1,0:T(8,128)S(1)}, f32[192,96]{1,0:T(8,128)}, u32[]{:S(2)}) copy-start(f32[192,96]{1,0:T(8,128)} %param.25) | copy-start | bytes 221188
  164.8 15.3 %copy-start.46 = (f32[192,96]{1,0:T(8,128)S(1)}, f32[192,96]{1,0:T(8,128)}, u32[]{:S(2)}) copy-start(f32[192,96]{1,0:T(8,128)} %param.30) | copy-start | bytes 221188
  164.8 16.0 %copy-start.21 = (f32[16,768]{1,0:T(8,128)S(1)}, f32[16,768]{1,0:T(8,128)}, u32[]{:S(2)}) copy-start(f32[16,768]{1,0:T(8,128)} %copy-done.19) | copy-start | bytes 147460
  177.4 39.5 %collective-permute-start.21 = (bf16[4,96,1536]{2,1,0:T(8,128)(2,1)}, bf16[4,96,1536]{2,1,0:T(8,128)(2,1)}, u32[]{:S(2)}, u32[]{:S(2)}) collective-permute-start(bf16[4,96,1536]{2,1,0:T(8,128)(2,1)} %get-tuple-element.88), channel_id=1, source_target_pairs={{0,2},{1,3},{2,0},{3,1},{4,6},{5,7},{6,4},{7,5},{8,10},{9,11},{10,... | collective-permute-start | bytes 3538952 | tf_op jit(solution)/shard_map/ppermute | solution.py:58
  178.8 38.1 %collective-permute-start.22 = (bf16[2,2,96,1536]{3,2,1,0:T(8,128)(2,1)}, bf16[2,2,96,1536]{3,2,1,0:T(8,128)(2,1)}, u32[]{:S(2)}, u32[]{:S(2)}) collective-permute-start(bf16[2,2,96,1536]{3,2,1,0:T(8,128)(2,1)} %get-tuple-element.89), channel_id=1, source_target_pairs={{0,4},{4,0},{8,12},{12,8},{16,20},{20,16},{24,28},{28,24},{1,5},{5... | collective-permute-start | bytes 3538952 | tf_op jit(solution)/shard_map/ppermute | solution.py:58
  193.7 17.2 %copy-start.22 = (bf16[768,1024]{1,0:T(8,128)(2,1)S(1)}, bf16[768,1024]{1,0:T(8,128)(2,1)}, u32[]{:S(2)}) copy-start(bf16[768,1024]{1,0:T(8,128)(2,1)} %get-tuple-element.73.norm_ref) | copy-start | bytes 4718596
  216.2 16.4 %collective-permute-start.13 = (bf16[4,96,768]{2,1,0:T(8,128)(2,1)S(1)}, bf16[4,96,768]{2,1,0:T(8,128)(2,1)}, u32[]{:S(2)}, u32[]{:S(2)}) collective-permute-start(bf16[4,96,768]{2,1,0:T(8,128)(2,1)S(1)} %get-tuple-element.75.after_ref), channel_id=1, source_target_pairs={{0,2},{1,3},{2,0},{3,1},{4,6},{5,7},{6,4},{7,5},{8,10},{9,11},{10,... | collective-permute-start | bytes 1769480 | tf_op jit(solution)/shard_map/ppermute | solution.py:58
  218.5 11.8 %copy-start.29 = (f32[2,2,96,1536]{3,2,1,0:T(8,128)}, f32[2,2,96,1536]{3,2,1,0:T(8,128)S(1)}, u32[]{:S(2)}) copy-start(f32[2,2,96,1536]{3,2,1,0:T(8,128)S(1)} %convert_add_fusion) | copy-start | bytes 7077892
  218.6 25.1 %collective-permute-start.25 = (bf16[2,1,96,1536]{3,2,0,1:T(8,128)(2,1)S(1)}, bf16[2,1,96,1536]{3,2,0,1:T(8,128)(2,1)}, u32[]{:S(2)}, u32[]{:S(2)}) collective-permute-start(bf16[2,1,96,1536]{3,2,0,1:T(8,128)(2,1)S(1)} %fusion.2), channel_id=1, source_target_pairs={{0,2},{1,3},{2,0},{3,1},{4,6},{5,7},{6,4},{7,5},{8,10},{9,11},{10,... | collective-permute-start | bytes 1769480 | tf_op jit(solution)/shard_map/ppermute | solution.py:58
  222.5 26.8 %collective-permute-start.23 = (bf16[2,1,96,1536]{3,2,1,0:T(8,128)(2,1)S(1)}, bf16[2,1,96,1536]{3,2,1,0:T(8,128)(2,1)}, u32[]{:S(2)}, u32[]{:S(2)}) collective-permute-start(bf16[2,1,96,1536]{3,2,1,0:T(8,128)(2,1)S(1)} %slice.301), channel_id=1, source_target_pairs={{0,4},{4,0},{8,12},{12,8},{16,20},{20,16},{24,28},{28,24},{1,5},{5... | collective-permute-start | bytes 1769480 | tf_op jit(solution)/shard_map/ppermute | solution.py:58
  224.0 27.2 %collective-permute-start.17 = (bf16[2,2,96,768]{3,2,1,0:T(8,128)(2,1)S(1)}, bf16[2,2,96,768]{3,2,1,0:T(8,128)(2,1)}, u32[]{:S(2)}, u32[]{:S(2)}) collective-permute-start(bf16[2,2,96,768]{3,2,1,0:T(8,128)(2,1)S(1)} %get-tuple-element.82), channel_id=1, source_target_pairs={{0,4},{4,0},{8,12},{12,8},{16,20},{20,16},{24,28},{28,24},{1,5},{5... | collective-permute-start | bytes 1769480 | tf_op jit(solution)/shard_map/ppermute | solution.py:58
  232.7 16.6 %copy-start.31 = (f32[4,96,1536]{2,1,0:T(8,128)S(1)}, f32[4,96,1536]{2,1,0:T(8,128)}, u32[]{:S(2)}) copy-start(f32[4,96,1536]{2,1,0:T(8,128)} %copy-done.30) | copy-start | bytes 7077892
  232.7 17.9 %collective-permute-start.28 = (f32[12,768]{1,0:T(8,128)S(1)}, f32[12,768]{1,0:T(8,128)S(1)}, u32[]{:S(2)}, u32[]{:S(2)}) collective-permute-start(f32[12,768]{1,0:T(8,128)S(1)} %concatenate.30), channel_id=1, source_target_pairs={{0,1},{1,0},{2,3},{3,2},{4,5},{5,4},{6,7},{7,6},{8,9},{9,8},{10,11... | collective-permute-start | bytes 110600 | tf_op jit(solution)/shard_map/ppermute | solution.py:58
  245.3 36.8 %collective-permute-start.26 = (bf16[96,1536]{1,0:T(8,128)(2,1)S(1)}, bf16[96,1536]{1,0:T(8,128)(2,1)S(1)}, u32[]{:S(2)}, u32[]{:S(2)}) collective-permute-start(bf16[96,1536]{1,0:T(8,128)(2,1)S(1)} %slice_bitcast_fusion.7), channel_id=1, source_target_pairs={{0,16},{4,20},{8,24},{12,28},{16,0},{20,4},{24,8},{28,12},{1,17},{... | collective-permute-start | bytes 884744 | tf_op jit(solution)/shard_map/ppermute | solution.py:58
  247.2 36.8 %collective-permute-start.27 = (bf16[96,1536]{1,0:T(8,128)(2,1)S(1)}, bf16[96,1536]{1,0:T(8,128)(2,1)S(1)}, u32[]{:S(2)}, u32[]{:S(2)}) collective-permute-start(bf16[96,1536]{1,0:T(8,128)(2,1)S(1)} %slice_bitcast_fusion.6), channel_id=1, source_target_pairs={{0,24},{4,28},{8,16},{12,20},{16,8},{20,12},{24,0},{28,4},{1,25},{... | collective-permute-start | bytes 884744 | tf_op jit(solution)/shard_map/ppermute | solution.py:58
  250.5 35.1 %collective-permute-start.24 = (bf16[96,1536]{1,0:T(8,128)(2,1)S(1)}, bf16[96,1536]{1,0:T(8,128)(2,1)S(1)}, u32[]{:S(2)}, u32[]{:S(2)}) collective-permute-start(bf16[96,1536]{1,0:T(8,128)(2,1)S(1)} %fusion.12), channel_id=1, source_target_pairs={{0,8},{4,12},{8,0},{12,4},{16,24},{20,28},{24,16},{28,20},{1,9},{5... | collective-permute-start | bytes 884744 | tf_op jit(solution)/shard_map/ppermute | solution.py:58
  250.6 4.2 %collective-permute-start.29 = (f32[12,768]{1,0:T(8,128)S(1)}, f32[12,768]{1,0:T(8,128)S(1)}, u32[]{:S(2)}, u32[]{:S(2)}) collective-permute-start(f32[12,768]{1,0:T(8,128)S(1)} %add.225), channel_id=1, source_target_pairs={{0,2},{1,3},{2,0},{3,1},{4,6},{5,7},{6,4},{7,5},{8,10},{9,11},{10,... | collective-permute-start | bytes 110600 | tf_op jit(solution)/shard_map/ppermute | solution.py:58
  254.8 15.4 %copy-start.2 = (f32[1024,768]{1,0:T(8,128)S(1)}, f32[1024,768]{1,0:T(8,128)}, u32[]{:S(2)}) copy-start(f32[1024,768]{1,0:T(8,128)} %get-tuple-element.78.part_ref) | copy-start | bytes 9437188
  254.8 4.2 %collective-permute-start.30 = (f32[12,768]{1,0:T(8,128)S(1)}, f32[12,768]{1,0:T(8,128)S(1)}, u32[]{:S(2)}, u32[]{:S(2)}) collective-permute-start(f32[12,768]{1,0:T(8,128)S(1)} %add.226), channel_id=1, source_target_pairs={{0,4},{4,0},{8,12},{12,8},{16,20},{20,16},{24,28},{28,24},{1,5},{5... | collective-permute-start | bytes 110600 | tf_op jit(solution)/shard_map/ppermute | solution.py:58
  256.6 20.8 %collective-permute-start.18 = (bf16[2,1,96,768]{3,2,0,1:T(8,128)(2,1)S(1)}, bf16[2,1,96,768]{3,2,0,1:T(8,128)(2,1)S(1)}, u32[]{:S(2)}, u32[]{:S(2)}) collective-permute-start(bf16[2,1,96,768]{3,2,0,1:T(8,128)(2,1)S(1)} %fusion.11), channel_id=1, source_target_pairs={{0,2},{1,3},{2,0},{3,1},{4,6},{5,7},{6,4},{7,5},{8,10},{9,11},{10,... | collective-permute-start | bytes 884744 | tf_op jit(solution)/shard_map/ppermute | solution.py:58
  259.0 11.2 %collective-permute-start.31 = (f32[12,768]{1,0:T(8,128)S(1)}, f32[12,768]{1,0:T(8,128)S(1)}, u32[]{:S(2)}, u32[]{:S(2)}) collective-permute-start(f32[12,768]{1,0:T(8,128)S(1)} %add.227), channel_id=1, source_target_pairs={{0,8},{4,12},{8,0},{12,4},{16,24},{20,28},{24,16},{28,20},{1,9},{5... | collective-permute-start | bytes 110600 | tf_op jit(solution)/shard_map/ppermute | solution.py:58
  262.2 14.4 %copy-start.48 = (f32[12,96]{1,0:T(8,128)S(1)}, f32[12,96]{1,0:T(8,128)}, u32[]{:S(2)}) copy-start(f32[12,96]{1,0:T(8,128)} %param.23) | copy-start | bytes 13828
  262.2 14.4 %copy-start.49 = (f32[12,96]{1,0:T(8,128)S(1)}, f32[12,96]{1,0:T(8,128)}, u32[]{:S(2)}) copy-start(f32[12,96]{1,0:T(8,128)} %param.28) | copy-start | bytes 13828
  262.2 14.4 %copy-start.50 = (f32[12,96]{1,0:T(8,128)S(1)}, f32[12,96]{1,0:T(8,128)}, u32[]{:S(2)}) copy-start(f32[12,96]{1,0:T(8,128)} %param.33) | copy-start | bytes 13828
  270.1 5.0 %collective-permute-start.32 = (f32[12,768]{1,0:T(8,128)S(1)}, f32[12,768]{1,0:T(8,128)S(1)}, u32[]{:S(2)}, u32[]{:S(2)}) collective-permute-start(f32[12,768]{1,0:T(8,128)S(1)} %add.228), channel_id=1, source_target_pairs={{0,16},{4,20},{8,24},{12,28},{16,0},{20,4},{24,8},{28,12},{1,17},{... | collective-permute-start | bytes 110600 | tf_op jit(solution)/shard_map/ppermute | solution.py:58
  275.2 6.7 %collective-permute-start.15 = (bf16[2,1,96,768]{3,2,1,0:T(8,128)(2,1)S(1)}, bf16[2,1,96,768]{3,2,1,0:T(8,128)(2,1)S(1)}, u32[]{:S(2)}, u32[]{:S(2)}) collective-permute-start(bf16[2,1,96,768]{3,2,1,0:T(8,128)(2,1)S(1)} %slice.302), channel_id=1, source_target_pairs={{0,4},{4,0},{8,12},{12,8},{16,20},{20,16},{24,28},{28,24},{1,5},{5... | collective-permute-start | bytes 884744 | tf_op jit(solution)/shard_map/ppermute | solution.py:58
  277.4 23.2 %collective-permute-start.14 = (bf16[512,768]{1,0:T(8,128)(2,1)}, bf16[512,768]{1,0:T(8,128)(2,1)}, u32[]{:S(2)}, u32[]{:S(2)}) collective-permute-start(bf16[512,768]{1,0:T(8,128)(2,1)} %dynamic-slice_convert_fusion), channel_id=1, source_target_pairs={{0,1},{1,0},{2,3},{3,2},{4,5},{5,4},{6,7},{7,6},{8,9},{9,8},{10,11... | collective-permute-start | bytes 2359304 | tf_op jit(solution)/shard_map/ppermute | solution.py:58
  281.9 10.4 %collective-permute-start.19 = (bf16[96,768]{1,0:T(8,128)(2,1)S(1)}, bf16[96,768]{1,0:T(8,128)(2,1)S(1)}, u32[]{:S(2)}, u32[]{:S(2)}) collective-permute-start(bf16[96,768]{1,0:T(8,128)(2,1)S(1)} %slice_bitcast_fusion.10), channel_id=1, source_target_pairs={{0,16},{4,20},{8,24},{12,28},{16,0},{20,4},{24,8},{28,12},{1,17},{... | collective-permute-start | bytes 442376 | tf_op jit(solution)/shard_map/ppermute | solution.py:58
  282.1 10.3 %collective-permute-start.20 = (bf16[96,768]{1,0:T(8,128)(2,1)S(1)}, bf16[96,768]{1,0:T(8,128)(2,1)S(1)}, u32[]{:S(2)}, u32[]{:S(2)}) collective-permute-start(bf16[96,768]{1,0:T(8,128)(2,1)S(1)} %slice_bitcast_fusion.9), channel_id=1, source_target_pairs={{0,24},{4,28},{8,16},{12,20},{16,8},{20,12},{24,0},{28,4},{1,25},{... | collective-permute-start | bytes 442376 | tf_op jit(solution)/shard_map/ppermute | solution.py:58
  284.1 8.3 %collective-permute-start.16 = (bf16[96,768]{1,0:T(8,128)(2,1)S(1)}, bf16[96,768]{1,0:T(8,128)(2,1)S(1)}, u32[]{:S(2)}, u32[]{:S(2)}) collective-permute-start(bf16[96,768]{1,0:T(8,128)(2,1)S(1)} %fusion.16), channel_id=1, source_target_pairs={{0,8},{4,12},{8,0},{12,4},{16,24},{20,28},{24,16},{28,20},{1,9},{5... | collective-permute-start | bytes 442376 | tf_op jit(solution)/shard_map/ppermute | solution.py:58
  (38 other events, 148.0 us)
Sparse Core Ops, SparseCore 0:
  10.8 76.7 all-gather.2
  90.3 51.1 all-gather.4
